TPU v7x, 512 devices: a whole 4x8x8 slice. The times are simulated.
512 devices in a mesh: section: 16 (over z, core), chan: 32 (over x, y).
Axes of the slice: x: 4, y: 8, z: 8, core: 2. Of those that a mesh axis runs over, the one named last changes fastest.
Arguments:
- opening_level_feeds: bfloat16 [16, 256, 2048], P('section', None, 'chan'), may hold values from -6 to 6
- newcomer_embeddings: bfloat16 [3, 256, 2048], P(None, None, 'chan'), may hold values from -6 to 6
- occupied_positions_per_piece: int32 [19], replicated, may hold values from 1 to 256, 3648 in all
- rootmean_gain_matrix: float32 [16, 2048], P('section'), may hold values from 0.5 to 1.5
- payload_projection_matrix: bfloat16 [16, 2048, 2048], P('section', None, 'chan'), may hold values from -0.125 to 0.125
- interior_multiplier_matrix: bfloat16 [16, 2048, 2048], P('section', None, 'chan'), may hold values from -0.125 to 0.125
- exterior_multiplier_matrix: bfloat16 [16, 2048, 2048], P('section', None, 'chan'), may hold values from -0.125 to 0.125
- emission_projection_matrix: bfloat16 [16, 2048, 2048], P('section', None, 'chan'), may hold values from -0.125 to 0.125
- bypass_channel_factors: float32 [16, 2048], P('section', 'chan'), may hold values from 0.5 to 1.5
- kernel_spectra_by_delay: float32 [16, 4, 2, 2048, 512], P('section', None, None, 'chan'), may hold values from -3 to 3
- archived_block_spectra: float32 [16, 3, 2, 2048, 512], P('section', None, None, 'chan'), may hold values from -96 to 96
Outputs:
- layer_out: bfloat16 [16, 4, 256, 2048], P('section', None, None, 'chan')
Inputs may be any that keep to these rules, and one draw needn't show every extreme that they name: `occupied_positions_per_piece`: every slice has at least one live token; the longest has exactly 256.
All inputs are finite; a program needn't handle non-finite values.
Results may differ from a plain program's by a relative error of at most 0.015.
Values may be sent and summed in bfloat16 or wider, within the bound.
No kernel may reach another device: no remote copies, remote signals or barrier semaphores. Data moves between devices by JAX's collectives and lax.ppermute only.
A program may use at most 64 MiB of HBM per device.

v0:
```python
import math

import jax
import jax.numpy as jnp
from jax import lax
from jax.sharding import PartitionSpec as P

highest = lax.Precision.HIGHEST


def shifted(value, axis, by):
    devices = lax.axis_size(axis)
    pairs = [(i, i + by) for i in range(devices) if 0 <= i + by < devices]
    return lax.ppermute(value, axis, pairs)


def tables(length, period):
    rows_index = jnp.arange(length, dtype=jnp.int32)[:, None]
    freq_index = jnp.arange(period, dtype=jnp.int32)[None, :]
    phase = rows_index * freq_index % period
    angle = phase.astype(jnp.float32) * (2.0 * math.pi / period)
    return (jnp.cos(angle), jnp.sin(angle))


def forward_spectrum(driven, cos_table, sin_table):
    contract = (((0,), (0,)), ((), ()))
    real_part = lax.dot_general(
        driven, cos_table, contract, precision=highest, preferred_element_type=jnp.float32
    )
    imag_part = -lax.dot_general(
        driven, sin_table, contract, precision=highest, preferred_element_type=jnp.float32
    )
    return (real_part, imag_part)


def inverse_rows(zreal, zimag, cos_table, sin_table):
    contract = (((1,), (1,)), ((), ()))
    cosine_part = lax.dot_general(
        cos_table, zreal, contract, precision=highest, preferred_element_type=jnp.float32
    )
    sine_part = lax.dot_general(
        sin_table, zimag, contract, precision=highest, preferred_element_type=jnp.float32
    )
    return (cosine_part - sine_part) / cos_table.shape[1]


def spectral_mix(spectrum, lagged, filter_spec):
    zreal = filter_spec[0, 0] * spectrum[0] - filter_spec[0, 1] * spectrum[1]
    zimag = filter_spec[0, 0] * spectrum[1] + filter_spec[0, 1] * spectrum[0]
    for lag_index in range(len(lagged)):
        earlier = lagged[lag_index]
        zreal = zreal + (
            filter_spec[lag_index + 1, 0] * earlier[0] - filter_spec[lag_index + 1, 1] * earlier[1]
        )
        zimag = zimag + (
            filter_spec[lag_index + 1, 0] * earlier[1] + filter_spec[lag_index + 1, 1] * earlier[0]
        )
    return (zreal, zimag)


def gather_features(local_rows):
    return lax.all_gather(local_rows, "chan", axis=1, tiled=True)


def local(
    opening_level_feeds,
    newcomer_embeddings,
    occupied_positions_per_piece,
    rootmean_gain_matrix,
    payload_projection_matrix,
    interior_multiplier_matrix,
    exterior_multiplier_matrix,
    emission_projection_matrix,
    bypass_channel_factors,
    kernel_spectra_by_delay,
    archived_block_spectra,
):
    section = lax.axis_index("section")
    layers = lax.axis_size("section")
    position_vectors = opening_level_feeds.shape[1]
    ticks = newcomer_embeddings.shape[0] + 1
    blocks = archived_block_spectra.shape[1]
    cos_table, sin_table = tables(position_vectors, 2 * position_vectors)
    positions = jnp.arange(position_vectors, dtype=jnp.int32)[:, None]
    gain_row = rootmean_gain_matrix[0][None, :]
    skip_row = bypass_channel_factors[0][None, :]
    out_weights = emission_projection_matrix[0]
    outputs = []
    spectra = []
    earlier_carry = opening_level_feeds[0]
    for tick in range(ticks):
        if tick == 0:
            neighbourhood_activation = opening_level_feeds[0]
            u_full = gather_features(neighbourhood_activation)
        else:
            arriving = shifted(earlier_carry, "section", 1)
            neighbourhood_activation = jnp.where(
                section == 0, newcomer_embeddings[tick - 1], arriving
            )
            u_full = gather_features(neighbourhood_activation)
        u_wide = u_full.astype(jnp.float32)
        scale = lax.rsqrt(jnp.mean(u_wide * u_wide, axis=1, keepdims=True) + 1e-06)
        normed = (u_wide * scale * gain_row).astype(jnp.bfloat16)
        value = jnp.dot(normed, payload_projection_matrix[0], preferred_element_type=jnp.float32)
        gate_in = jnp.dot(normed, interior_multiplier_matrix[0], preferred_element_type=jnp.float32)
        gate_out = jnp.dot(
            normed, exterior_multiplier_matrix[0], preferred_element_type=jnp.float32
        )
        slice_length = lax.dynamic_index_in_dim(
            occupied_positions_per_piece, tick - section + layers - 1, 0, keepdims=False
        )
        live = positions < slice_length
        driven = jnp.where(live, gate_in * value, jnp.float32(0.0))
        spectrum = forward_spectrum(driven, cos_table, sin_table)
        lagged = []
        for lag in range(1, blocks + 1):
            if lag <= tick:
                lagged.append(spectra[tick - lag])
            else:
                lagged.append(
                    (
                        archived_block_spectra[0, lag - tick - 1, 0],
                        archived_block_spectra[0, lag - tick - 1, 1],
                    )
                )
        spectra.append(spectrum)
        zreal, zimag = spectral_mix(spectrum, lagged, kernel_spectra_by_delay[0])
        conv = inverse_rows(zreal, zimag, cos_table, sin_table)
        mixed = (gate_out * (conv + skip_row * driven)).astype(jnp.bfloat16)
        total = jnp.dot(
            lax.all_gather(mixed, "chan", axis=1, tiled=True),
            out_weights,
            preferred_element_type=jnp.float32,
        )
        out_local = (neighbourhood_activation.astype(jnp.float32) + total).astype(jnp.bfloat16)
        outputs.append(out_local)
        earlier_carry = out_local
    return jnp.stack(outputs, axis=0)[None]


def solution(mesh):
    return jax.shard_map(
        local,
        mesh=mesh,
        in_specs=(
            P("section", None, "chan"),
            P(None, None, "chan"),
            P(),
            P("section", None),
            P("section", None, "chan"),
            P("section", None, "chan"),
            P("section", None, "chan"),
            P("section", None, "chan"),
            P("section", "chan"),
            P("section", None, None, "chan", None),
            P("section", None, None, "chan", None),
        ),
        out_specs=P("section", None, None, "chan"),
        check_vma=False,
    )
```

profile of v0, /device:TPU:16, one launch (start us, length us, event | category | flops | bytes accessed | tf_op | source)
XLA Modules:
  0.0 746.7 jit_solution(4488461641005426460)
XLA Ops:
  9.4 87.0 %all-gather.24.cloned.1.call-done = bf16[1,256,2048]{1,2,0:T(8,128)(2,1)} async-done(((bf16[1,256,64]{1,2,0:T(8,128)(2,1)}), bf16[1,256,2048]{1,2,0:T(8,128)(2,1)}) %all-gather.24.cloned.1.call-update) | async-done | bytes 1048592 | tf_op jit(solution)/shard_map/all_gather | solution.py:62
  100.1 2.5 convolution_negate_fusion.3
  102.6 2.5 fusion.76
  105.2 2.6 fusion.74
  108.4 3.2 fusion.29
  111.7 79.5 %all-gather.10.cloned.1.call-done = bf16[256,2048]{0,1:T(8,128)(2,1)} async-done(((bf16[256,64]{0,1:T(8,128)(2,1)}), bf16[256,2048]{0,1:T(8,128)(2,1)}) %all-gather.10.cloned.1.call-update) | async-done | bytes 1048592 | tf_op jit(solution)/shard_map/all_gather | solution.py:131
  196.5 83.0 %all-gather.12.cloned.1.call-done = bf16[256,2048]{0,1:T(8,128)(2,1)} async-done(((bf16[256,64]{0,1:T(8,128)(2,1)}), bf16[256,2048]{0,1:T(8,128)(2,1)}) %all-gather.12.cloned.1.call-update) | async-done | bytes 1048592 | tf_op jit(solution)/shard_map/all_gather | solution.py:62
  282.5 2.5 convolution_negate_fusion.2
  285.0 2.5 fusion.72
  287.6 2.6 fusion.70
  290.2 2.6 fusion.17
  294.0 79.5 %all-gather.14.cloned.1.call-done = bf16[256,2048]{0,1:T(8,128)(2,1)} async-done(((bf16[256,64]{0,1:T(8,128)(2,1)}), bf16[256,2048]{0,1:T(8,128)(2,1)}) %all-gather.14.cloned.1.call-update) | async-done | bytes 1048592 | tf_op jit(solution)/shard_map/all_gather | solution.py:131
  378.7 82.9 %all-gather.16.cloned.1.call-done = bf16[256,2048]{0,1:T(8,128)(2,1)} async-done(((bf16[256,64]{0,1:T(8,128)(2,1)}), bf16[256,2048]{0,1:T(8,128)(2,1)}) %all-gather.16.cloned.1.call-update) | async-done | bytes 1048592 | tf_op jit(solution)/shard_map/all_gather | solution.py:62
  464.3 2.5 convolution_negate_fusion.1
  466.9 2.5 fusion.68
  469.4 2.6 fusion.66
  472.0 2.6 fusion.15
  475.8 79.5 %all-gather.18.cloned.1.call-done = bf16[256,2048]{0,1:T(8,128)(2,1)} async-done(((bf16[256,64]{0,1:T(8,128)(2,1)}), bf16[256,2048]{0,1:T(8,128)(2,1)}) %all-gather.18.cloned.1.call-update) | async-done | bytes 1048592 | tf_op jit(solution)/shard_map/all_gather | solution.py:131
  560.5 83.0 %all-gather.20.cloned.1.call-done = bf16[256,2048]{0,1:T(8,128)(2,1)} async-done(((bf16[256,64]{0,1:T(8,128)(2,1)}), bf16[256,2048]{0,1:T(8,128)(2,1)}) %all-gather.20.cloned.1.call-update) | async-done | bytes 1048592 | tf_op jit(solution)/shard_map/all_gather | solution.py:62
  646.2 2.6 convolution_negate_fusion
  648.8 2.5 fusion.64
  651.3 2.6 fusion.62
  653.9 2.6 fusion.13
  657.7 79.5 %all-gather.22.cloned.1.call-done = bf16[256,2048]{0,1:T(8,128)(2,1)} async-done(((bf16[256,64]{0,1:T(8,128)(2,1)}), bf16[256,2048]{0,1:T(8,128)(2,1)}) %all-gather.22.cloned.1.call-update) | async-done | bytes 1048592 | tf_op jit(solution)/shard_map/all_gather | solution.py:131
  (103 shorter events, 36.8 us)
Async XLA Ops:
  6.5 93.0 %copy-start = (bf16[1,2048,64]{1,2,0:T(8,128)(2,1)S(1)}, bf16[1,2048,64]{1,2,0:T(8,128)(2,1)}, u32[]{:S(2)}) copy-start(bf16[1,2048,64]{1,2,0:T(8,128)(2,1)} %param.15) | copy-start | bytes 786436
  6.5 91.5 %copy-start.15 = (f32[1,2048]{1,0:T(1,128)S(1)}, f32[1,2048]{1,0:T(1,128)}, u32[]{:S(2)}) copy-start(f32[1,2048]{1,0:T(1,128)} %param.14) | copy-start | bytes 24580
  6.5 89.9 %all-gather.24.cloned.1.call-start = ((), (), s32[]{:S(2)}) async-start(), calls=%async_computation.7 | async-start | bytes 1081344 | tf_op jit(solution)/shard_map/all_gather | solution.py:62
  7.3 184.0 %all-gather.10.cloned.1.call-start = ((), (), s32[]{:S(2)}) async-start(), calls=%async_computation | async-start | bytes 1081344 | tf_op jit(solution)/shard_map/all_gather | solution.py:131
  108.4 82.8 %copy-start.1 = (bf16[1,2048,64]{1,2,0:T(8,128)(2,1)S(1)}, bf16[1,2048,64]{1,2,0:T(8,128)(2,1)}, u32[]{:S(2)}) copy-start(bf16[1,2048,64]{1,2,0:T(8,128)(2,1)} %param.18) | copy-start | bytes 786436
  108.4 82.8 %copy-start.9 = (bf16[1,256,64]{1,2,0:T(8,128)(2,1)S(1)}, bf16[1,256,64]{1,2,0:T(8,128)(2,1)}, u32[]{:S(2)}) copy-start(bf16[1,256,64]{1,2,0:T(8,128)(2,1)} %param.11) | copy-start | bytes 98308
  111.7 83.3 %copy-start.10 = (bf16[3,256,64]{1,2,0:T(8,128)(2,1)S(1)}, bf16[3,256,64]{1,2,0:T(8,128)(2,1)}, u32[]{:S(2)}) copy-start(bf16[3,256,64]{1,2,0:T(8,128)(2,1)} %param.12) | copy-start | bytes 294916
  111.7 167.7 %all-gather.12.cloned.1.call-start = ((), (), s32[]{:S(2)}) async-start(), calls=%async_computation.1 | async-start | bytes 1081344 | tf_op jit(solution)/shard_map/all_gather | solution.py:62
  192.8 2.1 collective-permute-start
  195.6 177.9 %all-gather.14.cloned.1.call-start = ((), (), s32[]{:S(2)}) async-start(), calls=%async_computation.2 | async-start | bytes 1081344 | tf_op jit(solution)/shard_map/all_gather | solution.py:131
  287.6 2.6 copy-start.17
  292.8 80.7 %copy-start.7 = (bf16[256,64]{0,1:T(8,128)(2,1)S(1)}, bf16[256,64]{0,1:T(8,128)(2,1)}, u32[]{:S(2)}) copy-start(bf16[256,64]{0,1:T(8,128)(2,1)} %bitcast_select_fusion.2) | copy-start | bytes 98308
  293.9 167.7 %all-gather.16.cloned.1.call-start = ((), (), s32[]{:S(2)}) async-start(), calls=%async_computation.3 | async-start | bytes 1081344 | tf_op jit(solution)/shard_map/all_gather | solution.py:62
  375.0 2.1 collective-permute-start.1
  377.8 177.6 %all-gather.18.cloned.1.call-start = ((), (), s32[]{:S(2)}) async-start(), calls=%async_computation.4 | async-start | bytes 1081344 | tf_op jit(solution)/shard_map/all_gather | solution.py:131
  466.9 5.2 copy-start.20
  469.4 2.6 copy-start.22
  474.6 80.7 %copy-start.8 = (bf16[256,64]{0,1:T(8,128)(2,1)S(1)}, bf16[256,64]{0,1:T(8,128)(2,1)}, u32[]{:S(2)}) copy-start(bf16[256,64]{0,1:T(8,128)(2,1)} %bitcast_select_fusion.1) | copy-start | bytes 98308
  475.8 167.7 %all-gather.20.cloned.1.call-start = ((), (), s32[]{:S(2)}) async-start(), calls=%async_computation.5 | async-start | bytes 1081344 | tf_op jit(solution)/shard_map/all_gather | solution.py:62
  556.9 2.1 collective-permute-start.2
  559.7 177.6 %all-gather.22.cloned.1.call-start = ((), (), s32[]{:S(2)}) async-start(), calls=%async_computation.6 | async-start | bytes 1081344 | tf_op jit(solution)/shard_map/all_gather | solution.py:131
  648.7 2.6 copy-start.19
  648.8 2.6 copy-start.21
  656.5 80.7 %copy-start.6 = (bf16[256,64]{0,1:T(8,128)(2,1)S(1)}, bf16[256,64]{0,1:T(8,128)(2,1)}, u32[]{:S(2)}) copy-start(bf16[256,64]{0,1:T(8,128)(2,1)} %bitcast_select_fusion) | copy-start | bytes 98308
  (11 other events, 21.0 us)
Sparse Core Ops, SparseCore 0:
  10.5 85.8 all-gather.23
  111.8 79.3 all-gather.9
  195.7 83.6 all-gather.11
  294.0 79.3 all-gather.13
  377.9 83.6 all-gather.15
  475.9 79.3 all-gather.17
  559.8 83.6 all-gather.19
  657.8 79.3 all-gather.21
where the time goes:
time: 754 us; the launch traced here: 747 us
  waiting for transfers between devices  657 us (87%)
  matrix products  56.6 us (8%)
  between operations  14.3 us (2%)
  other arithmetic  11.6 us (2%)
    all_gather x4, waiting for transfers between devices, gather_features(): return lax.all_gather(local_rows, 'chan', axis=1, tiled=True)  336 us
    all_gather x4, waiting for transfers between devices, local(): lax.all_gather(mixed, 'chan', axis=1, tiled=True)  318 us
  transfers between devices with their start and end apart: 11, of which 11 were waited for; matrix products, arithmetic and copies ran while one was open for 1% of the time, Pallas kernels for 0%

commit v1 on v0

v1 whole, which is shorter than its diff:
```python
import functools

import jax
import jax.numpy as jnp
import numpy as np
from jax import lax
from jax.experimental import pallas as pl
from jax.experimental.pallas import tpu as pltpu
from jax.sharding import Mesh
from jax.sharding import PartitionSpec as P

SECTION = ("z", "core")


def params(cost=None):
    return pltpu.CompilerParams(vmem_limit_bytes=48 * 1024 * 1024)


def tables(length, period):
    phase = np.arange(length)[:, None] * np.arange(period)[None, :] % period
    angle = phase * (2.0 * np.pi / period)
    forward = np.concatenate([np.cos(angle), -np.sin(angle)], axis=1)
    return forward.astype(jnp.bfloat16), (forward.T / period).astype(jnp.bfloat16)


def spread(block, axis):
    n = lax.axis_size(axis)
    copies = jnp.broadcast_to(block[None], (n,) + block.shape)
    got = lax.all_to_all(copies, axis, 0, 0, tiled=True)
    return got.reshape((n * block.shape[0],) + block.shape[1:])


def mix_kernel(tick, blocks, length_ref, u_ref, w_ref, fwd_ref, inv_ref, filt_ref, skip_ref, *rest):
    held = rest[: blocks - min(tick, blocks)]
    past = rest[len(held) : len(held) + min(tick, blocks)]
    mixed_ref, spec_ref = rest[len(held) + len(past) :]
    width, positions = mixed_ref.shape
    period = fwd_ref.shape[1] // 2
    u = u_ref[...]
    wide = u.astype(jnp.float32)
    square = jnp.sum(wide * wide, axis=0, keepdims=True) * (1.0 / u.shape[0])
    scale = lax.rsqrt(square + 1e-06)
    gates = jnp.dot(w_ref[...], u, preferred_element_type=jnp.float32) * scale
    live = lax.broadcasted_iota(jnp.int32, (1, positions), 1) < length_ref[0]
    driven = jnp.where(live, gates[width : 2 * width] * gates[:width], 0.0)
    spectrum = jnp.dot(driven.astype(jnp.bfloat16), fwd_ref[...], preferred_element_type=jnp.float32)
    real, imag = spectrum[:, :period], spectrum[:, period:]
    spec_ref[0] = real
    spec_ref[1] = imag
    zreal = filt_ref[0, 0] * real - filt_ref[0, 1] * imag
    zimag = filt_ref[0, 0] * imag + filt_ref[0, 1] * real
    for lag, ref in enumerate(past + held, 1):
        zreal += filt_ref[lag, 0] * ref[0] - filt_ref[lag, 1] * ref[1]
        zimag += filt_ref[lag, 0] * ref[1] + filt_ref[lag, 1] * ref[0]
    packed = jnp.concatenate([zreal, zimag], axis=1).astype(jnp.bfloat16)
    conv = jnp.dot(packed, inv_ref[...], preferred_element_type=jnp.float32)
    mixed_ref[...] = (gates[2 * width :] * (conv + skip_ref[...] * driven)).astype(mixed_ref.dtype)


def mix(tick, blocks, length, u, weights, forward, inverse, filters, skip, held, past):
    width, positions = skip.shape[0], u.shape[1]
    vmem = pl.BlockSpec(memory_space=pltpu.VMEM)
    operands = [u, weights, forward, inverse, filters, skip] + held + past
    return pl.pallas_call(
        functools.partial(mix_kernel, tick, blocks),
        out_shape=(
            jax.ShapeDtypeStruct((width, positions), jnp.bfloat16),
            jax.ShapeDtypeStruct((2, width, filters.shape[-1]), jnp.float32),
        ),
        in_specs=[pl.BlockSpec(memory_space=pltpu.SMEM)] + [vmem] * len(operands),
        out_specs=(vmem, vmem),
        compiler_params=params(),
        name="mix",
    )(length, *operands)


def emit_kernel(w_ref, mixed_ref, u_ref, out_ref):
    total = jnp.dot(w_ref[...], mixed_ref[...], preferred_element_type=jnp.float32)
    out_ref[...] = (u_ref[...].astype(jnp.float32) + total).astype(out_ref.dtype)


def emit(weights, mixed, u):
    vmem = pl.BlockSpec(memory_space=pltpu.VMEM)
    return pl.pallas_call(
        emit_kernel,
        out_shape=jax.ShapeDtypeStruct(u.shape, jnp.bfloat16),
        in_specs=[vmem] * 3,
        out_specs=vmem,
        compiler_params=params(),
        name="emit",
    )(weights, mixed, u)


def local(feeds, newcomers, occupied, gain, value_w, in_w, out_w, emit_w, skip, filters, archive):
    section = lax.axis_index(SECTION)
    layers = lax.axis_size(SECTION)
    ticks = newcomers.shape[0] + 1
    blocks = archive.shape[1]
    positions, width = feeds.shape[1:]
    row = lax.axis_index("y")
    forward, inverse = (jnp.asarray(t) for t in tables(positions, filters.shape[-1]))

    emit_t = emit_w[0].T
    depth = emit_t.shape[1]
    fresh = newcomers.transpose(2, 0, 1).reshape(width, -1)
    shared = lax.all_gather(jnp.concatenate([emit_t, fresh], axis=1), "y", axis=0, tiled=True)
    emit_rows = shared[:, :depth]

    weights = jnp.concatenate([value_w[0].T, in_w[0].T, out_w[0].T], axis=0).astype(jnp.float32)
    weights = (weights * gain).astype(jnp.bfloat16)
    skip_column = skip[0][:, None]

    pairs = [(i, i + 1) for i in range(layers - 1)]
    outputs, spectra = [], []
    part = spread(feeds[0].T, "y")
    for tick in range(ticks):
        u = spread(part, "x")
        length = lax.dynamic_slice_in_dim(occupied, tick - section + layers - 1, 1, 0)
        held = [archive[0, i] for i in range(blocks - min(tick, blocks))]
        mixed, spectrum = mix(
            tick, blocks, length, u, weights, forward, inverse, filters[0], skip_column, held, spectra[::-1][:blocks]
        )
        spectra.append(spectrum)
        mixed = spread(spread(mixed, "y"), "x")
        if tick < ticks - 1:
            part = emit(emit_rows, mixed, part)
            outputs.append(lax.dynamic_slice_in_dim(part, row * width, width, 0))
            arriving = lax.ppermute(part, SECTION, pairs)
            newcomer = shared[:, depth + tick * positions : depth + (tick + 1) * positions]
            part = jnp.where(section == 0, newcomer, arriving)
        else:
            own = lax.dynamic_slice_in_dim(part, row * width, width, 0)
            outputs.append(emit(emit_t, mixed, own))
    return jnp.stack(outputs, axis=0).transpose(0, 2, 1)[None]


def solution(mesh):
    grid = Mesh(mesh.devices.reshape(8, 2, 4, 8), ("z", "core", "x", "y"))
    chan = ("x", "y")
    return jax.shard_map(
        local,
        mesh=grid,
        in_specs=(
            P(SECTION, None, chan),
            P(None, None, chan),
            P(),
            P(SECTION, None),
            P(SECTION, None, chan),
            P(SECTION, None, chan),
            P(SECTION, None, chan),
            P(SECTION, None, chan),
            P(SECTION, chan),
            P(SECTION, None, None, chan, None),
            P(SECTION, None, None, chan, None),
        ),
        out_specs=P(SECTION, None, None, chan),
        check_vma=False,
    )
```

time: 754 us -> 282 us (0.37)
  the two profiles are of different devices: /device:TPU:16 before, /device:TPU:64 now
where the time goes in v1:
time: 282 us; the launch traced here: 280 us
  blocking collectives  162 us (57%)
  waiting for transfers between devices  53.1 us (19%)
  starting transfers between devices  17.9 us (6%)
  local copies, waits for them, and re-layouts  14.2 us (5%)
  between operations  13.7 us (5%)
  Pallas kernels  12.8 us (5%)
  other arithmetic  6.89 us (2%)
    all_to_all x10, blocking collectives, spread(): got = lax.all_to_all(copies, axis, 0, 0, tiled=True)  162 us
    all_to_all x3, waiting for transfers between devices, spread(): got = lax.all_to_all(copies, axis, 0, 0, tiled=True)  35.5 us
    ppermute x3, waiting for transfers between devices, local(): arriving = lax.ppermute(part, SECTION, pairs)  17.6 us
    all_to_all x3, starting transfers between devices, spread(): got = lax.all_to_all(copies, axis, 0, 0, tiled=True)  12.2 us
    pallas_call x4, Pallas kernels, mix(): pl.pallas_call(functools.partial(mix_kernel, tick, blocks), out_shape=(ja...  8.39 us
    ppermute x3, starting transfers between devices, local(): arriving = lax.ppermute(part, SECTION, pairs)  5.75 us
  transfers between devices with their start and end apart: 7, of which 6 were waited for; matrix products, arithmetic and copies ran while one was open for 4% of the time, Pallas kernels for 1%

profile of v1, /device:TPU:64, one launch (start us, length us, event | category | flops | bytes accessed | tf_op | source)
XLA Modules:
  0.0 280.5 jit_solution(49880109133172700)
XLA Ops:
  10.0 18.8 %all_to_all.65 = bf16[8,64,256]{2,1,0:T(8,128)(2,1)S(1)} all-to-all(bf16[8,64,256]{2,1,0:T(8,128)(2,1)S(1)} %broadcast_in_dim.38), channel_id=1, replica_groups=mesh['z'=8,'core'=2,'x'=4,'y'=8] {'y'}, dimensions={0} | all-to-all | bytes 524288 | tf_op jit(solution)/shard_map/all_to_all | solution.py:29
  30.5 4.4 %all-to-all-start.1 = ((bf16[4,512,256]{2,1,0:T(8,128)(2,1)}), bf16[4,512,256]{2,1,0:T(8,128)(2,1)}, u32[]{:S(2)}, u32[]{:S(2)}) async-start(bf16[4,512,256]{2,1,0:T(8,128)(2,1)} %broadcast_in_dim.40), calls=%async_computation.1 | async-start | bytes 2097152 | tf_op jit(solution)/shard_map/all_to_all | solution.py:29
  38.0 10.5 %all-to-all-done.1 = bf16[4,512,256]{2,1,0:T(8,128)(2,1)} async-done(((bf16[4,512,256]{2,1,0:T(8,128)(2,1)}), bf16[4,512,256]{2,1,0:T(8,128)(2,1)}, u32[]{:S(2)}, u32[]{:S(2)}) %all-to-all-start.1) | async-done | bytes 1048608 | tf_op jit(solution)/shard_map/all_to_all | solution.py:29
  49.5 2.9 %mix.4 = (bf16[64,256]{1,0:T(8,128)(2,1)S(1)}, f32[2,64,512]{2,1,0:T(8,128)S(1)}) custom-call(s32[1]{0:T(128)} %get-tuple-element.22.length_ref, bf16[2048,256]{1,0:T(8,128)(2,1)} %bitcast.6.u_ref, bf16[192,2048]{1,0:T(8,128)(2,1)S(1)} %multiply_convert_fusion.w_ref, bf16[256,1024]{1,0:T(8,128)(2,1)S(1)} %copy-done.3, bf16[1024,256]{1,0:T(8,128)(2,1)S(1)} %copy-done.2, ...), custom_call_target="tpu_custom_call" | custom-call | tf_op jit(solution)/shard_map/mix/pallas_call | solution.py:64
  53.1 13.4 %all_to_all.66 = bf16[8,64,256]{2,1,0:T(8,128)(2,1)S(1)} all-to-all(bf16[8,64,256]{2,1,0:T(8,128)(2,1)S(1)} %broadcast_in_dim.41), channel_id=1, replica_groups=mesh['z'=8,'core'=2,'x'=4,'y'=8] {'y'}, dimensions={0} | all-to-all | bytes 524288 | tf_op jit(solution)/shard_map/all_to_all | solution.py:29
  67.5 4.2 %all-to-all-start.3 = ((bf16[4,512,256]{2,1,0:T(8,128)(2,1)}), bf16[4,512,256]{2,1,0:T(8,128)(2,1)}, u32[]{:S(2)}, u32[]{:S(2)}) async-start(bf16[4,512,256]{2,1,0:T(8,128)(2,1)} %broadcast_in_dim.43), calls=%async_computation.3 | async-start | bytes 2097152 | tf_op jit(solution)/shard_map/all_to_all | solution.py:29
  73.5 11.7 %all-to-all-done.3 = bf16[4,512,256]{2,1,0:T(8,128)(2,1)} async-done(((bf16[4,512,256]{2,1,0:T(8,128)(2,1)}), bf16[4,512,256]{2,1,0:T(8,128)(2,1)}, u32[]{:S(2)}, u32[]{:S(2)}) %all-to-all-start.3) | async-done | bytes 1048608 | tf_op jit(solution)/shard_map/all_to_all | solution.py:29
  86.2 2.7 emit.4
  90.7 6.1 %collective-permute-done = bf16[512,256]{1,0:T(8,128)(2,1)} collective-permute-done((bf16[512,256]{1,0:T(8,128)(2,1)}, bf16[512,256]{1,0:T(8,128)(2,1)}, u32[]{:S(2)}, u32[]{:S(2)}) %collective-permute-start) | collective-permute-done | bytes 262176 | tf_op jit(solution)/shard_map/ppermute | solution.py:128
  98.0 16.8 %all_to_all.67 = bf16[4,512,256]{2,1,0:T(8,128)(2,1)S(1)} all-to-all(bf16[4,512,256]{2,1,0:T(8,128)(2,1)S(1)} %broadcast_in_dim.44), channel_id=1, replica_groups=mesh['z'=8,'core'=2,'x'=4,'y'=8] {'x'}, dimensions={0} | all-to-all | bytes 2097152 | tf_op jit(solution)/shard_map/all_to_all | solution.py:29
  116.6 13.5 %all_to_all.68 = bf16[8,64,256]{2,1,0:T(8,128)(2,1)S(1)} all-to-all(bf16[8,64,256]{2,1,0:T(8,128)(2,1)S(1)} %broadcast_in_dim.45), channel_id=1, replica_groups=mesh['z'=8,'core'=2,'x'=4,'y'=8] {'y'}, dimensions={0} | all-to-all | bytes 524288 | tf_op jit(solution)/shard_map/all_to_all | solution.py:29
  130.1 14.5 %all_to_all.69 = bf16[4,512,256]{2,1,0:T(8,128)(2,1)S(1)} all-to-all(bf16[4,512,256]{2,1,0:T(8,128)(2,1)S(1)} %broadcast_in_dim.47), channel_id=1, replica_groups=mesh['z'=8,'core'=2,'x'=4,'y'=8] {'x'}, dimensions={0} | all-to-all | bytes 2097152 | tf_op jit(solution)/shard_map/all_to_all | solution.py:29
  145.3 1.9 collective-permute-start.1
  147.3 5.8 %collective-permute-done.1 = bf16[512,256]{1,0:T(8,128)(2,1)S(1)} collective-permute-done((bf16[512,256]{1,0:T(8,128)(2,1)S(1)}, bf16[512,256]{1,0:T(8,128)(2,1)S(1)}, u32[]{:S(2)}, u32[]{:S(2)}) %collective-permute-start.1) | collective-permute-done | bytes 262176 | tf_op jit(solution)/shard_map/ppermute | solution.py:128
  154.1 18.4 %all_to_all.70 = bf16[4,512,256]{2,1,0:T(8,128)(2,1)S(1)} all-to-all(bf16[4,512,256]{2,1,0:T(8,128)(2,1)S(1)} %broadcast_in_dim.96), channel_id=1, replica_groups=mesh['z'=8,'core'=2,'x'=4,'y'=8] {'x'}, dimensions={0} | all-to-all | bytes 2097152 | tf_op jit(solution)/shard_map/all_to_all | solution.py:29
  174.1 15.1 %all_to_all.71 = bf16[8,64,256]{2,1,0:T(8,128)(2,1)S(1)} all-to-all(bf16[8,64,256]{2,1,0:T(8,128)(2,1)S(1)} %broadcast_in_dim.97), channel_id=1, replica_groups=mesh['z'=8,'core'=2,'x'=4,'y'=8] {'y'}, dimensions={0} | all-to-all | bytes 524288 | tf_op jit(solution)/shard_map/all_to_all | solution.py:29
  189.3 18.0 %all_to_all.72 = bf16[4,512,256]{2,1,0:T(8,128)(2,1)S(1)} all-to-all(bf16[4,512,256]{2,1,0:T(8,128)(2,1)S(1)} %broadcast_in_dim.99), channel_id=1, replica_groups=mesh['z'=8,'core'=2,'x'=4,'y'=8] {'x'}, dimensions={0} | all-to-all | bytes 2097152 | tf_op jit(solution)/shard_map/all_to_all | solution.py:29
  208.1 1.9 collective-permute-start.2
  210.0 5.8 %collective-permute-done.2 = bf16[512,256]{1,0:T(8,128)(2,1)S(1)} collective-permute-done((bf16[512,256]{1,0:T(8,128)(2,1)S(1)}, bf16[512,256]{1,0:T(8,128)(2,1)S(1)}, u32[]{:S(2)}, u32[]{:S(2)}) %collective-permute-start.2) | collective-permute-done | bytes 262176 | tf_op jit(solution)/shard_map/ppermute | solution.py:128
  216.8 18.2 %all_to_all.73 = bf16[4,512,256]{2,1,0:T(8,128)(2,1)S(1)} all-to-all(bf16[4,512,256]{2,1,0:T(8,128)(2,1)S(1)} %broadcast_in_dim.100), channel_id=1, replica_groups=mesh['z'=8,'core'=2,'x'=4,'y'=8] {'x'}, dimensions={0} | all-to-all | bytes 2097152 | tf_op jit(solution)/shard_map/all_to_all | solution.py:29
  235.0 2.2 mix.7
  237.2 15.3 %all_to_all.74 = bf16[8,64,256]{2,1,0:T(8,128)(2,1)S(1)} all-to-all(bf16[8,64,256]{2,1,0:T(8,128)(2,1)S(1)} %broadcast_in_dim.101), channel_id=1, replica_groups=mesh['z'=8,'core'=2,'x'=4,'y'=8] {'y'}, dimensions={0} | all-to-all | bytes 524288 | tf_op jit(solution)/shard_map/all_to_all | solution.py:29
  253.5 3.5 %all-to-all-start.12 = ((bf16[4,512,256]{2,1,0:T(8,128)(2,1)}), bf16[4,512,256]{2,1,0:T(8,128)(2,1)S(1)}, u32[]{:S(2)}, u32[]{:S(2)}) async-start(bf16[4,512,256]{2,1,0:T(8,128)(2,1)} %broadcast_in_dim.103), calls=%async_computation.12 | async-start | bytes 2097152 | tf_op jit(solution)/shard_map/all_to_all | solution.py:29
  259.4 13.3 %all-to-all-done.12 = bf16[4,512,256]{2,1,0:T(8,128)(2,1)S(1)} async-done(((bf16[4,512,256]{2,1,0:T(8,128)(2,1)}), bf16[4,512,256]{2,1,0:T(8,128)(2,1)S(1)}, u32[]{:S(2)}, u32[]{:S(2)}) %all-to-all-start.12) | async-done | bytes 1048608 | tf_op jit(solution)/shard_map/all_to_all | solution.py:29
  (79 shorter events, 28.1 us)
Async XLA Ops:
  6.5 65.3 %all-gather.2.cloned.1.call-start = ((), (), s32[]{:S(2)}) async-start(), calls=%async_computation.13 | async-start | bytes 3244032 | tf_op jit(solution)/shard_map/all_gather | solution.py:106
  28.7 6.2 %copy-start.20 = (f32[1,64]{1,0:T(1,128)S(1)}, f32[1,64]{1,0:T(1,128)}, u32[]{:S(2)}) copy-start(f32[1,64]{1,0:T(1,128)} %param.21) | copy-start | bytes 772
  28.7 6.3 %copy-start.19 = (s32[19]{0:T(128)S(1)}, s32[19]{0:T(128)}, u32[]{:S(2)}) copy-start(s32[19]{0:T(128)} %param.15) | copy-start | bytes 232
  28.7 7.0 %copy-start.17 = (f32[1,3,2,64,512]{4,3,2,1,0:T(8,128)S(1)}, f32[1,3,2,64,512]{4,3,2,1,0:T(8,128)}, u32[]{:S(2)}) copy-start(f32[1,3,2,64,512]{4,3,2,1,0:T(8,128)} %param.23) | copy-start | bytes 2359300
  30.5 6.0 %copy-start.18 = (f32[1,2048]{1,0:T(1,128)S(1)}, f32[1,2048]{1,0:T(1,128)}, u32[]{:S(2)}) copy-start(f32[1,2048]{1,0:T(1,128)} %param.16) | copy-start | bytes 24580
  30.5 18.0 %all-to-all-start.1 = ((bf16[4,512,256]{2,1,0:T(8,128)(2,1)}), bf16[4,512,256]{2,1,0:T(8,128)(2,1)}, u32[]{:S(2)}, u32[]{:S(2)}) async-start(bf16[4,512,256]{2,1,0:T(8,128)(2,1)} %broadcast_in_dim.40), calls=%async_computation.1 | async-start | bytes 2097152 | tf_op jit(solution)/shard_map/all_to_all | solution.py:29
  35.7 12.8 %copy-start = (f32[1,4,2,64,512]{4,3,2,1,0:T(8,128)S(1)}, f32[1,4,2,64,512]{4,3,2,1,0:T(8,128)}, u32[]{:S(2)}) copy-start(f32[1,4,2,64,512]{4,3,2,1,0:T(8,128)} %param.22) | copy-start | bytes 3145732
  35.7 12.8 %copy-start.2 = (bf16[1024,256]{1,0:T(8,128)(2,1)S(1)}, bf16[1024,256]{1,0:T(8,128)(2,1)}, u32[]{:S(2)}) copy-start(bf16[1024,256]{1,0:T(8,128)(2,1)} %constant.54.clone.inv_ref) | copy-start | bytes 1572868
  35.7 12.8 %copy-start.3 = (bf16[256,1024]{1,0:T(8,128)(2,1)S(1)}, bf16[256,1024]{1,0:T(8,128)(2,1)}, u32[]{:S(2)}) copy-start(bf16[256,1024]{1,0:T(8,128)(2,1)} %constant.53.clone.fwd_ref) | copy-start | bytes 1572868
  36.5 15.9 %copy-start.5 = (f32[2,64,512]{2,1,0:T(8,128)}, f32[2,64,512]{2,1,0:T(8,128)S(1)}, u32[]{:S(2)}) copy-start(f32[2,64,512]{2,1,0:T(8,128)S(1)} %get-tuple-element.20.rest_0_) | copy-start | bytes 786436
  36.5 15.9 %copy-start.11 = (f32[2,64,512]{2,1,0:T(8,128)}, f32[2,64,512]{2,1,0:T(8,128)S(1)}, u32[]{:S(2)}) copy-start(f32[2,64,512]{2,1,0:T(8,128)S(1)} %get-tuple-element.21.rest_1_) | copy-start | bytes 786436
  67.5 17.7 %all-to-all-start.3 = ((bf16[4,512,256]{2,1,0:T(8,128)(2,1)}), bf16[4,512,256]{2,1,0:T(8,128)(2,1)}, u32[]{:S(2)}, u32[]{:S(2)}) async-start(bf16[4,512,256]{2,1,0:T(8,128)(2,1)} %broadcast_in_dim.43), calls=%async_computation.3 | async-start | bytes 2097152 | tf_op jit(solution)/shard_map/all_to_all | solution.py:29
  88.8 8.0 %collective-permute-start = (bf16[512,256]{1,0:T(8,128)(2,1)}, bf16[512,256]{1,0:T(8,128)(2,1)}, u32[]{:S(2)}, u32[]{:S(2)}) collective-permute-start(bf16[512,256]{1,0:T(8,128)(2,1)} %emit.4), channel_id=1, source_target_pairs={{0,32},{32,64},{64,96},{96,128},{128,160},{160,192},{192,224},{224... | collective-permute-start | bytes 786440 | tf_op jit(solution)/shard_map/ppermute | solution.py:128
  97.9 17.0 %copy-start.1 = (f32[1,4,2,64,512]{4,3,2,1,0:T(8,128)S(1)}, f32[1,4,2,64,512]{4,3,2,1,0:T(8,128)}, u32[]{:S(2)}) copy-start(f32[1,4,2,64,512]{4,3,2,1,0:T(8,128)} %param.22) | copy-start | bytes 3145732
  97.9 17.0 %copy-start.4 = (bf16[256,1024]{1,0:T(8,128)(2,1)S(1)}, bf16[256,1024]{1,0:T(8,128)(2,1)}, u32[]{:S(2)}) copy-start(bf16[256,1024]{1,0:T(8,128)(2,1)} %constant.53.clone.fwd_ref) | copy-start | bytes 1572868
  97.9 17.0 %copy-start.6 = (f32[2,64,512]{2,1,0:T(8,128)S(1)}, f32[2,64,512]{2,1,0:T(8,128)}, u32[]{:S(2)}) copy-start(f32[2,64,512]{2,1,0:T(8,128)} %copy-done.5) | copy-start | bytes 786436
  97.9 17.0 %copy-start.10 = (f32[2,64,512]{2,1,0:T(8,128)S(1)}, f32[2,64,512]{2,1,0:T(8,128)}, u32[]{:S(2)}) copy-start(f32[2,64,512]{2,1,0:T(8,128)} %copy-done.9) | copy-start | bytes 786436
  97.9 17.0 %copy-start.12 = (f32[2,64,512]{2,1,0:T(8,128)S(1)}, f32[2,64,512]{2,1,0:T(8,128)}, u32[]{:S(2)}) copy-start(f32[2,64,512]{2,1,0:T(8,128)} %copy-done.11) | copy-start | bytes 786436
  145.3 8.7 %copy-start.15 = (bf16[512,256]{1,0:T(8,128)(2,1)}, bf16[512,256]{1,0:T(8,128)(2,1)S(1)}, u32[]{:S(2)}) copy-start(bf16[512,256]{1,0:T(8,128)(2,1)S(1)} %emit.5) | copy-start | bytes 786436
  145.3 7.7 %collective-permute-start.1 = (bf16[512,256]{1,0:T(8,128)(2,1)S(1)}, bf16[512,256]{1,0:T(8,128)(2,1)S(1)}, u32[]{:S(2)}, u32[]{:S(2)}) collective-permute-start(bf16[512,256]{1,0:T(8,128)(2,1)S(1)} %emit.5), channel_id=1, source_target_pairs={{0,32},{32,64},{64,96},{96,128},{128,160},{160,192},{192,224},{224... | collective-permute-start | bytes 786440 | tf_op jit(solution)/shard_map/ppermute | solution.py:128
  208.1 27.0 %copy-start.16 = (bf16[512,256]{1,0:T(8,128)(2,1)}, bf16[512,256]{1,0:T(8,128)(2,1)S(1)}, u32[]{:S(2)}) copy-start(bf16[512,256]{1,0:T(8,128)(2,1)S(1)} %emit.6) | copy-start | bytes 786436
  208.1 7.7 %collective-permute-start.2 = (bf16[512,256]{1,0:T(8,128)(2,1)S(1)}, bf16[512,256]{1,0:T(8,128)(2,1)S(1)}, u32[]{:S(2)}, u32[]{:S(2)}) collective-permute-start(bf16[512,256]{1,0:T(8,128)(2,1)S(1)} %emit.6), channel_id=1, source_target_pairs={{0,32},{32,64},{64,96},{96,128},{128,160},{160,192},{192,224},{224... | collective-permute-start | bytes 786440 | tf_op jit(solution)/shard_map/ppermute | solution.py:128
  252.5 20.1 %copy-start.14 = (bf16[1,2048,64]{1,2,0:T(8,128)(2,1)S(1)}, bf16[1,2048,64]{1,2,0:T(8,128)(2,1)}, u32[]{:S(2)}) copy-start(bf16[1,2048,64]{1,2,0:T(8,128)(2,1)} %param.20) | copy-start | bytes 786436
  253.5 19.1 %all-to-all-start.12 = ((bf16[4,512,256]{2,1,0:T(8,128)(2,1)}), bf16[4,512,256]{2,1,0:T(8,128)(2,1)S(1)}, u32[]{:S(2)}, u32[]{:S(2)}) async-start(bf16[4,512,256]{2,1,0:T(8,128)(2,1)} %broadcast_in_dim.103), calls=%async_computation.12 | async-start | bytes 2097152 | tf_op jit(solution)/shard_map/all_to_all | solution.py:29
  (4 other events, 3.3 us)
Sparse Core Ops, SparseCore 0:
  9.4 52.1 all-gather.1

commit v2 on v1

v2 whole, which is shorter than its diff:
```python
import functools

import jax
import jax.numpy as jnp
import numpy as np
from jax import lax
from jax.experimental import pallas as pl
from jax.experimental.pallas import tpu as pltpu
from jax.sharding import Mesh
from jax.sharding import PartitionSpec as P

SECTION = ("z", "core")
EXTRA = 16


def call(body, out, operands, name, smem=0):
    vmem = pl.BlockSpec(memory_space=pltpu.VMEM)
    scalars = pl.BlockSpec(memory_space=pltpu.SMEM)
    return pl.pallas_call(
        body,
        out_shape=out,
        in_specs=[scalars] * smem + [vmem] * (len(operands) - smem),
        out_specs=jax.tree.map(lambda _: vmem, out),
        compiler_params=pltpu.CompilerParams(vmem_limit_bytes=40 * 1024 * 1024),
        name=name,
    )(*operands)


def tables(length, period):
    phase = np.arange(length)[:, None] * np.arange(period)[None, :] % period
    angle = phase * (2.0 * np.pi / period)
    forward = np.concatenate([np.cos(angle), -np.sin(angle)], axis=1)
    return forward.astype(jnp.bfloat16), (forward.T / period).astype(jnp.bfloat16)


def swap(blocks, axis):
    return lax.all_to_all(blocks, axis, 0, 0, tiled=True)


def gather_rows(copies):
    got = swap(copies, "y")
    return got.reshape((-1, got.shape[-1]))


def gate_terms_kernel(w_ref, gain_ref, u_ref, out_ref):
    groups, rows, positions = out_ref.shape
    rows -= EXTRA
    u = u_ref[...].astype(jnp.float32)
    square = jnp.sum(u * u, axis=0, keepdims=True)
    upper = square.astype(jnp.bfloat16).astype(jnp.float32)
    at = lax.broadcasted_iota(jnp.int32, (EXTRA, positions), 0)
    extra = jnp.where(at == 0, upper, jnp.where(at == 1, square - upper, 0.0)).astype(out_ref.dtype)
    scaled = u * gain_ref[...]
    high = scaled.astype(jnp.bfloat16)
    low = (scaled - high.astype(jnp.float32)).astype(jnp.bfloat16)
    for x in range(groups):
        w = w_ref[x, :rows]
        term = jnp.dot(w, high, preferred_element_type=jnp.float32)
        term += jnp.dot(w, low, preferred_element_type=jnp.float32)
        out_ref[x, :rows] = term.astype(out_ref.dtype)
        out_ref[x, rows:] = extra


def mix_kernel(past, features, length_ref, terms_ref, fwd_ref, inv_ref, filt_ref, skip_ref, *rest):
    lagged, (mixed_ref, spec_ref) = rest[:-2], rest[-2:]
    copies, width, positions = mixed_ref.shape
    period = fwd_ref.shape[1] // 2
    terms = jnp.sum(terms_ref[...].astype(jnp.float32), axis=0)
    square = terms[3 * width : 3 * width + 1] + terms[3 * width + 1 : 3 * width + 2]
    gates = terms[: 3 * width] * lax.rsqrt(square * (1.0 / features) + 1e-06)
    live = lax.broadcasted_iota(jnp.int32, (1, positions), 1) < length_ref[0]
    driven = jnp.where(live, gates[width : 2 * width] * gates[:width], 0.0)
    spectrum = jnp.dot(driven.astype(jnp.bfloat16), fwd_ref[...], preferred_element_type=jnp.float32)
    real, imag = spectrum[:, :period], spectrum[:, period:]
    spec_ref[0] = real
    spec_ref[1] = imag
    zreal = filt_ref[0, 0] * real - filt_ref[0, 1] * imag
    zimag = filt_ref[0, 0] * imag + filt_ref[0, 1] * real
    for lag, ref in enumerate(lagged, 1):
        if lag <= past:
            first, second = ref[0], ref[1]
        else:
            first, second = ref[lag - past - 1, 0], ref[lag - past - 1, 1]
        zreal += filt_ref[lag, 0] * first - filt_ref[lag, 1] * second
        zimag += filt_ref[lag, 0] * second + filt_ref[lag, 1] * first
    packed = jnp.concatenate([zreal, zimag], axis=1).astype(jnp.bfloat16)
    conv = jnp.dot(packed, inv_ref[...], preferred_element_type=jnp.float32)
    mixed = (gates[2 * width :] * (conv + skip_ref[...] * driven)).astype(mixed_ref.dtype)
    for y in range(copies):
        mixed_ref[y] = mixed


def emit_terms_kernel(w_ref, mixed_ref, out_ref):
    groups, rows, _ = out_ref.shape
    mixed = mixed_ref[...]
    for x in range(groups):
        w = w_ref[x, w_ref.shape[1] - rows :]
        out_ref[x] = jnp.dot(w, mixed, preferred_element_type=jnp.float32).astype(out_ref.dtype)


def add_kernel(terms_ref, own_ref, out_ref):
    total = own_ref[...].astype(jnp.float32) + jnp.sum(terms_ref[...].astype(jnp.float32), axis=0)
    out_ref[...] = total.astype(out_ref.dtype)


def add_and_send_kernel(last_ref, terms_ref, own_ref, fresh_ref, out_ref, send_ref):
    add_kernel(terms_ref, own_ref, out_ref)
    send_ref[...] = jnp.where(last_ref[0] == 1, fresh_ref[...], out_ref[...])


def local(feeds, newcomers, occupied, gain, value_w, in_w, out_w, emit_w, skip, filters, archive):
    section = lax.axis_index(SECTION)
    layers = lax.axis_size(SECTION)
    groups, copies = lax.axis_size("x"), lax.axis_size("y")
    ticks = newcomers.shape[0] + 1
    blocks = archive.shape[1]
    positions, width = feeds.shape[1:]
    features = gain.shape[1]
    rows = features // groups
    bf16 = functools.partial(jax.ShapeDtypeStruct, dtype=jnp.bfloat16)
    f32 = functools.partial(jax.ShapeDtypeStruct, dtype=jnp.float32)
    forward, inverse = (jnp.asarray(t) for t in tables(positions, filters.shape[-1]))

    own = feeds[0].T
    part = gather_rows(jnp.broadcast_to(own[None], (copies,) + own.shape))
    weights = jnp.concatenate([value_w[0], in_w[0], out_w[0], emit_w[0]], axis=1).T
    weights = swap(weights.reshape(-1, groups, rows).transpose(1, 0, 2), "x")
    gain_column = lax.dynamic_slice_in_dim(gain[0], lax.axis_index("x") * rows, rows, 0)[:, None]
    skip_column = skip[0][:, None]
    fresh = newcomers.transpose(0, 2, 1)
    last = (section == layers - 1).astype(jnp.int32)[None]

    ring = [(i, (i + 1) % layers) for i in range(layers)]
    outputs, spectra = [], []
    for tick in range(ticks):
        terms = call(
            gate_terms_kernel,
            bf16((groups, 3 * width + EXTRA, positions)),
            [weights, gain_column, part],
            "gate_terms",
        )
        terms = swap(terms, "x")
        length = lax.dynamic_slice_in_dim(occupied, tick - section + layers - 1, 1, 0)
        past = min(tick, blocks)
        lagged = spectra[::-1][:past] + [archive[0]] * (blocks - past)
        mixed, spectrum = call(
            functools.partial(mix_kernel, past, features),
            (bf16((copies, width, positions)), f32((2, width, filters.shape[-1]))),
            [length, terms, forward, inverse, filters[0], skip_column] + lagged,
            "mix",
            smem=1,
        )
        spectra.append(spectrum)
        terms = call(
            emit_terms_kernel,
            bf16((groups, width, positions)),
            [weights, gather_rows(mixed)],
            "emit_terms",
        )
        terms = swap(terms, "x")
        if tick < ticks - 1:
            out, send = call(
                add_and_send_kernel, (bf16(own.shape), bf16(own.shape)), [last, terms, own, fresh[tick]], "add", smem=1
            )
            own = lax.ppermute(send, SECTION, ring)
            part = gather_rows(jnp.broadcast_to(own[None], (copies,) + own.shape))
        else:
            out = call(add_kernel, bf16(own.shape), [terms, own], "add")
        outputs.append(out)
    return jnp.stack(outputs, axis=0).transpose(0, 2, 1)[None]


def solution(mesh):
    grid = Mesh(mesh.devices.reshape(8, 2, 4, 8), ("z", "core", "x", "y"))
    chan = ("x", "y")
    return jax.shard_map(
        local,
        mesh=grid,
        in_specs=(
            P(SECTION, None, chan),
            P(None, None, chan),
            P(),
            P(SECTION, None),
            P(SECTION, None, chan),
            P(SECTION, None, chan),
            P(SECTION, None, chan),
            P(SECTION, None, chan),
            P(SECTION, chan),
            P(SECTION, None, None, chan, None),
            P(SECTION, None, None, chan, None),
        ),
        out_specs=P(SECTION, None, None, chan),
        check_vma=False,
    )
```

time: 282 us -> 250 us (0.89)
  between operations: 13.7 us -> 0.3 us
  waiting for transfers between devices: 53.1 us -> 41.6 us
  other arithmetic: 6.89 us -> 1.41 us
    ppermute x3, waiting for transfers between devices: 17.6 us -> 9.98 us  [local(): own = lax.ppermute(send, SECTION, ring)]
    all_to_all x3 -> x4, starting transfers between devices: 12.2 us -> 19.6 us  [swap(): return lax.all_to_all(blocks, axis, 0, 0, tiled=True)]
    ppermute x3, starting transfers between devices: 5.75 us -> 0.06 us  [local(): own = lax.ppermute(send, SECTION, ring)]
    unnamed x42 -> x46, local copies, waits for them, and re-layouts: 3.36 us -> 8.71 us
    all_to_all x3 -> x4, waiting for transfers between devices: 35.5 us -> 31.6 us  [swap(): return lax.all_to_all(blocks, axis, 0, 0, tiled=True)]
    select_n x3 -> x0, other arithmetic: 3.02 us -> none  [local(): part = jnp.where(section == 0, newcomer, arriving)]
    all_to_all x10 -> x13, blocking collectives: 162 us -> 160 us  [swap(): return lax.all_to_all(blocks, axis, 0, 0, tiled=True)]
    pallas_call x8 -> x16, Pallas kernels: 12.8 us -> 11.3 us  [call(): pl.pallas_call(body, out_shape=out, in_specs=[scalars] * smem + [vmem] *...]
  transfers between devices with their start and end apart: 7 -> 7, of which waited for: 6 -> 7; matrix products, arithmetic and copies ran while one was open for 4% -> 3% of each run, Pallas kernels for 1% -> 0%
where the time goes in v2:
time: 250 us; the launch traced here: 248 us
  blocking collectives  160 us (64%)
  waiting for transfers between devices  41.6 us (17%)
  starting transfers between devices  19.6 us (8%)
  local copies, waits for them, and re-layouts  14.6 us (6%)
  Pallas kernels  11.3 us (5%)
    all_to_all x13, blocking collectives, swap(): return lax.all_to_all(blocks, axis, 0, 0, tiled=True)  160 us
    all_to_all x4, waiting for transfers between devices, swap(): return lax.all_to_all(blocks, axis, 0, 0, tiled=True)  31.6 us
    all_to_all x4, starting transfers between devices, swap(): return lax.all_to_all(blocks, axis, 0, 0, tiled=True)  19.6 us
    pallas_call x16, Pallas kernels, call(): pl.pallas_call(body, out_shape=out, in_specs=[scalars] * smem + [vmem] *...  11.3 us
    ppermute x3, waiting for transfers between devices, local(): own = lax.ppermute(send, SECTION, ring)  9.98 us
    unnamed x46, local copies, waits for them, and re-layouts  8.71 us
  transfers between devices with their start and end apart: 7, of which 7 were waited for; matrix products, arithmetic and copies ran while one was open for 3% of the time, Pallas kernels for 0%

profile of v2, /device:TPU:64, one launch (start us, length us, event | category | flops | bytes accessed | tf_op | source)
XLA Modules:
  0.0 248.4 jit_solution(16037286545191115326)
XLA Ops:
  1.5 7.2 %all-to-all-start.1 = ((bf16[8,64,256]{2,1,0:T(8,128)(2,1)}), bf16[8,64,256]{2,1,0:T(8,128)(2,1)S(1)}, u32[]{:S(2)}, u32[]{:S(2)}) async-start(bf16[8,64,256]{2,1,0:T(8,128)(2,1)} %broadcast_in_dim.38), calls=%async_computation.1 | async-start | bytes 524288 | tf_op jit(solution)/shard_map/all_to_all | solution.py:37
  13.0 7.7 %all-to-all-done.1 = bf16[8,64,256]{2,1,0:T(8,128)(2,1)S(1)} async-done(((bf16[8,64,256]{2,1,0:T(8,128)(2,1)}), bf16[8,64,256]{2,1,0:T(8,128)(2,1)S(1)}, u32[]{:S(2)}, u32[]{:S(2)}) %all-to-all-start.1) | async-done | bytes 262176 | tf_op jit(solution)/shard_map/all_to_all | solution.py:37
  21.3 4.3 %all-to-all-start = ((bf16[4,256,512]{2,1,0:T(8,128)(2,1)}), bf16[4,256,512]{2,1,0:T(8,128)(2,1)S(1)}, u32[]{:S(2)}, u32[]{:S(2)}) async-start(bf16[4,256,512]{2,1,0:T(8,128)(2,1)} %bitcast.7), calls=%async_computation | async-start | bytes 2097152 | tf_op jit(solution)/shard_map/all_to_all | solution.py:37
  26.5 12.5 %all-to-all-done.w_ref = bf16[4,256,512]{2,1,0:T(8,128)(2,1)S(1)} async-done(((bf16[4,256,512]{2,1,0:T(8,128)(2,1)}), bf16[4,256,512]{2,1,0:T(8,128)(2,1)S(1)}, u32[]{:S(2)}, u32[]{:S(2)}) %all-to-all-start) | async-done | bytes 1048608 | tf_op jit(solution)/shard_map/all_to_all | solution.py:37
  42.3 4.1 %all-to-all-start.2 = ((bf16[4,208,256]{2,1,0:T(8,128)(2,1)}), bf16[4,208,256]{2,1,0:T(8,128)(2,1)}, u32[]{:S(2)}, u32[]{:S(2)}) async-start(bf16[4,208,256]{2,1,0:T(8,128)(2,1)} %copy-done.10), calls=%async_computation.2 | async-start | bytes 851968 | tf_op jit(solution)/shard_map/all_to_all | solution.py:37
  47.2 6.9 %all-to-all-done.2.terms_ref = bf16[4,208,256]{2,1,0:T(8,128)(2,1)} async-done(((bf16[4,208,256]{2,1,0:T(8,128)(2,1)}), bf16[4,208,256]{2,1,0:T(8,128)(2,1)}, u32[]{:S(2)}, u32[]{:S(2)}) %all-to-all-start.2) | async-done | bytes 426016 | tf_op jit(solution)/shard_map/all_to_all | solution.py:37
  58.1 13.3 %all_to_all.85 = bf16[8,64,256]{2,1,0:T(8,128)(2,1)S(1)} all-to-all(bf16[8,64,256]{2,1,0:T(8,128)(2,1)S(1)} %get-tuple-element.18), channel_id=1, replica_groups=mesh['z'=8,'core'=2,'x'=4,'y'=8] {'y'}, dimensions={0} | all-to-all | bytes 524288 | tf_op jit(solution)/shard_map/all_to_all | solution.py:37
  72.4 4.0 %all-to-all-start.4 = ((bf16[4,64,256]{2,1,0:T(8,128)(2,1)}), bf16[4,64,256]{2,1,0:T(8,128)(2,1)}, u32[]{:S(2)}, u32[]{:S(2)}) async-start(bf16[4,64,256]{2,1,0:T(8,128)(2,1)} %copy-done.13), calls=%async_computation.4 | async-start | bytes 262144 | tf_op jit(solution)/shard_map/all_to_all | solution.py:37
  77.8 4.6 %all-to-all-done.4.terms_ref = bf16[4,64,256]{2,1,0:T(8,128)(2,1)} async-done(((bf16[4,64,256]{2,1,0:T(8,128)(2,1)}), bf16[4,64,256]{2,1,0:T(8,128)(2,1)}, u32[]{:S(2)}, u32[]{:S(2)}) %all-to-all-start.4) | async-done | bytes 131104 | tf_op jit(solution)/shard_map/all_to_all | solution.py:37
  84.1 3.3 %collective-permute-done.own_ref = bf16[64,256]{1,0:T(8,128)(2,1)S(1)} collective-permute-done((bf16[64,256]{1,0:T(8,128)(2,1)S(1)}, bf16[64,256]{1,0:T(8,128)(2,1)S(1)}, u32[]{:S(2)}, u32[]{:S(2)}) %collective-permute-start) | collective-permute-done | bytes 32800 | tf_op jit(solution)/shard_map/ppermute | solution.py:165
  87.5 14.9 %all_to_all.86 = bf16[8,64,256]{2,1,0:T(8,128)(2,1)S(1)} all-to-all(bf16[8,64,256]{2,1,0:T(8,128)(2,1)S(1)} %broadcast_in_dim.39), channel_id=1, replica_groups=mesh['z'=8,'core'=2,'x'=4,'y'=8] {'y'}, dimensions={0} | all-to-all | bytes 524288 | tf_op jit(solution)/shard_map/all_to_all | solution.py:37
  103.1 11.3 %all_to_all.87.terms_ref = bf16[4,208,256]{2,1,0:T(8,128)(2,1)S(1)} all-to-all(bf16[4,208,256]{2,1,0:T(8,128)(2,1)S(1)} %gate_terms.5), channel_id=1, replica_groups=mesh['z'=8,'core'=2,'x'=4,'y'=8] {'x'}, dimensions={0} | all-to-all | bytes 851968 | tf_op jit(solution)/shard_map/all_to_all | solution.py:37
  115.5 13.9 %all_to_all.88 = bf16[8,64,256]{2,1,0:T(8,128)(2,1)S(1)} all-to-all(bf16[8,64,256]{2,1,0:T(8,128)(2,1)S(1)} %get-tuple-element.22), channel_id=1, replica_groups=mesh['z'=8,'core'=2,'x'=4,'y'=8] {'y'}, dimensions={0} | all-to-all | bytes 524288 | tf_op jit(solution)/shard_map/all_to_all | solution.py:37
  129.8 8.4 %all_to_all.89.terms_ref = bf16[4,64,256]{2,1,0:T(8,128)(2,1)S(1)} all-to-all(bf16[4,64,256]{2,1,0:T(8,128)(2,1)S(1)} %emit_terms.5), channel_id=1, replica_groups=mesh['z'=8,'core'=2,'x'=4,'y'=8] {'x'}, dimensions={0} | all-to-all | bytes 262144 | tf_op jit(solution)/shard_map/all_to_all | solution.py:37
  138.2 3.3 %collective-permute-done.1.own_ref = bf16[64,256]{1,0:T(8,128)(2,1)S(1)} collective-permute-done((bf16[64,256]{1,0:T(8,128)(2,1)S(1)}, bf16[64,256]{1,0:T(8,128)(2,1)S(1)}, u32[]{:S(2)}, u32[]{:S(2)}) %collective-permute-start.1) | collective-permute-done | bytes 32800 | tf_op jit(solution)/shard_map/ppermute | solution.py:165
  141.5 14.9 %all_to_all.90 = bf16[8,64,256]{2,1,0:T(8,128)(2,1)S(1)} all-to-all(bf16[8,64,256]{2,1,0:T(8,128)(2,1)S(1)} %broadcast_in_dim.40), channel_id=1, replica_groups=mesh['z'=8,'core'=2,'x'=4,'y'=8] {'y'}, dimensions={0} | all-to-all | bytes 524288 | tf_op jit(solution)/shard_map/all_to_all | solution.py:37
  157.1 11.3 %all_to_all.91.terms_ref = bf16[4,208,256]{2,1,0:T(8,128)(2,1)S(1)} all-to-all(bf16[4,208,256]{2,1,0:T(8,128)(2,1)S(1)} %gate_terms.6), channel_id=1, replica_groups=mesh['z'=8,'core'=2,'x'=4,'y'=8] {'x'}, dimensions={0} | all-to-all | bytes 851968 | tf_op jit(solution)/shard_map/all_to_all | solution.py:37
  169.6 13.9 %all_to_all.92 = bf16[8,64,256]{2,1,0:T(8,128)(2,1)S(1)} all-to-all(bf16[8,64,256]{2,1,0:T(8,128)(2,1)S(1)} %get-tuple-element.26), channel_id=1, replica_groups=mesh['z'=8,'core'=2,'x'=4,'y'=8] {'y'}, dimensions={0} | all-to-all | bytes 524288 | tf_op jit(solution)/shard_map/all_to_all | solution.py:37
  183.8 8.4 %all_to_all.93.terms_ref = bf16[4,64,256]{2,1,0:T(8,128)(2,1)S(1)} all-to-all(bf16[4,64,256]{2,1,0:T(8,128)(2,1)S(1)} %emit_terms.6), channel_id=1, replica_groups=mesh['z'=8,'core'=2,'x'=4,'y'=8] {'x'}, dimensions={0} | all-to-all | bytes 262144 | tf_op jit(solution)/shard_map/all_to_all | solution.py:37
  192.2 3.3 %collective-permute-done.2.own_ref = bf16[64,256]{1,0:T(8,128)(2,1)S(1)} collective-permute-done((bf16[64,256]{1,0:T(8,128)(2,1)S(1)}, bf16[64,256]{1,0:T(8,128)(2,1)S(1)}, u32[]{:S(2)}, u32[]{:S(2)}) %collective-permute-start.2) | collective-permute-done | bytes 32800 | tf_op jit(solution)/shard_map/ppermute | solution.py:165
  195.6 15.7 %all_to_all.94 = bf16[8,64,256]{2,1,0:T(8,128)(2,1)S(1)} all-to-all(bf16[8,64,256]{2,1,0:T(8,128)(2,1)S(1)} %broadcast_in_dim.41), channel_id=1, replica_groups=mesh['z'=8,'core'=2,'x'=4,'y'=8] {'y'}, dimensions={0} | all-to-all | bytes 524288 | tf_op jit(solution)/shard_map/all_to_all | solution.py:37
  211.9 11.4 %all_to_all.95.terms_ref = bf16[4,208,256]{2,1,0:T(8,128)(2,1)S(1)} all-to-all(bf16[4,208,256]{2,1,0:T(8,128)(2,1)S(1)} %gate_terms.7), channel_id=1, replica_groups=mesh['z'=8,'core'=2,'x'=4,'y'=8] {'x'}, dimensions={0} | all-to-all | bytes 851968 | tf_op jit(solution)/shard_map/all_to_all | solution.py:37
  225.1 13.9 %all_to_all.96 = bf16[8,64,256]{2,1,0:T(8,128)(2,1)S(1)} all-to-all(bf16[8,64,256]{2,1,0:T(8,128)(2,1)S(1)} %get-tuple-element.30), channel_id=1, replica_groups=mesh['z'=8,'core'=2,'x'=4,'y'=8] {'y'}, dimensions={0} | all-to-all | bytes 524288 | tf_op jit(solution)/shard_map/all_to_all | solution.py:37
  239.3 8.4 %all_to_all.97.terms_ref = bf16[4,64,256]{2,1,0:T(8,128)(2,1)S(1)} all-to-all(bf16[4,64,256]{2,1,0:T(8,128)(2,1)S(1)} %emit_terms.7), channel_id=1, replica_groups=mesh['z'=8,'core'=2,'x'=4,'y'=8] {'x'}, dimensions={0} | all-to-all | bytes 262144 | tf_op jit(solution)/shard_map/all_to_all | solution.py:37
  (77 shorter events, 27.4 us)
Async XLA Ops:
  0.0 25.6 %copy-start = (f32[1,2048]{1,0:T(1,128)S(1)}, f32[1,2048]{1,0:T(1,128)}, u32[]{:S(2)}) copy-start(f32[1,2048]{1,0:T(1,128)} %param.16) | copy-start | bytes 24580
  0.0 10.0 %copy-start.16 = (bf16[1,2048,64]{1,2,0:T(8,128)(2,1)S(1)}, bf16[1,2048,64]{1,2,0:T(8,128)(2,1)}, u32[]{:S(2)}) copy-start(bf16[1,2048,64]{1,2,0:T(8,128)(2,1)} %param.19) | copy-start | bytes 786436
  1.5 8.8 %copy-start.17 = (bf16[1,2048,64]{1,2,0:T(8,128)(2,1)S(1)}, bf16[1,2048,64]{1,2,0:T(8,128)(2,1)}, u32[]{:S(2)}) copy-start(bf16[1,2048,64]{1,2,0:T(8,128)(2,1)} %param.18) | copy-start | bytes 786436
  1.5 19.1 %all-to-all-start.1 = ((bf16[8,64,256]{2,1,0:T(8,128)(2,1)}), bf16[8,64,256]{2,1,0:T(8,128)(2,1)S(1)}, u32[]{:S(2)}, u32[]{:S(2)}) async-start(bf16[8,64,256]{2,1,0:T(8,128)(2,1)} %broadcast_in_dim.38), calls=%async_computation.1 | async-start | bytes 524288 | tf_op jit(solution)/shard_map/all_to_all | solution.py:37
  8.8 1.9 copy-start.18
  21.3 17.6 %all-to-all-start = ((bf16[4,256,512]{2,1,0:T(8,128)(2,1)}), bf16[4,256,512]{2,1,0:T(8,128)(2,1)S(1)}, u32[]{:S(2)}, u32[]{:S(2)}) async-start(bf16[4,256,512]{2,1,0:T(8,128)(2,1)} %bitcast.7), calls=%async_computation | async-start | bytes 2097152 | tf_op jit(solution)/shard_map/all_to_all | solution.py:37
  38.9 1.0 copy-start.6
  39.9 0.9 copy-start.12
  40.8 5.6 %copy-start.20 = (f32[1,64]{1,0:T(1,128)S(1)}, f32[1,64]{1,0:T(1,128)}, u32[]{:S(2)}) copy-start(f32[1,64]{1,0:T(1,128)} %param.21) | copy-start | bytes 772
  40.8 5.7 %copy-start.19 = (s32[19]{0:T(128)S(1)}, s32[19]{0:T(128)}, u32[]{:S(2)}) copy-start(s32[19]{0:T(128)} %param.15) | copy-start | bytes 232
  40.8 13.2 %copy-start.1 = (f32[1,3,2,64,512]{4,3,2,1,0:T(8,128)S(1)}, f32[1,3,2,64,512]{4,3,2,1,0:T(8,128)}, u32[]{:S(2)}) copy-start(f32[1,3,2,64,512]{4,3,2,1,0:T(8,128)} %param.23) | copy-start | bytes 2359300
  40.9 13.2 %copy-start.2 = (f32[1,4,2,64,512]{4,3,2,1,0:T(8,128)S(1)}, f32[1,4,2,64,512]{4,3,2,1,0:T(8,128)}, u32[]{:S(2)}) copy-start(f32[1,4,2,64,512]{4,3,2,1,0:T(8,128)} %param.22) | copy-start | bytes 3145732
  40.9 13.2 %copy-start.3 = (bf16[256,1024]{1,0:T(8,128)(2,1)S(1)}, bf16[256,1024]{1,0:T(8,128)(2,1)}, u32[]{:S(2)}) copy-start(bf16[256,1024]{1,0:T(8,128)(2,1)} %constant.57.clone.fwd_ref) | copy-start | bytes 1572868
  42.3 11.7 %all-to-all-start.2 = ((bf16[4,208,256]{2,1,0:T(8,128)(2,1)}), bf16[4,208,256]{2,1,0:T(8,128)(2,1)}, u32[]{:S(2)}, u32[]{:S(2)}) async-start(bf16[4,208,256]{2,1,0:T(8,128)(2,1)} %copy-done.10), calls=%async_computation.2 | async-start | bytes 851968 | tf_op jit(solution)/shard_map/all_to_all | solution.py:37
  54.1 1.0 copy-start.4
  71.4 11.0 %copy-start.14 = (bf16[1,256,64]{1,2,0:T(8,128)(2,1)S(1)}, bf16[1,256,64]{1,2,0:T(8,128)(2,1)}, u32[]{:S(2)}) copy-start(bf16[1,256,64]{1,2,0:T(8,128)(2,1)} %param.13) | copy-start | bytes 98308
  72.4 10.0 %all-to-all-start.4 = ((bf16[4,64,256]{2,1,0:T(8,128)(2,1)}), bf16[4,64,256]{2,1,0:T(8,128)(2,1)}, u32[]{:S(2)}, u32[]{:S(2)}) async-start(bf16[4,64,256]{2,1,0:T(8,128)(2,1)} %copy-done.13), calls=%async_computation.4 | async-start | bytes 262144 | tf_op jit(solution)/shard_map/all_to_all | solution.py:37
  82.4 20.0 %copy-start.7 = (f32[512,1]{1,0:T(8,128)S(1)}, f32[512,1]{1,0:T(8,128)}, u32[]{:S(2)}) copy-start(f32[512,1]{1,0:T(8,128)} %copy.23.gain_ref) | copy-start | bytes 6148
  82.4 0.8 copy-start.15
  84.1 3.4 %collective-permute-start = (bf16[64,256]{1,0:T(8,128)(2,1)S(1)}, bf16[64,256]{1,0:T(8,128)(2,1)S(1)}, u32[]{:S(2)}, u32[]{:S(2)}) collective-permute-start(bf16[64,256]{1,0:T(8,128)(2,1)S(1)} %get-tuple-element.20), channel_id=1, source_target_pairs={{0,32},{32,64},{64,96},{96,128},{128,160},{160,192},{192,224},{224... | collective-permute-start | bytes 98312 | tf_op jit(solution)/shard_map/ppermute | solution.py:165
  102.4 11.9 %copy-start.5 = (bf16[1024,256]{1,0:T(8,128)(2,1)S(1)}, bf16[1024,256]{1,0:T(8,128)(2,1)}, u32[]{:S(2)}) copy-start(bf16[1024,256]{1,0:T(8,128)(2,1)} %constant.58.clone.inv_ref) | copy-start | bytes 1572868
  102.4 11.9 %copy-start.9 = (f32[2,64,512]{2,1,0:T(8,128)S(1)}, f32[2,64,512]{2,1,0:T(8,128)}, u32[]{:S(2)}) copy-start(f32[2,64,512]{2,1,0:T(8,128)} %copy-done.8) | copy-start | bytes 786436
  138.2 3.4 %collective-permute-start.1 = (bf16[64,256]{1,0:T(8,128)(2,1)S(1)}, bf16[64,256]{1,0:T(8,128)(2,1)S(1)}, u32[]{:S(2)}, u32[]{:S(2)}) collective-permute-start(bf16[64,256]{1,0:T(8,128)(2,1)S(1)} %get-tuple-element.24), channel_id=1, source_target_pairs={{0,32},{32,64},{64,96},{96,128},{128,160},{160,192},{192,224},{224... | collective-permute-start | bytes 98312 | tf_op jit(solution)/shard_map/ppermute | solution.py:165
  192.2 3.4 %collective-permute-start.2 = (bf16[64,256]{1,0:T(8,128)(2,1)S(1)}, bf16[64,256]{1,0:T(8,128)(2,1)S(1)}, u32[]{:S(2)}, u32[]{:S(2)}) collective-permute-start(bf16[64,256]{1,0:T(8,128)(2,1)S(1)} %get-tuple-element.28), channel_id=1, source_target_pairs={{0,32},{32,64},{64,96},{96,128},{128,160},{160,192},{192,224},{224... | collective-permute-start | bytes 98312 | tf_op jit(solution)/shard_map/ppermute | solution.py:165
  (4 other events, 2.9 us)

commit v3 on v2

v3 whole, which is shorter than its diff:
```python
import functools

import jax
import jax.numpy as jnp
import numpy as np
from jax import lax
from jax.experimental import pallas as pl
from jax.experimental.pallas import tpu as pltpu
from jax.sharding import Mesh
from jax.sharding import PartitionSpec as P

SECTION = ("z", "core")
EXTRA = 16


def call(body, out, operands, name, smem=0):
    vmem = pl.BlockSpec(memory_space=pltpu.VMEM)
    scalars = pl.BlockSpec(memory_space=pltpu.SMEM)
    return pl.pallas_call(
        body,
        out_shape=out,
        in_specs=[scalars] * smem + [vmem] * (len(operands) - smem),
        out_specs=jax.tree.map(lambda _: vmem, out),
        compiler_params=pltpu.CompilerParams(vmem_limit_bytes=40 * 1024 * 1024),
        name=name,
    )(*operands)


def tables(length, period):
    phase = np.arange(length)[:, None] * np.arange(period)[None, :] % period
    angle = phase * (2.0 * np.pi / period)
    forward = np.concatenate([np.cos(angle), -np.sin(angle)], axis=1)
    return forward.astype(jnp.bfloat16), (forward.T / period).astype(jnp.bfloat16)


def swap(blocks, axis):
    return lax.all_to_all(blocks, axis, 0, 0, tiled=True)


def gather_rows(copies):
    got = swap(copies, "y")
    return got.reshape((-1, got.shape[-1]))


def deal_kernel(x_ref, gain_ref, *refs):
    matrices, blocks = refs[: len(refs) // 2], refs[len(refs) // 2 :]
    groups = len(blocks)
    width = matrices[0].shape[0]
    rows = blocks[0].shape[1]
    for step, block in enumerate(blocks):
        start = lax.rem(x_ref[0] + step, groups) * rows
        at = pl.ds(pl.multiple_of(start, rows), rows)
        gain = gain_ref[:, at]
        for m, matrix in enumerate(matrices):
            w = matrix[:, at]
            if m < len(matrices) - 1:
                w = (w.astype(jnp.float32) * gain).astype(w.dtype)
            block[m * width : (m + 1) * width] = w


def history_kernel(filt_ref, held_ref, fwd_ref, inv_ref, known_ref, filt_out, fwd_out, inv_out):
    blocks = held_ref.shape[0]
    for tick in range(blocks):
        real = imag = 0.0
        for lag in range(tick + 1, blocks + 1):
            held = held_ref.at[lag - tick - 1]
            real += filt_ref[lag, 0] * held[0] - filt_ref[lag, 1] * held[1]
            imag += filt_ref[lag, 0] * held[1] + filt_ref[lag, 1] * held[0]
        known_ref[tick, 0] = real
        known_ref[tick, 1] = imag
    filt_out[...] = filt_ref[...]
    fwd_out[...] = fwd_ref[...]
    inv_out[...] = inv_ref[...]


def gate_terms_kernel(x_ref, u_ref, *refs):
    blocks, out_ref = refs[:-1], refs[-1]
    groups, rows, positions = out_ref.shape
    rows -= EXTRA
    u = u_ref[...]
    wide = u.astype(jnp.float32)
    square = jnp.sum(wide * wide, axis=0, keepdims=True)
    upper = square.astype(jnp.bfloat16).astype(jnp.float32)
    at = lax.broadcasted_iota(jnp.int32, (EXTRA, positions), 0)
    extra = jnp.where(at == 0, upper, jnp.where(at == 1, square - upper, 0.0)).astype(out_ref.dtype)
    for step, block in enumerate(blocks):
        x = lax.rem(x_ref[0] + groups - step, groups)
        term = jnp.dot(block[:rows], u, preferred_element_type=jnp.float32)
        out_ref[x, :rows] = term.astype(out_ref.dtype)
        out_ref[x, rows:] = extra


def mix_kernel(past, stored, features, length_ref, terms_ref, fwd_ref, inv_ref, filt_ref, skip_ref, *rest):
    lagged, (mixed_ref, spec_ref) = rest[:-2], rest[-2:]
    copies, width, positions = mixed_ref.shape
    period = fwd_ref.shape[1] // 2
    terms = jnp.sum(terms_ref[...].astype(jnp.float32), axis=0)
    square = terms[3 * width : 3 * width + 1] + terms[3 * width + 1 : 3 * width + 2]
    gates = terms[: 3 * width] * lax.rsqrt(square * (1.0 / features) + 1e-06)
    live = lax.broadcasted_iota(jnp.int32, (1, positions), 1) < length_ref[0]
    driven = jnp.where(live, gates[width : 2 * width] * gates[:width], 0.0)
    spectrum = jnp.dot(driven.astype(jnp.bfloat16), fwd_ref[...], preferred_element_type=jnp.float32)
    real, imag = spectrum[:, :period], spectrum[:, period:]
    spec_ref[0] = real
    spec_ref[1] = imag
    zreal = filt_ref[0, 0] * real - filt_ref[0, 1] * imag
    zimag = filt_ref[0, 0] * imag + filt_ref[0, 1] * real
    for lag in range(1, past + 1):
        ref = lagged[lag - 1]
        zreal += filt_ref[lag, 0] * ref[0] - filt_ref[lag, 1] * ref[1]
        zimag += filt_ref[lag, 0] * ref[1] + filt_ref[lag, 1] * ref[0]
    if stored is not None:
        zreal += lagged[-1][stored, 0]
        zimag += lagged[-1][stored, 1]
    packed = jnp.concatenate([zreal, zimag], axis=1).astype(jnp.bfloat16)
    conv = jnp.dot(packed, inv_ref[...], preferred_element_type=jnp.float32)
    mixed = (gates[2 * width :] * (conv + skip_ref[...] * driven)).astype(mixed_ref.dtype)
    for y in range(copies):
        mixed_ref[y] = mixed


def emit_terms_kernel(x_ref, mixed_ref, *refs):
    blocks, out_ref = refs[:-1], refs[-1]
    groups, rows, _ = out_ref.shape
    mixed = mixed_ref[...]
    for step, block in enumerate(blocks):
        x = lax.rem(x_ref[0] + groups - step, groups)
        w = block[block.shape[0] - rows :]
        out_ref[x] = jnp.dot(w, mixed, preferred_element_type=jnp.float32).astype(out_ref.dtype)


def total_of(terms_ref, own_ref):
    total = own_ref[...].astype(jnp.float32) + jnp.sum(terms_ref[...].astype(jnp.float32), axis=0)
    return total.astype(own_ref.dtype)


def add_and_send_kernel(last_ref, terms_ref, own_ref, fresh_ref, out_ref, send_ref):
    out = total_of(terms_ref, own_ref)
    out_ref[...] = out
    send_ref[...] = jnp.where(last_ref[0] == 1, fresh_ref[...], out)


def finish_kernel(terms_ref, own_ref, *refs):
    earlier, out_ref = refs[:-1], refs[-1]
    for tick, ref in enumerate(earlier):
        out_ref[tick] = ref[...]
    out_ref[len(earlier)] = total_of(terms_ref, own_ref)


def local(feeds, newcomers, occupied, gain, value_w, in_w, out_w, emit_w, skip, filters, archive):
    section = lax.axis_index(SECTION)
    layers = lax.axis_size(SECTION)
    groups, copies = lax.axis_size("x"), lax.axis_size("y")
    ticks = newcomers.shape[0] + 1
    blocks = archive.shape[1]
    positions, width = feeds.shape[1:]
    features = gain.shape[1]
    rows = features // groups
    bf16 = functools.partial(jax.ShapeDtypeStruct, dtype=jnp.bfloat16)
    f32 = functools.partial(jax.ShapeDtypeStruct, dtype=jnp.float32)
    x = lax.axis_index("x").astype(jnp.int32)[None]
    last = (section == layers - 1).astype(jnp.int32)[None]
    lengths = [lax.dynamic_slice_in_dim(occupied, tick - section + layers - 1, 1, 0) for tick in range(ticks)]

    own = feeds[0].T
    part = gather_rows(jnp.broadcast_to(own[None], (copies,) + own.shape))
    dealt = call(
        deal_kernel,
        [bf16((4 * width, rows))] * groups,
        [x, gain] + [w[0].T for w in (value_w, in_w, out_w, emit_w)],
        "deal",
        smem=1,
    )
    weights = [dealt[0]] + [
        lax.ppermute(dealt[step], "x", [(i, (i + step) % groups) for i in range(groups)]) for step in range(1, groups)
    ]
    known, filters, forward, inverse = call(
        history_kernel,
        [f32((blocks,) + filters.shape[2:]), f32(filters.shape[1:])] + [bf16(t.shape) for t in tables(positions, filters.shape[-1])],
        [filters[0], archive[0]] + [jnp.asarray(t) for t in tables(positions, filters.shape[-1])],
        "history",
    )
    skip_column = skip[0][:, None]
    fresh = newcomers.transpose(0, 2, 1)

    ring = [(i, (i + 1) % layers) for i in range(layers)]
    outputs, spectra = [], []
    for tick in range(ticks):
        terms = call(
            gate_terms_kernel,
            bf16((groups, 3 * width + EXTRA, positions)),
            [x, part] + weights,
            "gate_terms",
            smem=1,
        )
        terms = swap(terms, "x")
        past = min(tick, blocks)
        stored = tick if tick < blocks else None
        lagged = spectra[::-1][:past] + ([known] if stored is not None else [])
        mixed, spectrum = call(
            functools.partial(mix_kernel, past, stored, features),
            [bf16((copies, width, positions)), f32((2, width, filters.shape[-1]))],
            [lengths[tick], terms, forward, inverse, filters, skip_column] + lagged,
            "mix",
            smem=1,
        )
        spectra.append(spectrum)
        terms = call(
            emit_terms_kernel,
            bf16((groups, width, positions)),
            [x, gather_rows(mixed)] + weights,
            "emit_terms",
            smem=1,
        )
        terms = swap(terms, "x")
        if tick < ticks - 1:
            out, send = call(
                add_and_send_kernel, [bf16(own.shape)] * 2, [last, terms, own, fresh[tick]], "add", smem=1
            )
            outputs.append(out)
            own = lax.ppermute(send, SECTION, ring)
            part = gather_rows(jnp.broadcast_to(own[None], (copies,) + own.shape))
    layer_out = call(finish_kernel, bf16((ticks,) + own.shape), [terms, own] + outputs, "finish")
    return layer_out.transpose(0, 2, 1)[None]


def solution(mesh):
    grid = Mesh(mesh.devices.reshape(8, 2, 4, 8), ("z", "core", "x", "y"))
    chan = ("x", "y")
    return jax.shard_map(
        local,
        mesh=grid,
        in_specs=(
            P(SECTION, None, chan),
            P(None, None, chan),
            P(),
            P(SECTION, None),
            P(SECTION, None, chan),
            P(SECTION, None, chan),
            P(SECTION, None, chan),
            P(SECTION, None, chan),
            P(SECTION, chan),
            P(SECTION, None, None, chan, None),
            P(SECTION, None, None, chan, None),
        ),
        out_specs=P(SECTION, None, None, chan),
        check_vma=False,
    )
```

time: 250 us -> 242 us (0.968)
  waiting for transfers between devices: 41.6 us -> 23.2 us
  starting transfers between devices: 19.6 us -> 27.9 us
  blocking collectives: 160 us -> 164 us
    all_to_all x4 -> x3, waiting for transfers between devices: 31.6 us -> 5.62 us  [swap(): return lax.all_to_all(blocks, axis, 0, 0, tiled=True)]
    ppermute x0 -> x3, starting transfers between devices: none -> 11.4 us  [local(): lax.ppermute(dealt[step], 'x', [(i, (i + step) % groups) for i in range(g...]
    ppermute x0 -> x3, waiting for transfers between devices: none -> 7.57 us  [local(): lax.ppermute(dealt[step], 'x', [(i, (i + step) % groups) for i in range(g...]
    all_to_all x13, blocking collectives: 160 us -> 164 us  [swap(): return lax.all_to_all(blocks, axis, 0, 0, tiled=True)]
    all_to_all x4 -> x3, starting transfers between devices: 19.6 us -> 16.4 us  [swap(): return lax.all_to_all(blocks, axis, 0, 0, tiled=True)]
    unnamed x46 -> x34, local copies, waits for them, and re-layouts: 8.71 us -> 10.1 us
    pallas_call x16 -> x18, Pallas kernels: 11.3 us -> 11.7 us  [call(): pl.pallas_call(body, out_shape=out, in_specs=[scalars] * smem + [vmem] *...]
  transfers between devices with their start and end apart: 7 -> 9, of which waited for: 7 -> 7; matrix products, arithmetic and copies ran while one was open for 3% -> 1% of each run, Pallas kernels for 0% -> 0%
where the time goes in v3:
time: 242 us; the launch traced here: 240 us
  blocking collectives  164 us (68%)
  starting transfers between devices  27.9 us (12%)
  waiting for transfers between devices  23.2 us (10%)
  local copies, waits for them, and re-layouts  13.8 us (6%)
  Pallas kernels  11.7 us (5%)
    all_to_all x13, blocking collectives, swap(): return lax.all_to_all(blocks, axis, 0, 0, tiled=True)  164 us
    all_to_all x3, starting transfers between devices, swap(): return lax.all_to_all(blocks, axis, 0, 0, tiled=True)  16.4 us
    pallas_call x18, Pallas kernels, call(): pl.pallas_call(body, out_shape=out, in_specs=[scalars] * smem + [vmem] *...  11.7 us
    ppermute x3, starting transfers between devices, local(): lax.ppermute(dealt[step], 'x', [(i, (i + step) % groups) for i in range(g...  11.4 us
    unnamed x34, local copies, waits for them, and re-layouts  10.1 us
    ppermute x3, waiting for transfers between devices, local(): own = lax.ppermute(send, SECTION, ring)  9.98 us
    ppermute x3, waiting for transfers between devices, local(): lax.ppermute(dealt[step], 'x', [(i, (i + step) % groups) for i in range(g...  7.57 us
    all_to_all x3, waiting for transfers between devices, swap(): return lax.all_to_all(blocks, axis, 0, 0, tiled=True)  5.62 us
  transfers between devices with their start and end apart: 9, of which 7 were waited for; matrix products, arithmetic and copies ran while one was open for 1% of the time, Pallas kernels for 0%

profile of v3, /device:TPU:64, one launch (start us, length us, event | category | flops | bytes accessed | tf_op | source)
XLA Modules:
  0.0 240.4 jit_solution(9553856858636558736)
XLA Ops:
  1.5 7.2 %all-to-all-start = ((bf16[8,64,256]{2,1,0:T(8,128)(2,1)}), bf16[8,64,256]{2,1,0:T(8,128)(2,1)S(1)}, u32[]{:S(2)}, u32[]{:S(2)}) async-start(bf16[8,64,256]{2,1,0:T(8,128)(2,1)} %broadcast_in_dim.38), calls=%async_computation | async-start | bytes 524288 | tf_op jit(solution)/shard_map/all_to_all | solution.py:37
  10.5 3.4 %collective-permute-start = (bf16[256,512]{1,0:T(8,128)(2,1)S(1)}, bf16[256,512]{1,0:T(8,128)(2,1)S(1)}, u32[]{:S(2)}, u32[]{:S(2)}) collective-permute-start(bf16[256,512]{1,0:T(8,128)(2,1)S(1)} %get-tuple-element.27), channel_id=1, source_target_pairs={{0,8},{8,16},{16,24},{24,0},{1,9},{9,17},{17,25},{25,1},{2,10},{10... | collective-permute-start | bytes 786440 | tf_op jit(solution)/shard_map/ppermute | solution.py:175
  13.9 4.6 %collective-permute-start.1 = (bf16[256,512]{1,0:T(8,128)(2,1)S(1)}, bf16[256,512]{1,0:T(8,128)(2,1)S(1)}, u32[]{:S(2)}, u32[]{:S(2)}) collective-permute-start(bf16[256,512]{1,0:T(8,128)(2,1)S(1)} %get-tuple-element.28), channel_id=1, source_target_pairs={{0,16},{8,24},{16,0},{24,8},{1,17},{9,25},{17,1},{25,9},{2,18},{10... | collective-permute-start | bytes 786440 | tf_op jit(solution)/shard_map/ppermute | solution.py:175
  18.6 3.3 %collective-permute-start.2 = (bf16[256,512]{1,0:T(8,128)(2,1)S(1)}, bf16[256,512]{1,0:T(8,128)(2,1)S(1)}, u32[]{:S(2)}, u32[]{:S(2)}) collective-permute-start(bf16[256,512]{1,0:T(8,128)(2,1)S(1)} %get-tuple-element.29), channel_id=1, source_target_pairs={{0,24},{8,0},{16,8},{24,16},{1,25},{9,1},{17,9},{25,17},{2,26},{10... | collective-permute-start | bytes 786440 | tf_op jit(solution)/shard_map/ppermute | solution.py:175
  22.0 6.1 %collective-permute-done.1.refs_2_ = bf16[256,512]{1,0:T(8,128)(2,1)S(1)} collective-permute-done((bf16[256,512]{1,0:T(8,128)(2,1)S(1)}, bf16[256,512]{1,0:T(8,128)(2,1)S(1)}, u32[]{:S(2)}, u32[]{:S(2)}) %collective-permute-start.1) | collective-permute-done | bytes 262176 | tf_op jit(solution)/shard_map/ppermute | solution.py:175
  30.7 4.3 %all-to-all-start.1 = ((bf16[4,208,256]{2,1,0:T(8,128)(2,1)}), bf16[4,208,256]{2,1,0:T(8,128)(2,1)}, u32[]{:S(2)}, u32[]{:S(2)}) async-start(bf16[4,208,256]{2,1,0:T(8,128)(2,1)} %gate_terms.4), calls=%async_computation.1 | async-start | bytes 851968 | tf_op jit(solution)/shard_map/all_to_all | solution.py:37
  46.3 17.2 %all_to_all.80 = bf16[8,64,256]{2,1,0:T(8,128)(2,1)S(1)} all-to-all(bf16[8,64,256]{2,1,0:T(8,128)(2,1)S(1)} %get-tuple-element.34), channel_id=1, replica_groups=mesh['z'=8,'core'=2,'x'=4,'y'=8] {'y'}, dimensions={0} | all-to-all | bytes 524288 | tf_op jit(solution)/shard_map/all_to_all | solution.py:37
  64.5 4.8 %all-to-all-start.3 = ((bf16[4,64,256]{2,1,0:T(8,128)(2,1)}), bf16[4,64,256]{2,1,0:T(8,128)(2,1)}, u32[]{:S(2)}, u32[]{:S(2)}) async-start(bf16[4,64,256]{2,1,0:T(8,128)(2,1)} %copy-done.7), calls=%async_computation.3 | async-start | bytes 262144 | tf_op jit(solution)/shard_map/all_to_all | solution.py:37
  70.8 4.7 %all-to-all-done.3.terms_ref = bf16[4,64,256]{2,1,0:T(8,128)(2,1)} async-done(((bf16[4,64,256]{2,1,0:T(8,128)(2,1)}), bf16[4,64,256]{2,1,0:T(8,128)(2,1)}, u32[]{:S(2)}, u32[]{:S(2)}) %all-to-all-start.3) | async-done | bytes 131104 | tf_op jit(solution)/shard_map/all_to_all | solution.py:37
  77.2 3.3 %collective-permute-done.3.own_ref = bf16[64,256]{1,0:T(8,128)(2,1)S(1)} collective-permute-done((bf16[64,256]{1,0:T(8,128)(2,1)S(1)}, bf16[64,256]{1,0:T(8,128)(2,1)S(1)}, u32[]{:S(2)}, u32[]{:S(2)}) %collective-permute-start.3) | collective-permute-done | bytes 32800 | tf_op jit(solution)/shard_map/ppermute | solution.py:221
  80.5 14.9 %all_to_all.81 = bf16[8,64,256]{2,1,0:T(8,128)(2,1)S(1)} all-to-all(bf16[8,64,256]{2,1,0:T(8,128)(2,1)S(1)} %broadcast_in_dim.39), channel_id=1, replica_groups=mesh['z'=8,'core'=2,'x'=4,'y'=8] {'y'}, dimensions={0} | all-to-all | bytes 524288 | tf_op jit(solution)/shard_map/all_to_all | solution.py:37
  95.8 11.4 %all_to_all.82.terms_ref = bf16[4,208,256]{2,1,0:T(8,128)(2,1)S(1)} all-to-all(bf16[4,208,256]{2,1,0:T(8,128)(2,1)S(1)} %gate_terms.5), channel_id=1, replica_groups=mesh['z'=8,'core'=2,'x'=4,'y'=8] {'x'}, dimensions={0} | all-to-all | bytes 851968 | tf_op jit(solution)/shard_map/all_to_all | solution.py:37
  108.3 13.9 %all_to_all.83 = bf16[8,64,256]{2,1,0:T(8,128)(2,1)S(1)} all-to-all(bf16[8,64,256]{2,1,0:T(8,128)(2,1)S(1)} %get-tuple-element.37), channel_id=1, replica_groups=mesh['z'=8,'core'=2,'x'=4,'y'=8] {'y'}, dimensions={0} | all-to-all | bytes 524288 | tf_op jit(solution)/shard_map/all_to_all | solution.py:37
  122.5 8.4 %all_to_all.84.terms_ref = bf16[4,64,256]{2,1,0:T(8,128)(2,1)S(1)} all-to-all(bf16[4,64,256]{2,1,0:T(8,128)(2,1)S(1)} %emit_terms.5), channel_id=1, replica_groups=mesh['z'=8,'core'=2,'x'=4,'y'=8] {'x'}, dimensions={0} | all-to-all | bytes 262144 | tf_op jit(solution)/shard_map/all_to_all | solution.py:37
  130.9 3.3 %collective-permute-done.4.own_ref = bf16[64,256]{1,0:T(8,128)(2,1)S(1)} collective-permute-done((bf16[64,256]{1,0:T(8,128)(2,1)S(1)}, bf16[64,256]{1,0:T(8,128)(2,1)S(1)}, u32[]{:S(2)}, u32[]{:S(2)}) %collective-permute-start.4) | collective-permute-done | bytes 32800 | tf_op jit(solution)/shard_map/ppermute | solution.py:221
  134.3 14.9 %all_to_all.85 = bf16[8,64,256]{2,1,0:T(8,128)(2,1)S(1)} all-to-all(bf16[8,64,256]{2,1,0:T(8,128)(2,1)S(1)} %broadcast_in_dim.40), channel_id=1, replica_groups=mesh['z'=8,'core'=2,'x'=4,'y'=8] {'y'}, dimensions={0} | all-to-all | bytes 524288 | tf_op jit(solution)/shard_map/all_to_all | solution.py:37
  149.6 11.3 %all_to_all.86.terms_ref = bf16[4,208,256]{2,1,0:T(8,128)(2,1)S(1)} all-to-all(bf16[4,208,256]{2,1,0:T(8,128)(2,1)S(1)} %gate_terms.6), channel_id=1, replica_groups=mesh['z'=8,'core'=2,'x'=4,'y'=8] {'x'}, dimensions={0} | all-to-all | bytes 851968 | tf_op jit(solution)/shard_map/all_to_all | solution.py:37
  162.0 13.9 %all_to_all.87 = bf16[8,64,256]{2,1,0:T(8,128)(2,1)S(1)} all-to-all(bf16[8,64,256]{2,1,0:T(8,128)(2,1)S(1)} %get-tuple-element.40), channel_id=1, replica_groups=mesh['z'=8,'core'=2,'x'=4,'y'=8] {'y'}, dimensions={0} | all-to-all | bytes 524288 | tf_op jit(solution)/shard_map/all_to_all | solution.py:37
  176.3 8.4 %all_to_all.88.terms_ref = bf16[4,64,256]{2,1,0:T(8,128)(2,1)S(1)} all-to-all(bf16[4,64,256]{2,1,0:T(8,128)(2,1)S(1)} %emit_terms.6), channel_id=1, replica_groups=mesh['z'=8,'core'=2,'x'=4,'y'=8] {'x'}, dimensions={0} | all-to-all | bytes 262144 | tf_op jit(solution)/shard_map/all_to_all | solution.py:37
  184.7 3.3 %collective-permute-done.5.own_ref = bf16[64,256]{1,0:T(8,128)(2,1)S(1)} collective-permute-done((bf16[64,256]{1,0:T(8,128)(2,1)S(1)}, bf16[64,256]{1,0:T(8,128)(2,1)S(1)}, u32[]{:S(2)}, u32[]{:S(2)}) %collective-permute-start.5) | collective-permute-done | bytes 32800 | tf_op jit(solution)/shard_map/ppermute | solution.py:221
  188.0 15.7 %all_to_all.89 = bf16[8,64,256]{2,1,0:T(8,128)(2,1)S(1)} all-to-all(bf16[8,64,256]{2,1,0:T(8,128)(2,1)S(1)} %broadcast_in_dim.41), channel_id=1, replica_groups=mesh['z'=8,'core'=2,'x'=4,'y'=8] {'y'}, dimensions={0} | all-to-all | bytes 524288 | tf_op jit(solution)/shard_map/all_to_all | solution.py:37
  204.1 11.4 %all_to_all.90.terms_ref = bf16[4,208,256]{2,1,0:T(8,128)(2,1)S(1)} all-to-all(bf16[4,208,256]{2,1,0:T(8,128)(2,1)S(1)} %gate_terms.7), channel_id=1, replica_groups=mesh['z'=8,'core'=2,'x'=4,'y'=8] {'x'}, dimensions={0} | all-to-all | bytes 851968 | tf_op jit(solution)/shard_map/all_to_all | solution.py:37
  217.1 13.9 %all_to_all.91 = bf16[8,64,256]{2,1,0:T(8,128)(2,1)S(1)} all-to-all(bf16[8,64,256]{2,1,0:T(8,128)(2,1)S(1)} %get-tuple-element.43), channel_id=1, replica_groups=mesh['z'=8,'core'=2,'x'=4,'y'=8] {'y'}, dimensions={0} | all-to-all | bytes 524288 | tf_op jit(solution)/shard_map/all_to_all | solution.py:37
  231.3 8.4 %all_to_all.92.terms_ref = bf16[4,64,256]{2,1,0:T(8,128)(2,1)S(1)} all-to-all(bf16[4,64,256]{2,1,0:T(8,128)(2,1)S(1)} %emit_terms.7), channel_id=1, replica_groups=mesh['z'=8,'core'=2,'x'=4,'y'=8] {'x'}, dimensions={0} | all-to-all | bytes 262144 | tf_op jit(solution)/shard_map/all_to_all | solution.py:37
  (66 shorter events, 28.1 us)
Async XLA Ops:
  0.0 8.8 %copy-start.10 = (bf16[1,2048,64]{1,2,0:T(8,128)(2,1)S(1)}, bf16[1,2048,64]{1,2,0:T(8,128)(2,1)}, u32[]{:S(2)}) copy-start(bf16[1,2048,64]{1,2,0:T(8,128)(2,1)} %param.19) | copy-start | bytes 786436
  1.5 7.3 %copy-start.8 = (bf16[1,2048,64]{1,2,0:T(8,128)(2,1)S(1)}, bf16[1,2048,64]{1,2,0:T(8,128)(2,1)}, u32[]{:S(2)}) copy-start(bf16[1,2048,64]{1,2,0:T(8,128)(2,1)} %param.17) | copy-start | bytes 786436
  1.5 7.3 %copy-start.9 = (bf16[1,2048,64]{1,2,0:T(8,128)(2,1)S(1)}, bf16[1,2048,64]{1,2,0:T(8,128)(2,1)}, u32[]{:S(2)}) copy-start(bf16[1,2048,64]{1,2,0:T(8,128)(2,1)} %param.18) | copy-start | bytes 786436
  1.5 28.0 %all-to-all-start = ((bf16[8,64,256]{2,1,0:T(8,128)(2,1)}), bf16[8,64,256]{2,1,0:T(8,128)(2,1)S(1)}, u32[]{:S(2)}, u32[]{:S(2)}) async-start(bf16[8,64,256]{2,1,0:T(8,128)(2,1)} %broadcast_in_dim.38), calls=%async_computation | async-start | bytes 524288 | tf_op jit(solution)/shard_map/all_to_all | solution.py:37
  8.8 0.7 copy-start.14
  9.5 0.9 copy-start.11
  10.5 11.4 %collective-permute-start = (bf16[256,512]{1,0:T(8,128)(2,1)S(1)}, bf16[256,512]{1,0:T(8,128)(2,1)S(1)}, u32[]{:S(2)}, u32[]{:S(2)}) collective-permute-start(bf16[256,512]{1,0:T(8,128)(2,1)S(1)} %get-tuple-element.27), channel_id=1, source_target_pairs={{0,8},{8,16},{16,24},{24,0},{1,9},{9,17},{17,25},{25,1},{2,10},{10... | collective-permute-start | bytes 786440 | tf_op jit(solution)/shard_map/ppermute | solution.py:175
  13.9 14.1 %collective-permute-start.1 = (bf16[256,512]{1,0:T(8,128)(2,1)S(1)}, bf16[256,512]{1,0:T(8,128)(2,1)S(1)}, u32[]{:S(2)}, u32[]{:S(2)}) collective-permute-start(bf16[256,512]{1,0:T(8,128)(2,1)S(1)} %get-tuple-element.28), channel_id=1, source_target_pairs={{0,16},{8,24},{16,0},{24,8},{1,17},{9,25},{17,1},{25,9},{2,18},{10... | collective-permute-start | bytes 786440 | tf_op jit(solution)/shard_map/ppermute | solution.py:175
  18.6 10.9 %collective-permute-start.2 = (bf16[256,512]{1,0:T(8,128)(2,1)S(1)}, bf16[256,512]{1,0:T(8,128)(2,1)S(1)}, u32[]{:S(2)}, u32[]{:S(2)}) collective-permute-start(bf16[256,512]{1,0:T(8,128)(2,1)S(1)} %get-tuple-element.29), channel_id=1, source_target_pairs={{0,24},{8,0},{16,8},{24,16},{1,25},{9,1},{17,9},{25,17},{2,26},{10... | collective-permute-start | bytes 786440 | tf_op jit(solution)/shard_map/ppermute | solution.py:175
  30.7 12.4 %all-to-all-start.1 = ((bf16[4,208,256]{2,1,0:T(8,128)(2,1)}), bf16[4,208,256]{2,1,0:T(8,128)(2,1)}, u32[]{:S(2)}, u32[]{:S(2)}) async-start(bf16[4,208,256]{2,1,0:T(8,128)(2,1)} %gate_terms.4), calls=%async_computation.1 | async-start | bytes 851968 | tf_op jit(solution)/shard_map/all_to_all | solution.py:37
  35.8 1.2 copy-start.3
  37.0 1.1 copy-start.4
  38.1 1.0 copy-start.5
  39.2 1.0 copy-start.6
  40.2 1.3 copy-start.15
  40.6 0.9 copy-start
  43.1 1.1 copy-start.1
  64.5 10.9 %all-to-all-start.3 = ((bf16[4,64,256]{2,1,0:T(8,128)(2,1)}), bf16[4,64,256]{2,1,0:T(8,128)(2,1)}, u32[]{:S(2)}, u32[]{:S(2)}) async-start(bf16[4,64,256]{2,1,0:T(8,128)(2,1)} %copy-done.7), calls=%async_computation.3 | async-start | bytes 262144 | tf_op jit(solution)/shard_map/all_to_all | solution.py:37
  69.4 6.1 %copy-start.12 = (bf16[1,256,64]{1,2,0:T(8,128)(2,1)S(1)}, bf16[1,256,64]{1,2,0:T(8,128)(2,1)}, u32[]{:S(2)}) copy-start(bf16[1,256,64]{1,2,0:T(8,128)(2,1)} %param.13) | copy-start | bytes 98308
  75.4 0.8 copy-start.13
  77.1 3.4 %collective-permute-start.3 = (bf16[64,256]{1,0:T(8,128)(2,1)S(1)}, bf16[64,256]{1,0:T(8,128)(2,1)S(1)}, u32[]{:S(2)}, u32[]{:S(2)}) collective-permute-start(bf16[64,256]{1,0:T(8,128)(2,1)S(1)} %get-tuple-element.35), channel_id=1, source_target_pairs={{0,32},{32,64},{64,96},{96,128},{128,160},{160,192},{192,224},{224... | collective-permute-start | bytes 98312 | tf_op jit(solution)/shard_map/ppermute | solution.py:221
  95.8 11.4 %copy-start.2 = (f32[3,2,64,512]{3,2,1,0:T(8,128)S(1)}, f32[3,2,64,512]{3,2,1,0:T(8,128)}, u32[]{:S(2)}) copy-start(f32[3,2,64,512]{3,2,1,0:T(8,128)} %copy-done) | copy-start | bytes 2359300
  130.9 3.4 %collective-permute-start.4 = (bf16[64,256]{1,0:T(8,128)(2,1)S(1)}, bf16[64,256]{1,0:T(8,128)(2,1)S(1)}, u32[]{:S(2)}, u32[]{:S(2)}) collective-permute-start(bf16[64,256]{1,0:T(8,128)(2,1)S(1)} %get-tuple-element.38), channel_id=1, source_target_pairs={{0,32},{32,64},{64,96},{96,128},{128,160},{160,192},{192,224},{224... | collective-permute-start | bytes 98312 | tf_op jit(solution)/shard_map/ppermute | solution.py:221
  184.6 3.4 %collective-permute-start.5 = (bf16[64,256]{1,0:T(8,128)(2,1)S(1)}, bf16[64,256]{1,0:T(8,128)(2,1)S(1)}, u32[]{:S(2)}, u32[]{:S(2)}) collective-permute-start(bf16[64,256]{1,0:T(8,128)(2,1)S(1)} %get-tuple-element.41), channel_id=1, source_target_pairs={{0,32},{32,64},{64,96},{96,128},{128,160},{160,192},{192,224},{224... | collective-permute-start | bytes 98312 | tf_op jit(solution)/shard_map/ppermute | solution.py:221
  (2 other events, 1.3 us)

commit v4 on v3

--- a/solution.py
+++ b/solution.py
@@ -21,16 +21,41 @@
         out_shape=out,
         in_specs=[scalars] * smem + [vmem] * (len(operands) - smem),
         out_specs=jax.tree.map(lambda _: vmem, out),
-        compiler_params=pltpu.CompilerParams(vmem_limit_bytes=40 * 1024 * 1024),
+        compiler_params=pltpu.CompilerParams(vmem_limit_bytes=16 * 1024 * 1024),
         name=name,
     )(*operands)
 
 
 def tables(length, period):
-    phase = np.arange(length)[:, None] * np.arange(period)[None, :] % period
-    angle = phase * (2.0 * np.pi / period)
-    forward = np.concatenate([np.cos(angle), -np.sin(angle)], axis=1)
-    return forward.astype(jnp.bfloat16), (forward.T / period).astype(jnp.bfloat16)
+    half = period // 2
+    phase = np.arange(length)[:, None] * np.arange(half)[None, :] % period
+    cos, sin = np.cos(phase * (2.0 * np.pi / period)), -np.sin(phase * (2.0 * np.pi / period))
+    sin[:, 0] = 1 - 2 * (np.arange(length) % 2)
+    forward = np.concatenate([cos, sin], axis=1)
+    weight = np.full((2 * half, 1), 2.0 / period)
+    weight[0] = weight[half] = 1.0 / period
+    return forward.astype(jnp.bfloat16), (forward.T * weight).astype(jnp.bfloat16)
+
+
+def fold(full):
+    half = full.shape[-1] // 2
+    lower, upper = full[..., :half], full[..., half:]
+    at = [lax.broadcasted_iota(jnp.int32, (half, half), axis) for axis in (0, 1)]
+    mirror = jnp.where(at[0] + at[1] == half, 1.0, 0.0)
+    mirrored = jnp.dot(
+        upper.reshape(-1, half), mirror, precision=lax.Precision.HIGHEST, preferred_element_type=jnp.float32
+    ).reshape(upper.shape)
+    first = lax.broadcasted_iota(jnp.int32, lower.shape[1:], 1) == 0
+    real = jnp.where(first, lower[0], 0.5 * (lower[0] + mirrored[0]))
+    imag = jnp.where(first, upper[0], 0.5 * (lower[1] - mirrored[1]))
+    return real, imag
+
+
+def times(filt, spectrum):
+    first = lax.broadcasted_iota(jnp.int32, filt[0].shape, 1) == 0
+    imag = jnp.where(first, 0.0, filt[1])
+    other = jnp.where(first, filt[1], filt[0])
+    return filt[0] * spectrum[0] - imag * spectrum[1], other * spectrum[1] + imag * spectrum[0]
 
 
 def swap(blocks, axis):
@@ -58,24 +83,36 @@
             block[m * width : (m + 1) * width] = w
 
 
-def history_kernel(filt_ref, held_ref, fwd_ref, inv_ref, known_ref, filt_out, fwd_out, inv_out):
+def history_kernel(section_ref, lengths_ref, skip_ref, filt_ref, held_ref, *rest):
+    passed, (live_ref, known_ref, filt_out, *handed) = rest[: (len(rest) - 3) // 2], rest[(len(rest) - 3) // 2 :]
+    ticks, _, positions = live_ref.shape
+    layers = lengths_ref.shape[0] - ticks + 1
+    at = lax.broadcasted_iota(jnp.int32, (1, positions), 1)
+    for tick in range(ticks):
+        length = lengths_ref[tick - section_ref[0] + layers - 1]
+        live_ref[tick] = jnp.where(at < length, 1.0, 0.0)
     blocks = held_ref.shape[0]
     for tick in range(blocks):
         real = imag = 0.0
         for lag in range(tick + 1, blocks + 1):
-            held = held_ref.at[lag - tick - 1]
-            real += filt_ref[lag, 0] * held[0] - filt_ref[lag, 1] * held[1]
-            imag += filt_ref[lag, 0] * held[1] + filt_ref[lag, 1] * held[0]
-        known_ref[tick, 0] = real
-        known_ref[tick, 1] = imag
-    filt_out[...] = filt_ref[...]
-    fwd_out[...] = fwd_ref[...]
-    inv_out[...] = inv_ref[...]
+            first, second = held_ref[lag - tick - 1, 0], held_ref[lag - tick - 1, 1]
+            real += filt_ref[lag, 0] * first - filt_ref[lag, 1] * second
+            imag += filt_ref[lag, 0] * second + filt_ref[lag, 1] * first
+        known_ref[tick, 0], known_ref[tick, 1] = fold(jnp.stack([real, imag]))
+    for lag in range(blocks + 1):
+        real, imag = fold(filt_ref[lag])
+        if lag == 0:
+            real += skip_ref[...]
+            imag += jnp.where(lax.broadcasted_iota(jnp.int32, imag.shape, 1) == 0, skip_ref[...], 0.0)
+        filt_out[lag, 0], filt_out[lag, 1] = real, imag
+    for source, target in zip(passed, handed, strict=True):
+        target[...] = source[...]
 
 
 def gate_terms_kernel(x_ref, u_ref, *refs):
-    blocks, out_ref = refs[:-1], refs[-1]
+    out_ref = refs[-1]
     groups, rows, positions = out_ref.shape
+    blocks = refs[:groups]
     rows -= EXTRA
     u = u_ref[...]
     wide = u.astype(jnp.float32)
@@ -90,31 +127,26 @@
         out_ref[x, rows:] = extra
 
 
-def mix_kernel(past, stored, features, length_ref, terms_ref, fwd_ref, inv_ref, filt_ref, skip_ref, *rest):
+def mix_kernel(tick, past, stored, features, live_ref, terms_ref, fwd_ref, inv_ref, filt_ref, *rest):
     lagged, (mixed_ref, spec_ref) = rest[:-2], rest[-2:]
-    copies, width, positions = mixed_ref.shape
-    period = fwd_ref.shape[1] // 2
+    copies, width, _ = mixed_ref.shape
+    half = fwd_ref.shape[1] // 2
     terms = jnp.sum(terms_ref[...].astype(jnp.float32), axis=0)
     square = terms[3 * width : 3 * width + 1] + terms[3 * width + 1 : 3 * width + 2]
     gates = terms[: 3 * width] * lax.rsqrt(square * (1.0 / features) + 1e-06)
-    live = lax.broadcasted_iota(jnp.int32, (1, positions), 1) < length_ref[0]
-    driven = jnp.where(live, gates[width : 2 * width] * gates[:width], 0.0)
+    driven = jnp.where(live_ref[tick] > 0.0, gates[width : 2 * width] * gates[:width], 0.0)
     spectrum = jnp.dot(driven.astype(jnp.bfloat16), fwd_ref[...], preferred_element_type=jnp.float32)
-    real, imag = spectrum[:, :period], spectrum[:, period:]
-    spec_ref[0] = real
-    spec_ref[1] = imag
-    zreal = filt_ref[0, 0] * real - filt_ref[0, 1] * imag
-    zimag = filt_ref[0, 0] * imag + filt_ref[0, 1] * real
+    spectrum = spectrum[:, :half], spectrum[:, half:]
+    spec_ref[0], spec_ref[1] = spectrum
+    real, imag = times(filt_ref[0], spectrum)
     for lag in range(1, past + 1):
-        ref = lagged[lag - 1]
-        zreal += filt_ref[lag, 0] * ref[0] - filt_ref[lag, 1] * ref[1]
-        zimag += filt_ref[lag, 0] * ref[1] + filt_ref[lag, 1] * ref[0]
+        more = times(filt_ref[lag], lagged[lag - 1][...])
+        real, imag = real + more[0], imag + more[1]
     if stored is not None:
-        zreal += lagged[-1][stored, 0]
-        zimag += lagged[-1][stored, 1]
-    packed = jnp.concatenate([zreal, zimag], axis=1).astype(jnp.bfloat16)
+        real, imag = real + lagged[-1][stored, 0], imag + lagged[-1][stored, 1]
+    packed = jnp.concatenate([real, imag], axis=1).astype(jnp.bfloat16)
     conv = jnp.dot(packed, inv_ref[...], preferred_element_type=jnp.float32)
-    mixed = (gates[2 * width :] * (conv + skip_ref[...] * driven)).astype(mixed_ref.dtype)
+    mixed = (gates[2 * width :] * conv).astype(mixed_ref.dtype)
     for y in range(copies):
         mixed_ref[y] = mixed
 
@@ -134,10 +166,10 @@
     return total.astype(own_ref.dtype)
 
 
-def add_and_send_kernel(last_ref, terms_ref, own_ref, fresh_ref, out_ref, send_ref):
+def add_and_send_kernel(tick, last_ref, terms_ref, own_ref, fresh_ref, out_ref, send_ref):
     out = total_of(terms_ref, own_ref)
     out_ref[...] = out
-    send_ref[...] = jnp.where(last_ref[0] == 1, fresh_ref[...], out)
+    send_ref[...] = jnp.where(last_ref[0] == 1, fresh_ref[tick], out)
 
 
 def finish_kernel(terms_ref, own_ref, *refs):
@@ -160,7 +192,6 @@
     f32 = functools.partial(jax.ShapeDtypeStruct, dtype=jnp.float32)
     x = lax.axis_index("x").astype(jnp.int32)[None]
     last = (section == layers - 1).astype(jnp.int32)[None]
-    lengths = [lax.dynamic_slice_in_dim(occupied, tick - section + layers - 1, 1, 0) for tick in range(ticks)]
 
     own = feeds[0].T
     part = gather_rows(jnp.broadcast_to(own[None], (copies,) + own.shape))
@@ -171,17 +202,20 @@
         "deal",
         smem=1,
     )
-    weights = [dealt[0]] + [
-        lax.ppermute(dealt[step], "x", [(i, (i + step) % groups) for i in range(groups)]) for step in range(1, groups)
-    ]
-    known, filters, forward, inverse = call(
+    weights = [dealt[0]] + [None] * (groups - 1)
+    for step in sorted(range(1, groups), key=lambda step: -min(step, groups - step)):
+        pairs = [(i, (i + step) % groups) for i in range(groups)]
+        weights[step] = lax.ppermute(dealt[step], "x", pairs)
+    half = filters.shape[-1] // 2
+    passed = [jnp.asarray(t) for t in tables(positions, 2 * half)] + [newcomers.transpose(0, 2, 1), own]
+    live, known, filters, forward, inverse, fresh, own = call(
         history_kernel,
-        [f32((blocks,) + filters.shape[2:]), f32(filters.shape[1:])] + [bf16(t.shape) for t in tables(positions, filters.shape[-1])],
-        [filters[0], archive[0]] + [jnp.asarray(t) for t in tables(positions, filters.shape[-1])],
+        [f32((ticks, 1, positions)), f32((blocks, 2, width, half)), f32((blocks + 1, 2, width, half))]
+        + [jax.ShapeDtypeStruct(t.shape, t.dtype) for t in passed],
+        [section.astype(jnp.int32)[None], occupied, skip[0][:, None], filters[0], archive[0]] + passed,
         "history",
+        smem=2,
     )
-    skip_column = skip[0][:, None]
-    fresh = newcomers.transpose(0, 2, 1)
 
     ring = [(i, (i + 1) % layers) for i in range(layers)]
     outputs, spectra = [], []
@@ -189,7 +223,7 @@
         terms = call(
             gate_terms_kernel,
             bf16((groups, 3 * width + EXTRA, positions)),
-            [x, part] + weights,
+            [x, part] + weights + ([live] if tick == 0 else []),
             "gate_terms",
             smem=1,
         )
@@ -198,11 +232,10 @@
         stored = tick if tick < blocks else None
         lagged = spectra[::-1][:past] + ([known] if stored is not None else [])
         mixed, spectrum = call(
-            functools.partial(mix_kernel, past, stored, features),
-            [bf16((copies, width, positions)), f32((2, width, filters.shape[-1]))],
-            [lengths[tick], terms, forward, inverse, filters, skip_column] + lagged,
+            functools.partial(mix_kernel, tick, past, stored, features),
+            [bf16((copies, width, positions)), f32((2, width, half))],
+            [live, terms, forward, inverse, filters] + lagged,
             "mix",
-            smem=1,
         )
         spectra.append(spectrum)
         terms = call(
@@ -215,7 +248,11 @@
         terms = swap(terms, "x")
         if tick < ticks - 1:
             out, send = call(
-                add_and_send_kernel, [bf16(own.shape)] * 2, [last, terms, own, fresh[tick]], "add", smem=1
+                functools.partial(add_and_send_kernel, tick),
+                [bf16(own.shape)] * 2,
+                [last, terms, own, fresh],
+                "add",
+                smem=1,
             )
             outputs.append(out)
             own = lax.ppermute(send, SECTION, ring)

time: 242 us -> 233 us (0.963)
  blocking collectives: 164 us -> 176 us
  local copies, waits for them, and re-layouts: 13.8 us -> 6.87 us
  starting transfers between devices: 27.9 us -> 22.2 us
  waiting for transfers between devices: 23.2 us -> 18.3 us
  Pallas kernels: 11.7 us -> 8.67 us
    all_to_all x13 -> x14, blocking collectives: 164 us -> 176 us  [swap(): return lax.all_to_all(blocks, axis, 0, 0, tiled=True)]
    all_to_all x3 -> x2, starting transfers between devices: 16.4 us -> 10.7 us  [swap(): return lax.all_to_all(blocks, axis, 0, 0, tiled=True)]
    ppermute x3, waiting for transfers between devices: 7.57 us -> 2.43 us  [local(): weights[step] = lax.ppermute(dealt[step], 'x', pairs)]
    unnamed x34 -> x30, local copies, waits for them, and re-layouts: 10.1 us -> 5.21 us
    pallas_call x18, Pallas kernels: 11.7 us -> 8.67 us  [call(): pl.pallas_call(body, out_shape=out, in_specs=[scalars] * smem + [vmem] *...]
    all_to_all x3 -> x2, waiting for transfers between devices: 5.62 us -> 5.94 us  [swap(): return lax.all_to_all(blocks, axis, 0, 0, tiled=True)]
  transfers between devices with their start and end apart: 9 -> 8, of which waited for: 7 -> 6; matrix products, arithmetic and copies ran while one was open for 1% -> 0% of each run, Pallas kernels for 0% -> 1%
where the time goes in v4:
time: 233 us; the launch traced here: 232 us
  blocking collectives  176 us (76%)
  starting transfers between devices  22.2 us (10%)
  waiting for transfers between devices  18.3 us (8%)
  Pallas kernels  8.67 us (4%)
  local copies, waits for them, and re-layouts  6.87 us (3%)
    all_to_all x14, blocking collectives, swap(): return lax.all_to_all(blocks, axis, 0, 0, tiled=True)  176 us
    ppermute x3, starting transfers between devices, local(): weights[step] = lax.ppermute(dealt[step], 'x', pairs)  11.5 us
    all_to_all x2, starting transfers between devices, swap(): return lax.all_to_all(blocks, axis, 0, 0, tiled=True)  10.7 us
    ppermute x3, waiting for transfers between devices, local(): own = lax.ppermute(send, SECTION, ring)  9.98 us
    pallas_call x18, Pallas kernels, call(): pl.pallas_call(body, out_shape=out, in_specs=[scalars] * smem + [vmem] *...  8.67 us
    all_to_all x2, waiting for transfers between devices, swap(): return lax.all_to_all(blocks, axis, 0, 0, tiled=True)  5.94 us
    unnamed x30, local copies, waits for them, and re-layouts  5.21 us
  transfers between devices with their start and end apart: 8, of which 6 were waited for; matrix products, arithmetic and copies ran while one was open for 0% of the time, Pallas kernels for 1%

profile of v4, /device:TPU:64, one launch (start us, length us, event | category | flops | bytes accessed | tf_op | source)
XLA Modules:
  0.0 231.9 jit_solution(17805960930031290942)
XLA Ops:
  1.5 7.2 %all-to-all-start = ((bf16[8,64,256]{2,1,0:T(8,128)(2,1)}), bf16[8,64,256]{2,1,0:T(8,128)(2,1)S(1)}, u32[]{:S(2)}, u32[]{:S(2)}) async-start(bf16[8,64,256]{2,1,0:T(8,128)(2,1)} %broadcast_in_dim.42), calls=%async_computation | async-start | bytes 524288 | tf_op jit(solution)/shard_map/all_to_all | solution.py:62
  11.4 3.5 %collective-permute-start = (bf16[256,512]{1,0:T(8,128)(2,1)}, bf16[256,512]{1,0:T(8,128)(2,1)S(1)}, u32[]{:S(2)}, u32[]{:S(2)}) collective-permute-start(bf16[256,512]{1,0:T(8,128)(2,1)} %get-tuple-element.31), channel_id=1, source_target_pairs={{0,8},{8,16},{16,24},{24,0},{1,9},{9,17},{17,25},{25,1},{2,10},{10... | collective-permute-start | bytes 786440 | tf_op jit(solution)/shard_map/ppermute | solution.py:208
  14.9 4.6 %collective-permute-start.1 = (bf16[256,512]{1,0:T(8,128)(2,1)}, bf16[256,512]{1,0:T(8,128)(2,1)S(1)}, u32[]{:S(2)}, u32[]{:S(2)}) collective-permute-start(bf16[256,512]{1,0:T(8,128)(2,1)} %get-tuple-element.32), channel_id=1, source_target_pairs={{0,16},{8,24},{16,0},{24,8},{1,17},{9,25},{17,1},{25,9},{2,18},{10... | collective-permute-start | bytes 786440 | tf_op jit(solution)/shard_map/ppermute | solution.py:208
  19.5 3.3 %collective-permute-start.2 = (bf16[256,512]{1,0:T(8,128)(2,1)}, bf16[256,512]{1,0:T(8,128)(2,1)S(1)}, u32[]{:S(2)}, u32[]{:S(2)}) collective-permute-start(bf16[256,512]{1,0:T(8,128)(2,1)} %get-tuple-element.33), channel_id=1, source_target_pairs={{0,24},{8,0},{16,8},{24,16},{1,25},{9,1},{17,9},{25,17},{2,26},{10... | collective-permute-start | bytes 786440 | tf_op jit(solution)/shard_map/ppermute | solution.py:208
  26.0 1.6 history.1
  31.1 12.1 %all_to_all.80.terms_ref = bf16[4,208,256]{2,1,0:T(8,128)(2,1)S(1)} all-to-all(bf16[4,208,256]{2,1,0:T(8,128)(2,1)S(1)} %gate_terms.4), channel_id=1, replica_groups=mesh['z'=8,'core'=2,'x'=4,'y'=8] {'x'}, dimensions={0} | all-to-all | bytes 851968 | tf_op jit(solution)/shard_map/all_to_all | solution.py:62
  43.5 17.2 %all_to_all.81 = bf16[8,64,256]{2,1,0:T(8,128)(2,1)S(1)} all-to-all(bf16[8,64,256]{2,1,0:T(8,128)(2,1)S(1)} %get-tuple-element.38), channel_id=1, replica_groups=mesh['z'=8,'core'=2,'x'=4,'y'=8] {'y'}, dimensions={0} | all-to-all | bytes 524288 | tf_op jit(solution)/shard_map/all_to_all | solution.py:62
  61.7 3.5 %all-to-all-start.3 = ((bf16[4,64,256]{2,1,0:T(8,128)(2,1)}), bf16[4,64,256]{2,1,0:T(8,128)(2,1)S(1)}, u32[]{:S(2)}, u32[]{:S(2)}) async-start(bf16[4,64,256]{2,1,0:T(8,128)(2,1)} %emit_terms.4), calls=%async_computation.3 | async-start | bytes 262144 | tf_op jit(solution)/shard_map/all_to_all | solution.py:62
  65.2 5.9 %all-to-all-done.3.terms_ref = bf16[4,64,256]{2,1,0:T(8,128)(2,1)S(1)} async-done(((bf16[4,64,256]{2,1,0:T(8,128)(2,1)}), bf16[4,64,256]{2,1,0:T(8,128)(2,1)S(1)}, u32[]{:S(2)}, u32[]{:S(2)}) %all-to-all-start.3) | async-done | bytes 131104 | tf_op jit(solution)/shard_map/all_to_all | solution.py:62
  71.2 3.3 %collective-permute-done.3.own_ref = bf16[64,256]{1,0:T(8,128)(2,1)S(1)} collective-permute-done((bf16[64,256]{1,0:T(8,128)(2,1)S(1)}, bf16[64,256]{1,0:T(8,128)(2,1)S(1)}, u32[]{:S(2)}, u32[]{:S(2)}) %collective-permute-start.3) | collective-permute-done | bytes 32800 | tf_op jit(solution)/shard_map/ppermute | solution.py:258
  74.5 14.9 %all_to_all.82 = bf16[8,64,256]{2,1,0:T(8,128)(2,1)S(1)} all-to-all(bf16[8,64,256]{2,1,0:T(8,128)(2,1)S(1)} %broadcast_in_dim.43), channel_id=1, replica_groups=mesh['z'=8,'core'=2,'x'=4,'y'=8] {'y'}, dimensions={0} | all-to-all | bytes 524288 | tf_op jit(solution)/shard_map/all_to_all | solution.py:62
  89.8 11.3 %all_to_all.83.terms_ref = bf16[4,208,256]{2,1,0:T(8,128)(2,1)S(1)} all-to-all(bf16[4,208,256]{2,1,0:T(8,128)(2,1)S(1)} %gate_terms.5), channel_id=1, replica_groups=mesh['z'=8,'core'=2,'x'=4,'y'=8] {'x'}, dimensions={0} | all-to-all | bytes 851968 | tf_op jit(solution)/shard_map/all_to_all | solution.py:62
  101.4 13.9 %all_to_all.84 = bf16[8,64,256]{2,1,0:T(8,128)(2,1)S(1)} all-to-all(bf16[8,64,256]{2,1,0:T(8,128)(2,1)S(1)} %get-tuple-element.43), channel_id=1, replica_groups=mesh['z'=8,'core'=2,'x'=4,'y'=8] {'y'}, dimensions={0} | all-to-all | bytes 524288 | tf_op jit(solution)/shard_map/all_to_all | solution.py:62
  115.7 8.4 %all_to_all.85.terms_ref = bf16[4,64,256]{2,1,0:T(8,128)(2,1)S(1)} all-to-all(bf16[4,64,256]{2,1,0:T(8,128)(2,1)S(1)} %emit_terms.5), channel_id=1, replica_groups=mesh['z'=8,'core'=2,'x'=4,'y'=8] {'x'}, dimensions={0} | all-to-all | bytes 262144 | tf_op jit(solution)/shard_map/all_to_all | solution.py:62
  124.1 3.3 %collective-permute-done.4.own_ref = bf16[64,256]{1,0:T(8,128)(2,1)S(1)} collective-permute-done((bf16[64,256]{1,0:T(8,128)(2,1)S(1)}, bf16[64,256]{1,0:T(8,128)(2,1)S(1)}, u32[]{:S(2)}, u32[]{:S(2)}) %collective-permute-start.4) | collective-permute-done | bytes 32800 | tf_op jit(solution)/shard_map/ppermute | solution.py:258
  127.4 14.9 %all_to_all.86 = bf16[8,64,256]{2,1,0:T(8,128)(2,1)S(1)} all-to-all(bf16[8,64,256]{2,1,0:T(8,128)(2,1)S(1)} %broadcast_in_dim.44), channel_id=1, replica_groups=mesh['z'=8,'core'=2,'x'=4,'y'=8] {'y'}, dimensions={0} | all-to-all | bytes 524288 | tf_op jit(solution)/shard_map/all_to_all | solution.py:62
  142.7 11.3 %all_to_all.87.terms_ref = bf16[4,208,256]{2,1,0:T(8,128)(2,1)S(1)} all-to-all(bf16[4,208,256]{2,1,0:T(8,128)(2,1)S(1)} %gate_terms.6), channel_id=1, replica_groups=mesh['z'=8,'core'=2,'x'=4,'y'=8] {'x'}, dimensions={0} | all-to-all | bytes 851968 | tf_op jit(solution)/shard_map/all_to_all | solution.py:62
  154.4 13.9 %all_to_all.88 = bf16[8,64,256]{2,1,0:T(8,128)(2,1)S(1)} all-to-all(bf16[8,64,256]{2,1,0:T(8,128)(2,1)S(1)} %get-tuple-element.46), channel_id=1, replica_groups=mesh['z'=8,'core'=2,'x'=4,'y'=8] {'y'}, dimensions={0} | all-to-all | bytes 524288 | tf_op jit(solution)/shard_map/all_to_all | solution.py:62
  168.6 8.4 %all_to_all.89.terms_ref = bf16[4,64,256]{2,1,0:T(8,128)(2,1)S(1)} all-to-all(bf16[4,64,256]{2,1,0:T(8,128)(2,1)S(1)} %emit_terms.6), channel_id=1, replica_groups=mesh['z'=8,'core'=2,'x'=4,'y'=8] {'x'}, dimensions={0} | all-to-all | bytes 262144 | tf_op jit(solution)/shard_map/all_to_all | solution.py:62
  177.0 3.3 %collective-permute-done.5.own_ref = bf16[64,256]{1,0:T(8,128)(2,1)S(1)} collective-permute-done((bf16[64,256]{1,0:T(8,128)(2,1)S(1)}, bf16[64,256]{1,0:T(8,128)(2,1)S(1)}, u32[]{:S(2)}, u32[]{:S(2)}) %collective-permute-start.5) | collective-permute-done | bytes 32800 | tf_op jit(solution)/shard_map/ppermute | solution.py:258
  180.4 15.7 %all_to_all.90 = bf16[8,64,256]{2,1,0:T(8,128)(2,1)S(1)} all-to-all(bf16[8,64,256]{2,1,0:T(8,128)(2,1)S(1)} %broadcast_in_dim.45), channel_id=1, replica_groups=mesh['z'=8,'core'=2,'x'=4,'y'=8] {'y'}, dimensions={0} | all-to-all | bytes 524288 | tf_op jit(solution)/shard_map/all_to_all | solution.py:62
  196.4 11.4 %all_to_all.91.terms_ref = bf16[4,208,256]{2,1,0:T(8,128)(2,1)S(1)} all-to-all(bf16[4,208,256]{2,1,0:T(8,128)(2,1)S(1)} %gate_terms.7), channel_id=1, replica_groups=mesh['z'=8,'core'=2,'x'=4,'y'=8] {'x'}, dimensions={0} | all-to-all | bytes 851968 | tf_op jit(solution)/shard_map/all_to_all | solution.py:62
  208.7 13.9 %all_to_all.92 = bf16[8,64,256]{2,1,0:T(8,128)(2,1)S(1)} all-to-all(bf16[8,64,256]{2,1,0:T(8,128)(2,1)S(1)} %get-tuple-element.49), channel_id=1, replica_groups=mesh['z'=8,'core'=2,'x'=4,'y'=8] {'y'}, dimensions={0} | all-to-all | bytes 524288 | tf_op jit(solution)/shard_map/all_to_all | solution.py:62
  222.9 8.4 %all_to_all.93.terms_ref = bf16[4,64,256]{2,1,0:T(8,128)(2,1)S(1)} all-to-all(bf16[4,64,256]{2,1,0:T(8,128)(2,1)S(1)} %emit_terms.7), channel_id=1, replica_groups=mesh['z'=8,'core'=2,'x'=4,'y'=8] {'x'}, dimensions={0} | all-to-all | bytes 262144 | tf_op jit(solution)/shard_map/all_to_all | solution.py:62
  (59 shorter events, 16.4 us)
Async XLA Ops:
  0.0 8.8 %copy-start.6 = (bf16[1,2048,64]{1,2,0:T(8,128)(2,1)S(1)}, bf16[1,2048,64]{1,2,0:T(8,128)(2,1)}, u32[]{:S(2)}) copy-start(bf16[1,2048,64]{1,2,0:T(8,128)(2,1)} %param.19) | copy-start | bytes 786436
  1.5 7.3 %copy-start.4 = (bf16[1,2048,64]{1,2,0:T(8,128)(2,1)S(1)}, bf16[1,2048,64]{1,2,0:T(8,128)(2,1)}, u32[]{:S(2)}) copy-start(bf16[1,2048,64]{1,2,0:T(8,128)(2,1)} %param.17) | copy-start | bytes 786436
  1.5 7.3 %copy-start.5 = (bf16[1,2048,64]{1,2,0:T(8,128)(2,1)S(1)}, bf16[1,2048,64]{1,2,0:T(8,128)(2,1)}, u32[]{:S(2)}) copy-start(bf16[1,2048,64]{1,2,0:T(8,128)(2,1)} %param.18) | copy-start | bytes 786436
  1.5 29.2 %all-to-all-start = ((bf16[8,64,256]{2,1,0:T(8,128)(2,1)}), bf16[8,64,256]{2,1,0:T(8,128)(2,1)S(1)}, u32[]{:S(2)}, u32[]{:S(2)}) async-start(bf16[8,64,256]{2,1,0:T(8,128)(2,1)} %broadcast_in_dim.42), calls=%async_computation | async-start | bytes 524288 | tf_op jit(solution)/shard_map/all_to_all | solution.py:62
  8.7 0.7 copy-start.12
  9.4 0.9 copy-start.7
  10.4 12.5 %copy-start.14 = (f32[1,64]{1,0:T(1,128)S(1)}, f32[1,64]{1,0:T(1,128)}, u32[]{:S(2)}) copy-start(f32[1,64]{1,0:T(1,128)} %param.21) | copy-start | bytes 772
  10.4 12.6 %copy-start.2 = (bf16[512,256]{1,0:T(8,128)(2,1)S(1)}, bf16[512,256]{1,0:T(8,128)(2,1)}, u32[]{:S(2)}) copy-start(bf16[512,256]{1,0:T(8,128)(2,1)} %constant.25.clone.rest_1_) | copy-start | bytes 786436
  10.4 12.6 %copy-start.3 = (bf16[256,512]{1,0:T(8,128)(2,1)S(1)}, bf16[256,512]{1,0:T(8,128)(2,1)}, u32[]{:S(2)}) copy-start(bf16[256,512]{1,0:T(8,128)(2,1)} %constant.24.clone.rest_0_) | copy-start | bytes 786436
  10.4 12.6 %copy-start.9 = (bf16[3,256,64]{1,2,0:T(8,128)(2,1)S(1)}, bf16[3,256,64]{1,2,0:T(8,128)(2,1)}, u32[]{:S(2)}) copy-start(bf16[3,256,64]{1,2,0:T(8,128)(2,1)} %param.14) | copy-start | bytes 294916
  11.4 11.7 %copy-start.8 = (bf16[1,256,64]{1,2,0:T(8,128)(2,1)S(1)}, bf16[1,256,64]{1,2,0:T(8,128)(2,1)}, u32[]{:S(2)}) copy-start(bf16[1,256,64]{1,2,0:T(8,128)(2,1)} %param.13) | copy-start | bytes 98308
  11.4 16.9 %collective-permute-start = (bf16[256,512]{1,0:T(8,128)(2,1)}, bf16[256,512]{1,0:T(8,128)(2,1)S(1)}, u32[]{:S(2)}, u32[]{:S(2)}) collective-permute-start(bf16[256,512]{1,0:T(8,128)(2,1)} %get-tuple-element.31), channel_id=1, source_target_pairs={{0,8},{8,16},{16,24},{24,0},{1,9},{9,17},{17,25},{25,1},{2,10},{10... | collective-permute-start | bytes 786440 | tf_op jit(solution)/shard_map/ppermute | solution.py:208
  14.9 14.3 %collective-permute-start.1 = (bf16[256,512]{1,0:T(8,128)(2,1)}, bf16[256,512]{1,0:T(8,128)(2,1)S(1)}, u32[]{:S(2)}, u32[]{:S(2)}) collective-permute-start(bf16[256,512]{1,0:T(8,128)(2,1)} %get-tuple-element.32), channel_id=1, source_target_pairs={{0,16},{8,24},{16,0},{24,8},{1,17},{9,25},{17,1},{25,9},{2,18},{10... | collective-permute-start | bytes 786440 | tf_op jit(solution)/shard_map/ppermute | solution.py:208
  19.5 11.1 %collective-permute-start.2 = (bf16[256,512]{1,0:T(8,128)(2,1)}, bf16[256,512]{1,0:T(8,128)(2,1)S(1)}, u32[]{:S(2)}, u32[]{:S(2)}) collective-permute-start(bf16[256,512]{1,0:T(8,128)(2,1)} %get-tuple-element.33), channel_id=1, source_target_pairs={{0,24},{8,0},{16,8},{24,16},{1,25},{9,1},{17,9},{25,17},{2,26},{10... | collective-permute-start | bytes 786440 | tf_op jit(solution)/shard_map/ppermute | solution.py:208
  23.0 0.7 copy-start.13
  23.7 1.2 copy-start
  24.9 1.1 copy-start.1
  27.6 0.6 copy-start.10
  61.7 9.4 %copy-start.11 = (bf16[64,256]{1,0:T(8,128)(2,1)S(1)}, bf16[64,256]{1,0:T(8,128)(2,1)}, u32[]{:S(2)}) copy-start(bf16[64,256]{1,0:T(8,128)(2,1)} %copy-done.10) | copy-start | bytes 98308
  61.7 9.4 %all-to-all-start.3 = ((bf16[4,64,256]{2,1,0:T(8,128)(2,1)}), bf16[4,64,256]{2,1,0:T(8,128)(2,1)S(1)}, u32[]{:S(2)}, u32[]{:S(2)}) async-start(bf16[4,64,256]{2,1,0:T(8,128)(2,1)} %emit_terms.4), calls=%async_computation.3 | async-start | bytes 262144 | tf_op jit(solution)/shard_map/all_to_all | solution.py:62
  71.1 3.4 %collective-permute-start.3 = (bf16[64,256]{1,0:T(8,128)(2,1)S(1)}, bf16[64,256]{1,0:T(8,128)(2,1)S(1)}, u32[]{:S(2)}, u32[]{:S(2)}) collective-permute-start(bf16[64,256]{1,0:T(8,128)(2,1)S(1)} %get-tuple-element.41), channel_id=1, source_target_pairs={{0,32},{32,64},{64,96},{96,128},{128,160},{160,192},{192,224},{224... | collective-permute-start | bytes 98312 | tf_op jit(solution)/shard_map/ppermute | solution.py:258
  124.0 3.4 %collective-permute-start.4 = (bf16[64,256]{1,0:T(8,128)(2,1)S(1)}, bf16[64,256]{1,0:T(8,128)(2,1)S(1)}, u32[]{:S(2)}, u32[]{:S(2)}) collective-permute-start(bf16[64,256]{1,0:T(8,128)(2,1)S(1)} %get-tuple-element.44), channel_id=1, source_target_pairs={{0,32},{32,64},{64,96},{96,128},{128,160},{160,192},{192,224},{224... | collective-permute-start | bytes 98312 | tf_op jit(solution)/shard_map/ppermute | solution.py:258
  177.0 3.4 %collective-permute-start.5 = (bf16[64,256]{1,0:T(8,128)(2,1)S(1)}, bf16[64,256]{1,0:T(8,128)(2,1)S(1)}, u32[]{:S(2)}, u32[]{:S(2)}) collective-permute-start(bf16[64,256]{1,0:T(8,128)(2,1)S(1)} %get-tuple-element.47), channel_id=1, source_target_pairs={{0,32},{32,64},{64,96},{96,128},{128,160},{160,192},{192,224},{224... | collective-permute-start | bytes 98312 | tf_op jit(solution)/shard_map/ppermute | solution.py:258

commit v5 on v4

--- a/solution.py
+++ b/solution.py
@@ -98,7 +98,8 @@
             first, second = held_ref[lag - tick - 1, 0], held_ref[lag - tick - 1, 1]
             real += filt_ref[lag, 0] * first - filt_ref[lag, 1] * second
             imag += filt_ref[lag, 0] * second + filt_ref[lag, 1] * first
-        known_ref[tick, 0], known_ref[tick, 1] = fold(jnp.stack([real, imag]))
+        real, imag = fold(jnp.stack([real, imag]))
+        known_ref[tick, 0], known_ref[tick, 1] = real.astype(known_ref.dtype), imag.astype(known_ref.dtype)
     for lag in range(blocks + 1):
         real, imag = fold(filt_ref[lag])
         if lag == 0:
@@ -128,7 +129,8 @@
 
 
 def mix_kernel(tick, past, stored, features, live_ref, terms_ref, fwd_ref, inv_ref, filt_ref, *rest):
-    lagged, (mixed_ref, spec_ref) = rest[:-2], rest[-2:]
+    count = past + (stored is not None)
+    lagged, mixed_ref, spec_ref = rest[:count], rest[count], rest[count + 1 :]
     copies, width, _ = mixed_ref.shape
     half = fwd_ref.shape[1] // 2
     terms = jnp.sum(terms_ref[...].astype(jnp.float32), axis=0)
@@ -137,13 +139,15 @@
     driven = jnp.where(live_ref[tick] > 0.0, gates[width : 2 * width] * gates[:width], 0.0)
     spectrum = jnp.dot(driven.astype(jnp.bfloat16), fwd_ref[...], preferred_element_type=jnp.float32)
     spectrum = spectrum[:, :half], spectrum[:, half:]
-    spec_ref[0], spec_ref[1] = spectrum
+    for ref in spec_ref:
+        ref[0], ref[1] = spectrum
     real, imag = times(filt_ref[0], spectrum)
     for lag in range(1, past + 1):
         more = times(filt_ref[lag], lagged[lag - 1][...])
         real, imag = real + more[0], imag + more[1]
     if stored is not None:
-        real, imag = real + lagged[-1][stored, 0], imag + lagged[-1][stored, 1]
+        more = lagged[-1][stored].astype(jnp.float32)
+        real, imag = real + more[0], imag + more[1]
     packed = jnp.concatenate([real, imag], axis=1).astype(jnp.bfloat16)
     conv = jnp.dot(packed, inv_ref[...], preferred_element_type=jnp.float32)
     mixed = (gates[2 * width :] * conv).astype(mixed_ref.dtype)
@@ -166,10 +170,10 @@
     return total.astype(own_ref.dtype)
 
 
-def add_and_send_kernel(tick, last_ref, terms_ref, own_ref, fresh_ref, out_ref, send_ref):
+def add_and_send_kernel(tick, layers, section_ref, terms_ref, own_ref, fresh_ref, out_ref, send_ref):
     out = total_of(terms_ref, own_ref)
     out_ref[...] = out
-    send_ref[...] = jnp.where(last_ref[0] == 1, fresh_ref[tick], out)
+    send_ref[...] = jnp.where(section_ref[0] == layers - 1, fresh_ref[tick], out)
 
 
 def finish_kernel(terms_ref, own_ref, *refs):
@@ -191,7 +195,7 @@
     bf16 = functools.partial(jax.ShapeDtypeStruct, dtype=jnp.bfloat16)
     f32 = functools.partial(jax.ShapeDtypeStruct, dtype=jnp.float32)
     x = lax.axis_index("x").astype(jnp.int32)[None]
-    last = (section == layers - 1).astype(jnp.int32)[None]
+    place = section.astype(jnp.int32)[None]
 
     own = feeds[0].T
     part = gather_rows(jnp.broadcast_to(own[None], (copies,) + own.shape))
@@ -210,9 +214,9 @@
     passed = [jnp.asarray(t) for t in tables(positions, 2 * half)] + [newcomers.transpose(0, 2, 1), own]
     live, known, filters, forward, inverse, fresh, own = call(
         history_kernel,
-        [f32((ticks, 1, positions)), f32((blocks, 2, width, half)), f32((blocks + 1, 2, width, half))]
+        [f32((ticks, 1, positions)), bf16((blocks, 2, width, half)), f32((blocks + 1, 2, width, half))]
         + [jax.ShapeDtypeStruct(t.shape, t.dtype) for t in passed],
-        [section.astype(jnp.int32)[None], occupied, skip[0][:, None], filters[0], archive[0]] + passed,
+        [place, occupied, skip[0][:, None], filters[0], archive[0]] + passed,
         "history",
         smem=2,
     )
@@ -231,13 +235,13 @@
         past = min(tick, blocks)
         stored = tick if tick < blocks else None
         lagged = spectra[::-1][:past] + ([known] if stored is not None else [])
-        mixed, spectrum = call(
+        mixed, *spectrum = call(
             functools.partial(mix_kernel, tick, past, stored, features),
-            [bf16((copies, width, positions)), f32((2, width, half))],
+            [bf16((copies, width, positions))] + [f32((2, width, half))] * (tick < ticks - 1),
             [live, terms, forward, inverse, filters] + lagged,
             "mix",
         )
-        spectra.append(spectrum)
+        spectra += spectrum
         terms = call(
             emit_terms_kernel,
             bf16((groups, width, positions)),
@@ -248,9 +252,9 @@
         terms = swap(terms, "x")
         if tick < ticks - 1:
             out, send = call(
-                functools.partial(add_and_send_kernel, tick),
+                functools.partial(add_and_send_kernel, tick, layers),
                 [bf16(own.shape)] * 2,
-                [last, terms, own, fresh],
+                [place, terms, own, fresh],
                 "add",
                 smem=1,
             )

time: 233 us -> 231 us (level)
  blocking collectives: 176 us -> 184 us
  waiting for transfers between devices: 18.3 us -> 11.4 us
  starting transfers between devices: 22.2 us -> 18.8 us
    all_to_all x14 -> x15, blocking collectives: 176 us -> 184 us  [swap(): return lax.all_to_all(blocks, axis, 0, 0, tiled=True)]
    all_to_all x2 -> x1, waiting for transfers between devices: 5.94 us -> 0.01 us  [swap(): return lax.all_to_all(blocks, axis, 0, 0, tiled=True)]
    all_to_all x2 -> x1, starting transfers between devices: 10.7 us -> 7.23 us  [swap(): return lax.all_to_all(blocks, axis, 0, 0, tiled=True)]
    unnamed x30 -> x26, local copies, waits for them, and re-layouts: 5.21 us -> 6.32 us
  transfers between devices with their start and end apart: 8 -> 7, of which waited for: 6 -> 4; matrix products, arithmetic and copies ran while one was open for 0% -> 0% of each run, Pallas kernels for 1% -> 1%
where the time goes in v5:
time: 231 us; the launch traced here: 230 us
  blocking collectives  184 us (80%)
  starting transfers between devices  18.8 us (8%)
  waiting for transfers between devices  11.4 us (5%)
  local copies, waits for them, and re-layouts  8.03 us (3%)
  Pallas kernels  7.44 us (3%)
    all_to_all x15, blocking collectives, swap(): return lax.all_to_all(blocks, axis, 0, 0, tiled=True)  184 us
    ppermute x3, starting transfers between devices, local(): weights[step] = lax.ppermute(dealt[step], 'x', pairs)  11.5 us
    ppermute x3, waiting for transfers between devices, local(): own = lax.ppermute(send, SECTION, ring)  9.98 us
    pallas_call x18, Pallas kernels, call(): pl.pallas_call(body, out_shape=out, in_specs=[scalars] * smem + [vmem] *...  7.44 us
    all_to_all x1, starting transfers between devices, swap(): return lax.all_to_all(blocks, axis, 0, 0, tiled=True)  7.23 us
    unnamed x26, local copies, waits for them, and re-layouts  6.32 us
  transfers between devices with their start and end apart: 7, of which 4 were waited for; matrix products, arithmetic and copies ran while one was open for 0% of the time, Pallas kernels for 1%

profile of v5, /device:TPU:64, one launch (start us, length us, event | category | flops | bytes accessed | tf_op | source)
XLA Modules:
  0.0 229.8 jit_solution(5155975069402818612)
XLA Ops:
  0.0 1.6 broadcast_in_dim.16
  1.6 7.2 %all-to-all-start = ((bf16[8,64,256]{2,1,0:T(8,128)(2,1)}), bf16[8,64,256]{2,1,0:T(8,128)(2,1)S(1)}, u32[]{:S(2)}, u32[]{:S(2)}) async-start(bf16[8,64,256]{2,1,0:T(8,128)(2,1)} %broadcast_in_dim.16), calls=%async_computation | async-start | bytes 524288 | tf_op jit(solution)/shard_map/all_to_all | solution.py:62
  11.4 3.5 %collective-permute-start = (bf16[256,512]{1,0:T(8,128)(2,1)}, bf16[256,512]{1,0:T(8,128)(2,1)S(1)}, u32[]{:S(2)}, u32[]{:S(2)}) collective-permute-start(bf16[256,512]{1,0:T(8,128)(2,1)} %get-tuple-element.30), channel_id=1, source_target_pairs={{0,8},{8,16},{16,24},{24,0},{1,9},{9,17},{17,25},{25,1},{2,10},{10... | collective-permute-start | bytes 786440 | tf_op jit(solution)/shard_map/ppermute | solution.py:212
  14.9 4.6 %collective-permute-start.1 = (bf16[256,512]{1,0:T(8,128)(2,1)}, bf16[256,512]{1,0:T(8,128)(2,1)S(1)}, u32[]{:S(2)}, u32[]{:S(2)}) collective-permute-start(bf16[256,512]{1,0:T(8,128)(2,1)} %get-tuple-element.31), channel_id=1, source_target_pairs={{0,16},{8,24},{16,0},{24,8},{1,17},{9,25},{17,1},{25,9},{2,18},{10... | collective-permute-start | bytes 786440 | tf_op jit(solution)/shard_map/ppermute | solution.py:212
  19.6 3.3 %collective-permute-start.2 = (bf16[256,512]{1,0:T(8,128)(2,1)}, bf16[256,512]{1,0:T(8,128)(2,1)S(1)}, u32[]{:S(2)}, u32[]{:S(2)}) collective-permute-start(bf16[256,512]{1,0:T(8,128)(2,1)} %get-tuple-element.32), channel_id=1, source_target_pairs={{0,24},{8,0},{16,8},{24,16},{1,25},{9,1},{17,9},{25,17},{2,26},{10... | collective-permute-start | bytes 786440 | tf_op jit(solution)/shard_map/ppermute | solution.py:212
  27.7 1.6 history.1
  31.1 12.1 %all_to_all.80.terms_ref = bf16[4,208,256]{2,1,0:T(8,128)(2,1)S(1)} all-to-all(bf16[4,208,256]{2,1,0:T(8,128)(2,1)S(1)} %gate_terms.4), channel_id=1, replica_groups=mesh['z'=8,'core'=2,'x'=4,'y'=8] {'x'}, dimensions={0} | all-to-all | bytes 851968 | tf_op jit(solution)/shard_map/all_to_all | solution.py:62
  43.6 17.2 %all_to_all.81 = bf16[8,64,256]{2,1,0:T(8,128)(2,1)S(1)} all-to-all(bf16[8,64,256]{2,1,0:T(8,128)(2,1)S(1)} %get-tuple-element.37), channel_id=1, replica_groups=mesh['z'=8,'core'=2,'x'=4,'y'=8] {'y'}, dimensions={0} | all-to-all | bytes 524288 | tf_op jit(solution)/shard_map/all_to_all | solution.py:62
  61.1 8.4 %all_to_all.82.terms_ref = bf16[4,64,256]{2,1,0:T(8,128)(2,1)S(1)} all-to-all(bf16[4,64,256]{2,1,0:T(8,128)(2,1)S(1)} %emit_terms.4), channel_id=1, replica_groups=mesh['z'=8,'core'=2,'x'=4,'y'=8] {'x'}, dimensions={0} | all-to-all | bytes 262144 | tf_op jit(solution)/shard_map/all_to_all | solution.py:62
  69.5 3.3 %collective-permute-done.3.own_ref = bf16[64,256]{1,0:T(8,128)(2,1)S(1)} collective-permute-done((bf16[64,256]{1,0:T(8,128)(2,1)S(1)}, bf16[64,256]{1,0:T(8,128)(2,1)S(1)}, u32[]{:S(2)}, u32[]{:S(2)}) %collective-permute-start.3) | collective-permute-done | bytes 32800 | tf_op jit(solution)/shard_map/ppermute | solution.py:262
  72.9 14.9 %all_to_all.83 = bf16[8,64,256]{2,1,0:T(8,128)(2,1)S(1)} all-to-all(bf16[8,64,256]{2,1,0:T(8,128)(2,1)S(1)} %broadcast_in_dim.17), channel_id=1, replica_groups=mesh['z'=8,'core'=2,'x'=4,'y'=8] {'y'}, dimensions={0} | all-to-all | bytes 524288 | tf_op jit(solution)/shard_map/all_to_all | solution.py:62
  88.1 11.3 %all_to_all.84.terms_ref = bf16[4,208,256]{2,1,0:T(8,128)(2,1)S(1)} all-to-all(bf16[4,208,256]{2,1,0:T(8,128)(2,1)S(1)} %gate_terms.5), channel_id=1, replica_groups=mesh['z'=8,'core'=2,'x'=4,'y'=8] {'x'}, dimensions={0} | all-to-all | bytes 851968 | tf_op jit(solution)/shard_map/all_to_all | solution.py:62
  99.8 13.9 %all_to_all.85 = bf16[8,64,256]{2,1,0:T(8,128)(2,1)S(1)} all-to-all(bf16[8,64,256]{2,1,0:T(8,128)(2,1)S(1)} %get-tuple-element.42), channel_id=1, replica_groups=mesh['z'=8,'core'=2,'x'=4,'y'=8] {'y'}, dimensions={0} | all-to-all | bytes 524288 | tf_op jit(solution)/shard_map/all_to_all | solution.py:62
  114.0 8.4 %all_to_all.86.terms_ref = bf16[4,64,256]{2,1,0:T(8,128)(2,1)S(1)} all-to-all(bf16[4,64,256]{2,1,0:T(8,128)(2,1)S(1)} %emit_terms.5), channel_id=1, replica_groups=mesh['z'=8,'core'=2,'x'=4,'y'=8] {'x'}, dimensions={0} | all-to-all | bytes 262144 | tf_op jit(solution)/shard_map/all_to_all | solution.py:62
  122.4 3.3 %collective-permute-done.4.own_ref = bf16[64,256]{1,0:T(8,128)(2,1)S(1)} collective-permute-done((bf16[64,256]{1,0:T(8,128)(2,1)S(1)}, bf16[64,256]{1,0:T(8,128)(2,1)S(1)}, u32[]{:S(2)}, u32[]{:S(2)}) %collective-permute-start.4) | collective-permute-done | bytes 32800 | tf_op jit(solution)/shard_map/ppermute | solution.py:262
  125.8 14.9 %all_to_all.87 = bf16[8,64,256]{2,1,0:T(8,128)(2,1)S(1)} all-to-all(bf16[8,64,256]{2,1,0:T(8,128)(2,1)S(1)} %broadcast_in_dim.18), channel_id=1, replica_groups=mesh['z'=8,'core'=2,'x'=4,'y'=8] {'y'}, dimensions={0} | all-to-all | bytes 524288 | tf_op jit(solution)/shard_map/all_to_all | solution.py:62
  141.1 11.3 %all_to_all.88.terms_ref = bf16[4,208,256]{2,1,0:T(8,128)(2,1)S(1)} all-to-all(bf16[4,208,256]{2,1,0:T(8,128)(2,1)S(1)} %gate_terms.6), channel_id=1, replica_groups=mesh['z'=8,'core'=2,'x'=4,'y'=8] {'x'}, dimensions={0} | all-to-all | bytes 851968 | tf_op jit(solution)/shard_map/all_to_all | solution.py:62
  152.7 13.9 %all_to_all.89 = bf16[8,64,256]{2,1,0:T(8,128)(2,1)S(1)} all-to-all(bf16[8,64,256]{2,1,0:T(8,128)(2,1)S(1)} %get-tuple-element.45), channel_id=1, replica_groups=mesh['z'=8,'core'=2,'x'=4,'y'=8] {'y'}, dimensions={0} | all-to-all | bytes 524288 | tf_op jit(solution)/shard_map/all_to_all | solution.py:62
  166.9 8.4 %all_to_all.90.terms_ref = bf16[4,64,256]{2,1,0:T(8,128)(2,1)S(1)} all-to-all(bf16[4,64,256]{2,1,0:T(8,128)(2,1)S(1)} %emit_terms.6), channel_id=1, replica_groups=mesh['z'=8,'core'=2,'x'=4,'y'=8] {'x'}, dimensions={0} | all-to-all | bytes 262144 | tf_op jit(solution)/shard_map/all_to_all | solution.py:62
  175.4 3.3 %collective-permute-done.5.own_ref = bf16[64,256]{1,0:T(8,128)(2,1)S(1)} collective-permute-done((bf16[64,256]{1,0:T(8,128)(2,1)S(1)}, bf16[64,256]{1,0:T(8,128)(2,1)S(1)}, u32[]{:S(2)}, u32[]{:S(2)}) %collective-permute-start.5) | collective-permute-done | bytes 32800 | tf_op jit(solution)/shard_map/ppermute | solution.py:262
  178.7 15.7 %all_to_all.91 = bf16[8,64,256]{2,1,0:T(8,128)(2,1)S(1)} all-to-all(bf16[8,64,256]{2,1,0:T(8,128)(2,1)S(1)} %broadcast_in_dim.38), channel_id=1, replica_groups=mesh['z'=8,'core'=2,'x'=4,'y'=8] {'y'}, dimensions={0} | all-to-all | bytes 524288 | tf_op jit(solution)/shard_map/all_to_all | solution.py:62
  194.8 11.4 %all_to_all.92.terms_ref = bf16[4,208,256]{2,1,0:T(8,128)(2,1)S(1)} all-to-all(bf16[4,208,256]{2,1,0:T(8,128)(2,1)S(1)} %gate_terms.7), channel_id=1, replica_groups=mesh['z'=8,'core'=2,'x'=4,'y'=8] {'x'}, dimensions={0} | all-to-all | bytes 851968 | tf_op jit(solution)/shard_map/all_to_all | solution.py:62
  206.5 13.9 %all_to_all.93 = bf16[8,64,256]{2,1,0:T(8,128)(2,1)S(1)} all-to-all(bf16[8,64,256]{2,1,0:T(8,128)(2,1)S(1)} %mix.7), channel_id=1, replica_groups=mesh['z'=8,'core'=2,'x'=4,'y'=8] {'y'}, dimensions={0} | all-to-all | bytes 524288 | tf_op jit(solution)/shard_map/all_to_all | solution.py:62
  220.7 8.4 %all_to_all.94.terms_ref = bf16[4,64,256]{2,1,0:T(8,128)(2,1)S(1)} all-to-all(bf16[4,64,256]{2,1,0:T(8,128)(2,1)S(1)} %emit_terms.7), channel_id=1, replica_groups=mesh['z'=8,'core'=2,'x'=4,'y'=8] {'x'}, dimensions={0} | all-to-all | bytes 262144 | tf_op jit(solution)/shard_map/all_to_all | solution.py:62
  (54 shorter events, 13.8 us)
Async XLA Ops:
  0.0 8.8 %copy-start.4 = (bf16[1,2048,64]{1,2,0:T(8,128)(2,1)S(1)}, bf16[1,2048,64]{1,2,0:T(8,128)(2,1)}, u32[]{:S(2)}) copy-start(bf16[1,2048,64]{1,2,0:T(8,128)(2,1)} %param.17) | copy-start | bytes 786436
  0.0 8.8 %copy-start.5 = (bf16[1,2048,64]{1,2,0:T(8,128)(2,1)S(1)}, bf16[1,2048,64]{1,2,0:T(8,128)(2,1)}, u32[]{:S(2)}) copy-start(bf16[1,2048,64]{1,2,0:T(8,128)(2,1)} %param.18) | copy-start | bytes 786436
  0.0 8.8 %copy-start.6 = (bf16[1,2048,64]{1,2,0:T(8,128)(2,1)S(1)}, bf16[1,2048,64]{1,2,0:T(8,128)(2,1)}, u32[]{:S(2)}) copy-start(bf16[1,2048,64]{1,2,0:T(8,128)(2,1)} %param.19) | copy-start | bytes 786436
  1.6 21.5 %copy-start.1 = (f32[1,3,2,64,512]{4,3,2,1,0:T(8,128)S(1)}, f32[1,3,2,64,512]{4,3,2,1,0:T(8,128)}, u32[]{:S(2)}) copy-start(f32[1,3,2,64,512]{4,3,2,1,0:T(8,128)} %param.23) | copy-start | bytes 2359300
  1.6 29.2 %all-to-all-start = ((bf16[8,64,256]{2,1,0:T(8,128)(2,1)}), bf16[8,64,256]{2,1,0:T(8,128)(2,1)S(1)}, u32[]{:S(2)}, u32[]{:S(2)}) async-start(bf16[8,64,256]{2,1,0:T(8,128)(2,1)} %broadcast_in_dim.16), calls=%async_computation | async-start | bytes 524288 | tf_op jit(solution)/shard_map/all_to_all | solution.py:62
  8.8 1.0 copy-start.7
  9.8 0.7 copy-start.10
  10.5 12.5 %copy-start.12 = (f32[1,64]{1,0:T(1,128)S(1)}, f32[1,64]{1,0:T(1,128)}, u32[]{:S(2)}) copy-start(f32[1,64]{1,0:T(1,128)} %param.21) | copy-start | bytes 772
  11.4 11.6 %copy-start.8 = (bf16[1,256,64]{1,2,0:T(8,128)(2,1)S(1)}, bf16[1,256,64]{1,2,0:T(8,128)(2,1)}, u32[]{:S(2)}) copy-start(bf16[1,256,64]{1,2,0:T(8,128)(2,1)} %param.13) | copy-start | bytes 98308
  11.4 17.9 %collective-permute-start = (bf16[256,512]{1,0:T(8,128)(2,1)}, bf16[256,512]{1,0:T(8,128)(2,1)S(1)}, u32[]{:S(2)}, u32[]{:S(2)}) collective-permute-start(bf16[256,512]{1,0:T(8,128)(2,1)} %get-tuple-element.30), channel_id=1, source_target_pairs={{0,8},{8,16},{16,24},{24,0},{1,9},{9,17},{17,25},{25,1},{2,10},{10... | collective-permute-start | bytes 786440 | tf_op jit(solution)/shard_map/ppermute | solution.py:212
  14.9 14.4 %collective-permute-start.1 = (bf16[256,512]{1,0:T(8,128)(2,1)}, bf16[256,512]{1,0:T(8,128)(2,1)S(1)}, u32[]{:S(2)}, u32[]{:S(2)}) collective-permute-start(bf16[256,512]{1,0:T(8,128)(2,1)} %get-tuple-element.31), channel_id=1, source_target_pairs={{0,16},{8,24},{16,0},{24,8},{1,17},{9,25},{17,1},{25,9},{2,18},{10... | collective-permute-start | bytes 786440 | tf_op jit(solution)/shard_map/ppermute | solution.py:212
  19.6 11.1 %collective-permute-start.2 = (bf16[256,512]{1,0:T(8,128)(2,1)}, bf16[256,512]{1,0:T(8,128)(2,1)S(1)}, u32[]{:S(2)}, u32[]{:S(2)}) collective-permute-start(bf16[256,512]{1,0:T(8,128)(2,1)} %get-tuple-element.32), channel_id=1, source_target_pairs={{0,24},{8,0},{16,8},{24,16},{1,25},{9,1},{17,9},{25,17},{2,26},{10... | collective-permute-start | bytes 786440 | tf_op jit(solution)/shard_map/ppermute | solution.py:212
  23.1 0.7 copy-start.11
  23.7 1.2 copy-start
  24.9 0.9 copy-start.2
  25.9 0.9 copy-start.3
  26.8 0.9 copy-start.9
  69.5 3.4 %collective-permute-start.3 = (bf16[64,256]{1,0:T(8,128)(2,1)S(1)}, bf16[64,256]{1,0:T(8,128)(2,1)S(1)}, u32[]{:S(2)}, u32[]{:S(2)}) collective-permute-start(bf16[64,256]{1,0:T(8,128)(2,1)S(1)} %get-tuple-element.40), channel_id=1, source_target_pairs={{0,32},{32,64},{64,96},{96,128},{128,160},{160,192},{192,224},{224... | collective-permute-start | bytes 98312 | tf_op jit(solution)/shard_map/ppermute | solution.py:262
  122.4 3.4 %collective-permute-start.4 = (bf16[64,256]{1,0:T(8,128)(2,1)S(1)}, bf16[64,256]{1,0:T(8,128)(2,1)S(1)}, u32[]{:S(2)}, u32[]{:S(2)}) collective-permute-start(bf16[64,256]{1,0:T(8,128)(2,1)S(1)} %get-tuple-element.43), channel_id=1, source_target_pairs={{0,32},{32,64},{64,96},{96,128},{128,160},{160,192},{192,224},{224... | collective-permute-start | bytes 98312 | tf_op jit(solution)/shard_map/ppermute | solution.py:262
  175.3 3.4 %collective-permute-start.5 = (bf16[64,256]{1,0:T(8,128)(2,1)S(1)}, bf16[64,256]{1,0:T(8,128)(2,1)S(1)}, u32[]{:S(2)}, u32[]{:S(2)}) collective-permute-start(bf16[64,256]{1,0:T(8,128)(2,1)S(1)} %get-tuple-element.46), channel_id=1, source_target_pairs={{0,32},{32,64},{64,96},{96,128},{128,160},{160,192},{192,224},{224... | collective-permute-start | bytes 98312 | tf_op jit(solution)/shard_map/ppermute | solution.py:262

commit v6 on v5

--- a/solution.py
+++ b/solution.py
@@ -13,13 +13,15 @@
 EXTRA = 16
 
 
-def call(body, out, operands, name, smem=0):
+def call(body, out, operands, name, smem=0, after=0):
     vmem = pl.BlockSpec(memory_space=pltpu.VMEM)
     scalars = pl.BlockSpec(memory_space=pltpu.SMEM)
     return pl.pallas_call(
         body,
         out_shape=out,
-        in_specs=[scalars] * smem + [vmem] * (len(operands) - smem),
+        in_specs=[scalars] * smem
+        + [vmem] * (len(operands) - smem - after)
+        + [pl.BlockSpec(memory_space=pl.ANY)] * after,
         out_specs=jax.tree.map(lambda _: vmem, out),
         compiler_params=pltpu.CompilerParams(vmem_limit_bytes=16 * 1024 * 1024),
         name=name,
@@ -67,20 +69,27 @@
     return got.reshape((-1, got.shape[-1]))
 
 
-def deal_kernel(x_ref, gain_ref, *refs):
-    matrices, blocks = refs[: len(refs) // 2], refs[len(refs) // 2 :]
-    groups = len(blocks)
-    width = matrices[0].shape[0]
-    rows = blocks[0].shape[1]
+def scaled(matrix_ref, gain_ref, at):
+    return (matrix_ref[:, at].astype(jnp.float32) * gain_ref[:, at]).astype(matrix_ref.dtype)
+
+
+def deal_kernel(x_ref, gain_ref, value_ref, in_ref, out_ref, _, *blocks):
+    width, rows = value_ref.shape[0], blocks[0].shape[1]
     for step, block in enumerate(blocks):
-        start = lax.rem(x_ref[0] + step, groups) * rows
+        start = lax.rem(x_ref[0] + step, len(blocks)) * rows
         at = pl.ds(pl.multiple_of(start, rows), rows)
-        gain = gain_ref[:, at]
-        for m, matrix in enumerate(matrices):
-            w = matrix[:, at]
-            if m < len(matrices) - 1:
-                w = (w.astype(jnp.float32) * gain).astype(w.dtype)
-            block[m * width : (m + 1) * width] = w
+        for m, matrix in enumerate((value_ref, in_ref, out_ref)):
+            block[m * width : (m + 1) * width] = scaled(matrix, gain_ref, at)
+
+
+def pack_kernel(part_ref, emit_ref, _, out_ref):
+    groups, size, positions = out_ref.shape
+    rows, width = part_ref.shape[0], emit_ref.shape[0]
+    for x in range(groups):
+        out_ref[x, :rows] = part_ref[...]
+        for piece in range((size - rows) // width):
+            at = x * rows + piece * positions
+            out_ref[x, rows + piece * width : rows + (piece + 1) * width] = emit_ref[:, at : at + positions]
 
 
 def history_kernel(section_ref, lengths_ref, skip_ref, filt_ref, held_ref, *rest):
@@ -123,30 +132,26 @@
     extra = jnp.where(at == 0, upper, jnp.where(at == 1, square - upper, 0.0)).astype(out_ref.dtype)
     for step, block in enumerate(blocks):
         x = lax.rem(x_ref[0] + groups - step, groups)
-        term = jnp.dot(block[:rows], u, preferred_element_type=jnp.float32)
+        term = jnp.dot(block[...], u, preferred_element_type=jnp.float32)
         out_ref[x, :rows] = term.astype(out_ref.dtype)
         out_ref[x, rows:] = extra
 
 
-def mix_kernel(tick, past, stored, features, live_ref, terms_ref, fwd_ref, inv_ref, filt_ref, *rest):
-    count = past + (stored is not None)
-    lagged, mixed_ref, spec_ref = rest[:count], rest[count], rest[count + 1 :]
+def mix_of(gates, square, live, fwd_ref, inv_ref, filt_ref, lagged, stored, mixed_ref, spec_ref):
     copies, width, _ = mixed_ref.shape
     half = fwd_ref.shape[1] // 2
-    terms = jnp.sum(terms_ref[...].astype(jnp.float32), axis=0)
-    square = terms[3 * width : 3 * width + 1] + terms[3 * width + 1 : 3 * width + 2]
-    gates = terms[: 3 * width] * lax.rsqrt(square * (1.0 / features) + 1e-06)
-    driven = jnp.where(live_ref[tick] > 0.0, gates[width : 2 * width] * gates[:width], 0.0)
+    gates = gates * lax.rsqrt(square + 1e-06)
+    driven = jnp.where(live > 0.0, gates[width : 2 * width] * gates[:width], 0.0)
     spectrum = jnp.dot(driven.astype(jnp.bfloat16), fwd_ref[...], preferred_element_type=jnp.float32)
     spectrum = spectrum[:, :half], spectrum[:, half:]
     for ref in spec_ref:
         ref[0], ref[1] = spectrum
     real, imag = times(filt_ref[0], spectrum)
-    for lag in range(1, past + 1):
-        more = times(filt_ref[lag], lagged[lag - 1][...])
+    for lag, ref in enumerate(lagged, 1):
+        more = times(filt_ref[lag], ref[...])
         real, imag = real + more[0], imag + more[1]
     if stored is not None:
-        more = lagged[-1][stored].astype(jnp.float32)
+        more = stored.astype(jnp.float32)
         real, imag = real + more[0], imag + more[1]
     packed = jnp.concatenate([real, imag], axis=1).astype(jnp.bfloat16)
     conv = jnp.dot(packed, inv_ref[...], preferred_element_type=jnp.float32)
@@ -155,14 +160,45 @@
         mixed_ref[y] = mixed
 
 
-def emit_terms_kernel(x_ref, mixed_ref, *refs):
-    blocks, out_ref = refs[:-1], refs[-1]
-    groups, rows, _ = out_ref.shape
-    mixed = mixed_ref[...]
-    for step, block in enumerate(blocks):
-        x = lax.rem(x_ref[0] + groups - step, groups)
-        w = block[block.shape[0] - rows :]
-        out_ref[x] = jnp.dot(w, mixed, preferred_element_type=jnp.float32).astype(out_ref.dtype)
+def first_mix_kernel(live_ref, packed_ref, gain_ref, value_ref, in_ref, out_ref, *rest):
+    fwd_ref, inv_ref, filt_ref, known_ref, mixed_ref, spec_ref, emit_ref = rest
+    groups = packed_ref.shape[0]
+    rows = value_ref.shape[1] // groups
+    width = value_ref.shape[0]
+    gates = square = 0.0
+    for x in range(groups):
+        u = packed_ref[x, :rows]
+        at = pl.ds(x * rows, rows)
+        w = jnp.concatenate([scaled(m, gain_ref, at) for m in (value_ref, in_ref, out_ref)], axis=0)
+        gates += jnp.dot(w, u, preferred_element_type=jnp.float32)
+        wide = u.astype(jnp.float32)
+        square += jnp.sum(wide * wide, axis=0, keepdims=True)
+        for piece in range(emit_ref.shape[1]):
+            emit_ref[x, piece] = packed_ref[x, rows + piece * width : rows + (piece + 1) * width]
+    square = square * (1.0 / (groups * rows))
+    mix_of(gates, square, live_ref[0], fwd_ref, inv_ref, filt_ref, (), known_ref[0], mixed_ref, (spec_ref,))
+
+
+def mix_kernel(tick, past, stored, features, live_ref, terms_ref, fwd_ref, inv_ref, filt_ref, *rest):
+    count = past + (stored is not None)
+    lagged, mixed_ref, spec_ref = rest[:count], rest[count], rest[count + 1 :]
+    width = mixed_ref.shape[1]
+    terms = jnp.sum(terms_ref[...].astype(jnp.float32), axis=0)
+    square = (terms[3 * width : 3 * width + 1] + terms[3 * width + 1 : 3 * width + 2]) * (1.0 / features)
+    known = None if stored is None else lagged[-1][stored]
+    mix_of(
+        terms[: 3 * width], square, live_ref[tick], fwd_ref, inv_ref, filt_ref, lagged[:past], known, mixed_ref, spec_ref
+    )
+
+
+def emit_terms_kernel(w_ref, mixed_ref, out_ref):
+    groups, pieces, _, size = w_ref.shape
+    for x in range(groups):
+        term = 0.0
+        for piece in range(pieces):
+            rows = mixed_ref[piece * size : (piece + 1) * size]
+            term += jnp.dot(w_ref[x, piece], rows, preferred_element_type=jnp.float32)
+        out_ref[x] = term.astype(out_ref.dtype)
 
 
 def total_of(terms_ref, own_ref):
@@ -170,7 +206,8 @@
     return total.astype(own_ref.dtype)
 
 
-def add_and_send_kernel(tick, layers, section_ref, terms_ref, own_ref, fresh_ref, out_ref, send_ref):
+def add_and_send_kernel(tick, layers, section_ref, terms_ref, own_ref, fresh_ref, *rest):
+    out_ref, send_ref = rest[-2:]
     out = total_of(terms_ref, own_ref)
     out_ref[...] = out
     send_ref[...] = jnp.where(section_ref[0] == layers - 1, fresh_ref[tick], out)
@@ -199,17 +236,7 @@
 
     own = feeds[0].T
     part = gather_rows(jnp.broadcast_to(own[None], (copies,) + own.shape))
-    dealt = call(
-        deal_kernel,
-        [bf16((4 * width, rows))] * groups,
-        [x, gain] + [w[0].T for w in (value_w, in_w, out_w, emit_w)],
-        "deal",
-        smem=1,
-    )
-    weights = [dealt[0]] + [None] * (groups - 1)
-    for step in sorted(range(1, groups), key=lambda step: -min(step, groups - step)):
-        pairs = [(i, (i + step) % groups) for i in range(groups)]
-        weights[step] = lax.ppermute(dealt[step], "x", pairs)
+    gate_w = [w[0].T for w in (value_w, in_w, out_w)]
     half = filters.shape[-1] // 2
     passed = [jnp.asarray(t) for t in tables(positions, 2 * half)] + [newcomers.transpose(0, 2, 1), own]
     live, known, filters, forward, inverse, fresh, own = call(
@@ -221,42 +248,56 @@
         smem=2,
     )
 
+    size = rows + width * rows // positions
+    packed = swap(call(pack_kernel, bf16((groups, size, positions)), [part, emit_w[0].T, live], "pack"), "x")
+    mixed, spectrum, emit_rows = call(
+        first_mix_kernel,
+        [bf16((copies, width, positions)), f32((2, width, half)), bf16((groups, rows // positions, width, positions))],
+        [live, packed, gain] + gate_w + [forward, inverse, filters, known],
+        "first_mix",
+    )
+    spectra = [spectrum]
+    dealt = call(
+        deal_kernel, [bf16((3 * width, rows))] * groups, [x, gain] + gate_w + [spectrum], "deal", smem=1
+    )
+    weights = [dealt[0]] + [
+        lax.ppermute(dealt[step], "x", [(i, (i + step) % groups) for i in range(groups)]) for step in range(1, groups)
+    ]
+
     ring = [(i, (i + 1) % layers) for i in range(layers)]
-    outputs, spectra = [], []
+    outputs = []
     for tick in range(ticks):
+        if tick > 0:
+            terms = call(
+                gate_terms_kernel,
+                bf16((groups, 3 * width + EXTRA, positions)),
+                [x, part] + weights,
+                "gate_terms",
+                smem=1,
+            )
+            terms = swap(terms, "x")
+            past = min(tick, blocks)
+            stored = tick if tick < blocks else None
+            lagged = spectra[::-1][:past] + ([known] if stored is not None else [])
+            mixed, *spectrum = call(
+                functools.partial(mix_kernel, tick, past, stored, features),
+                [bf16((copies, width, positions))] + [f32((2, width, half))] * (tick < ticks - 1),
+                [live, terms, forward, inverse, filters] + lagged,
+                "mix",
+            )
+            spectra += spectrum
         terms = call(
-            gate_terms_kernel,
-            bf16((groups, 3 * width + EXTRA, positions)),
-            [x, part] + weights + ([live] if tick == 0 else []),
-            "gate_terms",
-            smem=1,
-        )
-        terms = swap(terms, "x")
-        past = min(tick, blocks)
-        stored = tick if tick < blocks else None
-        lagged = spectra[::-1][:past] + ([known] if stored is not None else [])
-        mixed, *spectrum = call(
-            functools.partial(mix_kernel, tick, past, stored, features),
-            [bf16((copies, width, positions))] + [f32((2, width, half))] * (tick < ticks - 1),
-            [live, terms, forward, inverse, filters] + lagged,
-            "mix",
-        )
-        spectra += spectrum
-        terms = call(
-            emit_terms_kernel,
-            bf16((groups, width, positions)),
-            [x, gather_rows(mixed)] + weights,
-            "emit_terms",
-            smem=1,
+            emit_terms_kernel, bf16((groups, width, positions)), [emit_rows, gather_rows(mixed)], "emit_terms"
         )
         terms = swap(terms, "x")
         if tick < ticks - 1:
             out, send = call(
                 functools.partial(add_and_send_kernel, tick, layers),
                 [bf16(own.shape)] * 2,
-                [place, terms, own, fresh],
+                [place, terms, own, fresh] + (weights if tick == 0 else []),
                 "add",
                 smem=1,
+                after=len(weights) if tick == 0 else 0,
             )
             outputs.append(out)
             own = lax.ppermute(send, SECTION, ring)

time: 231 us -> 229 us (level)
  blocking collectives: 184 us -> 166 us
  waiting for transfers between devices: 11.4 us -> 20.6 us
  starting transfers between devices: 18.8 us -> 24.1 us
    all_to_all x15 -> x13, blocking collectives: 184 us -> 166 us  [swap(): return lax.all_to_all(blocks, axis, 0, 0, tiled=True)]
    all_to_all x1 -> x3, waiting for transfers between devices: 0.01 us -> 9.72 us  [swap(): return lax.all_to_all(blocks, axis, 0, 0, tiled=True)]
    all_to_all x1 -> x3, starting transfers between devices: 7.23 us -> 14.9 us  [swap(): return lax.all_to_all(blocks, axis, 0, 0, tiled=True)]
    ppermute x3, starting transfers between devices: 11.5 us -> 9.16 us  [local(): lax.ppermute(dealt[step], 'x', [(i, (i + step) % groups) for i in range(g...]
    unnamed x26 -> x24, local copies, waits for them, and re-layouts: 6.32 us -> 5.45 us
  transfers between devices with their start and end apart: 7 -> 9, of which waited for: 4 -> 7; matrix products, arithmetic and copies ran while one was open for 0% -> 0% of each run, Pallas kernels for 1% -> 1%
where the time goes in v6:
time: 229 us; the launch traced here: 228 us
  blocking collectives  166 us (72%)
  starting transfers between devices  24.1 us (11%)
  waiting for transfers between devices  20.6 us (9%)
  Pallas kernels  8.72 us (4%)
  local copies, waits for them, and re-layouts  7.8 us (3%)
    all_to_all x13, blocking collectives, swap(): return lax.all_to_all(blocks, axis, 0, 0, tiled=True)  166 us
    all_to_all x3, starting transfers between devices, swap(): return lax.all_to_all(blocks, axis, 0, 0, tiled=True)  14.9 us
    ppermute x3, waiting for transfers between devices, local(): own = lax.ppermute(send, SECTION, ring)  9.98 us
    all_to_all x3, waiting for transfers between devices, swap(): return lax.all_to_all(blocks, axis, 0, 0, tiled=True)  9.72 us
    ppermute x3, starting transfers between devices, local(): lax.ppermute(dealt[step], 'x', [(i, (i + step) % groups) for i in range(g...  9.16 us
    pallas_call x18, Pallas kernels, call(): pl.pallas_call(body, out_shape=out, in_specs=[scalars] * smem + [vmem] *...  8.72 us
    unnamed x24, local copies, waits for them, and re-layouts  5.45 us
  transfers between devices with their start and end apart: 9, of which 7 were waited for; matrix products, arithmetic and copies ran while one was open for 0% of the time, Pallas kernels for 1%

profile of v6, /device:TPU:64, one launch (start us, length us, event | category | flops | bytes accessed | tf_op | source)
XLA Modules:
  0.0 227.8 jit_solution(13314243075538739524)
XLA Ops:
  1.6 7.1 %all-to-all-start = ((bf16[8,64,256]{2,1,0:T(8,128)(2,1)}), bf16[8,64,256]{2,1,0:T(8,128)(2,1)S(1)}, u32[]{:S(2)}, u32[]{:S(2)}) async-start(bf16[8,64,256]{2,1,0:T(8,128)(2,1)} %broadcast_in_dim.15), calls=%async_computation | async-start | bytes 524288 | tf_op jit(solution)/shard_map/all_to_all | solution.py:64
  16.4 4.1 %all-to-all-done = bf16[8,64,256]{2,1,0:T(8,128)(2,1)S(1)} async-done(((bf16[8,64,256]{2,1,0:T(8,128)(2,1)}), bf16[8,64,256]{2,1,0:T(8,128)(2,1)S(1)}, u32[]{:S(2)}, u32[]{:S(2)}) %all-to-all-start) | async-done | bytes 262176 | tf_op jit(solution)/shard_map/all_to_all | solution.py:64
  20.7 20.3 %all_to_all.80.packed_ref = bf16[4,640,256]{2,1,0:T(8,128)(2,1)S(1)} all-to-all(bf16[4,640,256]{2,1,0:T(8,128)(2,1)S(1)} %pack.1), channel_id=1, replica_groups=mesh['z'=8,'core'=2,'x'=4,'y'=8] {'x'}, dimensions={0} | all-to-all | bytes 2621440 | tf_op jit(solution)/shard_map/all_to_all | solution.py:64
  42.5 4.4 %all-to-all-start.2 = ((bf16[8,64,256]{2,1,0:T(8,128)(2,1)}), bf16[8,64,256]{2,1,0:T(8,128)(2,1)S(1)}, u32[]{:S(2)}, u32[]{:S(2)}) async-start(bf16[8,64,256]{2,1,0:T(8,128)(2,1)} %get-tuple-element.35), calls=%async_computation.2 | async-start | bytes 524288 | tf_op jit(solution)/shard_map/all_to_all | solution.py:64
  47.6 2.5 %collective-permute-start = (bf16[192,512]{1,0:T(8,128)(2,1)}, bf16[192,512]{1,0:T(8,128)(2,1)S(1)}, u32[]{:S(2)}, u32[]{:S(2)}) collective-permute-start(bf16[192,512]{1,0:T(8,128)(2,1)} %get-tuple-element.40), channel_id=1, source_target_pairs={{0,8},{8,16},{16,24},{24,0},{1,9},{9,17},{17,25},{25,1},{2,10},{10... | collective-permute-start | bytes 589832 | tf_op jit(solution)/shard_map/ppermute | solution.py:264
  50.1 4.0 %collective-permute-start.1 = (bf16[192,512]{1,0:T(8,128)(2,1)S(1)}, bf16[192,512]{1,0:T(8,128)(2,1)S(1)}, u32[]{:S(2)}, u32[]{:S(2)}) collective-permute-start(bf16[192,512]{1,0:T(8,128)(2,1)S(1)} %get-tuple-element.41), channel_id=1, source_target_pairs={{0,16},{8,24},{16,0},{24,8},{1,17},{9,25},{17,1},{25,9},{2,18},{10... | collective-permute-start | bytes 589832 | tf_op jit(solution)/shard_map/ppermute | solution.py:264
  54.1 2.7 %collective-permute-start.2 = (bf16[192,512]{1,0:T(8,128)(2,1)S(1)}, bf16[192,512]{1,0:T(8,128)(2,1)S(1)}, u32[]{:S(2)}, u32[]{:S(2)}) collective-permute-start(bf16[192,512]{1,0:T(8,128)(2,1)S(1)} %get-tuple-element.42), channel_id=1, source_target_pairs={{0,24},{8,0},{16,8},{24,16},{1,25},{9,1},{17,9},{25,17},{2,26},{10... | collective-permute-start | bytes 589832 | tf_op jit(solution)/shard_map/ppermute | solution.py:264
  58.3 3.4 %all-to-all-start.3 = ((bf16[4,64,256]{2,1,0:T(8,128)(2,1)}), bf16[4,64,256]{2,1,0:T(8,128)(2,1)S(1)}, u32[]{:S(2)}, u32[]{:S(2)}) async-start(bf16[4,64,256]{2,1,0:T(8,128)(2,1)} %emit_terms.4), calls=%async_computation.3 | async-start | bytes 262144 | tf_op jit(solution)/shard_map/all_to_all | solution.py:64
  62.7 5.0 %all-to-all-done.3.terms_ref = bf16[4,64,256]{2,1,0:T(8,128)(2,1)S(1)} async-done(((bf16[4,64,256]{2,1,0:T(8,128)(2,1)}), bf16[4,64,256]{2,1,0:T(8,128)(2,1)S(1)}, u32[]{:S(2)}, u32[]{:S(2)}) %all-to-all-start.3) | async-done | bytes 131104 | tf_op jit(solution)/shard_map/all_to_all | solution.py:64
  67.8 3.3 %collective-permute-done.3.own_ref = bf16[64,256]{1,0:T(8,128)(2,1)S(1)} collective-permute-done((bf16[64,256]{1,0:T(8,128)(2,1)S(1)}, bf16[64,256]{1,0:T(8,128)(2,1)S(1)}, u32[]{:S(2)}, u32[]{:S(2)}) %collective-permute-start.3) | collective-permute-done | bytes 32800 | tf_op jit(solution)/shard_map/ppermute | solution.py:303
  71.1 19.2 %all_to_all.81 = bf16[8,64,256]{2,1,0:T(8,128)(2,1)S(1)} all-to-all(bf16[8,64,256]{2,1,0:T(8,128)(2,1)S(1)} %broadcast_in_dim.17), channel_id=1, replica_groups=mesh['z'=8,'core'=2,'x'=4,'y'=8] {'y'}, dimensions={0} | all-to-all | bytes 524288 | tf_op jit(solution)/shard_map/all_to_all | solution.py:64
  90.7 10.1 %all_to_all.82.terms_ref = bf16[4,208,256]{2,1,0:T(8,128)(2,1)S(1)} all-to-all(bf16[4,208,256]{2,1,0:T(8,128)(2,1)S(1)} %gate_terms.3), channel_id=1, replica_groups=mesh['z'=8,'core'=2,'x'=4,'y'=8] {'x'}, dimensions={0} | all-to-all | bytes 851968 | tf_op jit(solution)/shard_map/all_to_all | solution.py:64
  101.2 12.9 %all_to_all.83 = bf16[8,64,256]{2,1,0:T(8,128)(2,1)S(1)} all-to-all(bf16[8,64,256]{2,1,0:T(8,128)(2,1)S(1)} %get-tuple-element.44), channel_id=1, replica_groups=mesh['z'=8,'core'=2,'x'=4,'y'=8] {'y'}, dimensions={0} | all-to-all | bytes 524288 | tf_op jit(solution)/shard_map/all_to_all | solution.py:64
  114.4 8.4 %all_to_all.84.terms_ref = bf16[4,64,256]{2,1,0:T(8,128)(2,1)S(1)} all-to-all(bf16[4,64,256]{2,1,0:T(8,128)(2,1)S(1)} %emit_terms.5), channel_id=1, replica_groups=mesh['z'=8,'core'=2,'x'=4,'y'=8] {'x'}, dimensions={0} | all-to-all | bytes 262144 | tf_op jit(solution)/shard_map/all_to_all | solution.py:64
  122.8 3.3 %collective-permute-done.4.own_ref = bf16[64,256]{1,0:T(8,128)(2,1)S(1)} collective-permute-done((bf16[64,256]{1,0:T(8,128)(2,1)S(1)}, bf16[64,256]{1,0:T(8,128)(2,1)S(1)}, u32[]{:S(2)}, u32[]{:S(2)}) %collective-permute-start.4) | collective-permute-done | bytes 32800 | tf_op jit(solution)/shard_map/ppermute | solution.py:303
  126.2 14.9 %all_to_all.85 = bf16[8,64,256]{2,1,0:T(8,128)(2,1)S(1)} all-to-all(bf16[8,64,256]{2,1,0:T(8,128)(2,1)S(1)} %broadcast_in_dim.18), channel_id=1, replica_groups=mesh['z'=8,'core'=2,'x'=4,'y'=8] {'y'}, dimensions={0} | all-to-all | bytes 524288 | tf_op jit(solution)/shard_map/all_to_all | solution.py:64
  141.4 11.3 %all_to_all.86.terms_ref = bf16[4,208,256]{2,1,0:T(8,128)(2,1)S(1)} all-to-all(bf16[4,208,256]{2,1,0:T(8,128)(2,1)S(1)} %gate_terms.4), channel_id=1, replica_groups=mesh['z'=8,'core'=2,'x'=4,'y'=8] {'x'}, dimensions={0} | all-to-all | bytes 851968 | tf_op jit(solution)/shard_map/all_to_all | solution.py:64
  153.1 13.9 %all_to_all.87 = bf16[8,64,256]{2,1,0:T(8,128)(2,1)S(1)} all-to-all(bf16[8,64,256]{2,1,0:T(8,128)(2,1)S(1)} %get-tuple-element.47), channel_id=1, replica_groups=mesh['z'=8,'core'=2,'x'=4,'y'=8] {'y'}, dimensions={0} | all-to-all | bytes 524288 | tf_op jit(solution)/shard_map/all_to_all | solution.py:64
  167.3 8.4 %all_to_all.88.terms_ref = bf16[4,64,256]{2,1,0:T(8,128)(2,1)S(1)} all-to-all(bf16[4,64,256]{2,1,0:T(8,128)(2,1)S(1)} %emit_terms.6), channel_id=1, replica_groups=mesh['z'=8,'core'=2,'x'=4,'y'=8] {'x'}, dimensions={0} | all-to-all | bytes 262144 | tf_op jit(solution)/shard_map/all_to_all | solution.py:64
  175.7 3.3 %collective-permute-done.5.own_ref = bf16[64,256]{1,0:T(8,128)(2,1)S(1)} collective-permute-done((bf16[64,256]{1,0:T(8,128)(2,1)S(1)}, bf16[64,256]{1,0:T(8,128)(2,1)S(1)}, u32[]{:S(2)}, u32[]{:S(2)}) %collective-permute-start.5) | collective-permute-done | bytes 32800 | tf_op jit(solution)/shard_map/ppermute | solution.py:303
  179.1 14.7 %all_to_all.89 = bf16[8,64,256]{2,1,0:T(8,128)(2,1)S(1)} all-to-all(bf16[8,64,256]{2,1,0:T(8,128)(2,1)S(1)} %broadcast_in_dim.38), channel_id=1, replica_groups=mesh['z'=8,'core'=2,'x'=4,'y'=8] {'y'}, dimensions={0} | all-to-all | bytes 524288 | tf_op jit(solution)/shard_map/all_to_all | solution.py:64
  194.1 10.7 %all_to_all.90.terms_ref = bf16[4,208,256]{2,1,0:T(8,128)(2,1)S(1)} all-to-all(bf16[4,208,256]{2,1,0:T(8,128)(2,1)S(1)} %gate_terms.5), channel_id=1, replica_groups=mesh['z'=8,'core'=2,'x'=4,'y'=8] {'x'}, dimensions={0} | all-to-all | bytes 851968 | tf_op jit(solution)/shard_map/all_to_all | solution.py:64
  205.2 13.2 %all_to_all.91 = bf16[8,64,256]{2,1,0:T(8,128)(2,1)S(1)} all-to-all(bf16[8,64,256]{2,1,0:T(8,128)(2,1)S(1)} %mix.5), channel_id=1, replica_groups=mesh['z'=8,'core'=2,'x'=4,'y'=8] {'y'}, dimensions={0} | all-to-all | bytes 524288 | tf_op jit(solution)/shard_map/all_to_all | solution.py:64
  218.7 8.4 %all_to_all.92.terms_ref = bf16[4,64,256]{2,1,0:T(8,128)(2,1)S(1)} all-to-all(bf16[4,64,256]{2,1,0:T(8,128)(2,1)S(1)} %emit_terms.7), channel_id=1, replica_groups=mesh['z'=8,'core'=2,'x'=4,'y'=8] {'x'}, dimensions={0} | all-to-all | bytes 262144 | tf_op jit(solution)/shard_map/all_to_all | solution.py:64
  (54 shorter events, 18.1 us)
Async XLA Ops:
  0.0 9.4 %copy-start.4 = (f32[1,3,2,64,512]{4,3,2,1,0:T(8,128)S(1)}, f32[1,3,2,64,512]{4,3,2,1,0:T(8,128)}, u32[]{:S(2)}) copy-start(f32[1,3,2,64,512]{4,3,2,1,0:T(8,128)} %param.23) | copy-start | bytes 2359300
  1.6 19.0 %all-to-all-start = ((bf16[8,64,256]{2,1,0:T(8,128)(2,1)}), bf16[8,64,256]{2,1,0:T(8,128)(2,1)S(1)}, u32[]{:S(2)}, u32[]{:S(2)}) async-start(bf16[8,64,256]{2,1,0:T(8,128)(2,1)} %broadcast_in_dim.15), calls=%async_computation | async-start | bytes 524288 | tf_op jit(solution)/shard_map/all_to_all | solution.py:64
  9.4 1.2 copy-start.3
  10.6 0.9 copy-start.6
  11.6 0.9 copy-start.7
  12.5 0.8 copy-start.8
  13.3 0.9 copy-start.9
  14.2 0.7 copy-start.11
  14.8 5.7 %copy-start.5 = (bf16[1,2048,64]{1,2,0:T(8,128)(2,1)S(1)}, bf16[1,2048,64]{1,2,0:T(8,128)(2,1)}, u32[]{:S(2)}) copy-start(bf16[1,2048,64]{1,2,0:T(8,128)(2,1)} %param.20) | copy-start | bytes 786436
  20.6 20.4 %copy-start = (bf16[1,2048,64]{1,2,0:T(8,128)(2,1)S(1)}, bf16[1,2048,64]{1,2,0:T(8,128)(2,1)}, u32[]{:S(2)}) copy-start(bf16[1,2048,64]{1,2,0:T(8,128)(2,1)} %param.17) | copy-start | bytes 786436
  20.6 20.4 %copy-start.1 = (bf16[1,2048,64]{1,2,0:T(8,128)(2,1)S(1)}, bf16[1,2048,64]{1,2,0:T(8,128)(2,1)}, u32[]{:S(2)}) copy-start(bf16[1,2048,64]{1,2,0:T(8,128)(2,1)} %param.18) | copy-start | bytes 786436
  20.6 20.4 %copy-start.2 = (bf16[1,2048,64]{1,2,0:T(8,128)(2,1)S(1)}, bf16[1,2048,64]{1,2,0:T(8,128)(2,1)}, u32[]{:S(2)}) copy-start(bf16[1,2048,64]{1,2,0:T(8,128)(2,1)} %param.19) | copy-start | bytes 786436
  20.7 20.4 %copy-start.10 = (f32[1,2048]{1,0:T(1,128)S(1)}, f32[1,2048]{1,0:T(1,128)}, u32[]{:S(2)}) copy-start(f32[1,2048]{1,0:T(1,128)} %gain_ref.3) | copy-start | bytes 24580
  42.5 14.8 %all-to-all-start.2 = ((bf16[8,64,256]{2,1,0:T(8,128)(2,1)}), bf16[8,64,256]{2,1,0:T(8,128)(2,1)S(1)}, u32[]{:S(2)}, u32[]{:S(2)}) async-start(bf16[8,64,256]{2,1,0:T(8,128)(2,1)} %get-tuple-element.35), calls=%async_computation.2 | async-start | bytes 524288 | tf_op jit(solution)/shard_map/all_to_all | solution.py:64
  47.6 14.1 %collective-permute-start = (bf16[192,512]{1,0:T(8,128)(2,1)}, bf16[192,512]{1,0:T(8,128)(2,1)S(1)}, u32[]{:S(2)}, u32[]{:S(2)}) collective-permute-start(bf16[192,512]{1,0:T(8,128)(2,1)} %get-tuple-element.40), channel_id=1, source_target_pairs={{0,8},{8,16},{16,24},{24,0},{1,9},{9,17},{17,25},{25,1},{2,10},{10... | collective-permute-start | bytes 589832 | tf_op jit(solution)/shard_map/ppermute | solution.py:264
  50.1 11.7 %collective-permute-start.1 = (bf16[192,512]{1,0:T(8,128)(2,1)S(1)}, bf16[192,512]{1,0:T(8,128)(2,1)S(1)}, u32[]{:S(2)}, u32[]{:S(2)}) collective-permute-start(bf16[192,512]{1,0:T(8,128)(2,1)S(1)} %get-tuple-element.41), channel_id=1, source_target_pairs={{0,16},{8,24},{16,0},{24,8},{1,17},{9,25},{17,1},{25,9},{2,18},{10... | collective-permute-start | bytes 589832 | tf_op jit(solution)/shard_map/ppermute | solution.py:264
  54.1 8.6 %collective-permute-start.2 = (bf16[192,512]{1,0:T(8,128)(2,1)S(1)}, bf16[192,512]{1,0:T(8,128)(2,1)S(1)}, u32[]{:S(2)}, u32[]{:S(2)}) collective-permute-start(bf16[192,512]{1,0:T(8,128)(2,1)S(1)} %get-tuple-element.42), channel_id=1, source_target_pairs={{0,24},{8,0},{16,8},{24,16},{1,25},{9,1},{17,9},{25,17},{2,26},{10... | collective-permute-start | bytes 589832 | tf_op jit(solution)/shard_map/ppermute | solution.py:264
  58.3 9.4 %all-to-all-start.3 = ((bf16[4,64,256]{2,1,0:T(8,128)(2,1)}), bf16[4,64,256]{2,1,0:T(8,128)(2,1)S(1)}, u32[]{:S(2)}, u32[]{:S(2)}) async-start(bf16[4,64,256]{2,1,0:T(8,128)(2,1)} %emit_terms.4), calls=%async_computation.3 | async-start | bytes 262144 | tf_op jit(solution)/shard_map/all_to_all | solution.py:64
  67.7 3.4 %collective-permute-start.3 = (bf16[64,256]{1,0:T(8,128)(2,1)S(1)}, bf16[64,256]{1,0:T(8,128)(2,1)S(1)}, u32[]{:S(2)}, u32[]{:S(2)}) collective-permute-start(bf16[64,256]{1,0:T(8,128)(2,1)S(1)} %get-tuple-element.43), channel_id=1, source_target_pairs={{0,32},{32,64},{64,96},{96,128},{128,160},{160,192},{192,224},{224... | collective-permute-start | bytes 98312 | tf_op jit(solution)/shard_map/ppermute | solution.py:303
  122.8 3.4 %collective-permute-start.4 = (bf16[64,256]{1,0:T(8,128)(2,1)S(1)}, bf16[64,256]{1,0:T(8,128)(2,1)S(1)}, u32[]{:S(2)}, u32[]{:S(2)}) collective-permute-start(bf16[64,256]{1,0:T(8,128)(2,1)S(1)} %get-tuple-element.45), channel_id=1, source_target_pairs={{0,32},{32,64},{64,96},{96,128},{128,160},{160,192},{192,224},{224... | collective-permute-start | bytes 98312 | tf_op jit(solution)/shard_map/ppermute | solution.py:303
  175.7 3.4 %collective-permute-start.5 = (bf16[64,256]{1,0:T(8,128)(2,1)S(1)}, bf16[64,256]{1,0:T(8,128)(2,1)S(1)}, u32[]{:S(2)}, u32[]{:S(2)}) collective-permute-start(bf16[64,256]{1,0:T(8,128)(2,1)S(1)} %get-tuple-element.48), channel_id=1, source_target_pairs={{0,32},{32,64},{64,96},{96,128},{128,160},{160,192},{192,224},{224... | collective-permute-start | bytes 98312 | tf_op jit(solution)/shard_map/ppermute | solution.py:303

commit v7 on v6

--- a/solution.py
+++ b/solution.py
@@ -36,7 +36,9 @@
     forward = np.concatenate([cos, sin], axis=1)
     weight = np.full((2 * half, 1), 2.0 / period)
     weight[0] = weight[half] = 1.0 / period
-    return forward.astype(jnp.bfloat16), (forward.T * weight).astype(jnp.bfloat16)
+    inverse = forward.T * weight
+    inverse = np.concatenate([inverse[:half], inverse[half:]], axis=1)
+    return np.concatenate([forward, inverse], axis=0).astype(jnp.bfloat16)
 
 
 def fold(full):
@@ -100,6 +102,9 @@
     for tick in range(ticks):
         length = lengths_ref[tick - section_ref[0] + layers - 1]
         live_ref[tick] = jnp.where(at < length, 1.0, 0.0)
+    width = skip_ref.shape[1]
+    diagonal = [lax.broadcasted_iota(jnp.int32, (width, width), axis) for axis in (0, 1)]
+    skip = jnp.sum(jnp.where(diagonal[0] == diagonal[1], skip_ref[...], 0.0), axis=1, keepdims=True)
     blocks = held_ref.shape[0]
     for tick in range(blocks):
         real = imag = 0.0
@@ -112,8 +117,8 @@
     for lag in range(blocks + 1):
         real, imag = fold(filt_ref[lag])
         if lag == 0:
-            real += skip_ref[...]
-            imag += jnp.where(lax.broadcasted_iota(jnp.int32, imag.shape, 1) == 0, skip_ref[...], 0.0)
+            real += skip
+            imag += jnp.where(lax.broadcasted_iota(jnp.int32, imag.shape, 1) == 0, skip, 0.0)
         filt_out[lag, 0], filt_out[lag, 1] = real, imag
     for source, target in zip(passed, handed, strict=True):
         target[...] = source[...]
@@ -137,12 +142,12 @@
         out_ref[x, rows:] = extra
 
 
-def mix_of(gates, square, live, fwd_ref, inv_ref, filt_ref, lagged, stored, mixed_ref, spec_ref):
-    copies, width, _ = mixed_ref.shape
-    half = fwd_ref.shape[1] // 2
+def mix_of(gates, square, live, table_ref, filt_ref, lagged, stored, mixed_ref, spec_ref):
+    copies, width, positions = mixed_ref.shape
+    half = table_ref.shape[1] // 2
     gates = gates * lax.rsqrt(square + 1e-06)
     driven = jnp.where(live > 0.0, gates[width : 2 * width] * gates[:width], 0.0)
-    spectrum = jnp.dot(driven.astype(jnp.bfloat16), fwd_ref[...], preferred_element_type=jnp.float32)
+    spectrum = jnp.dot(driven.astype(jnp.bfloat16), table_ref[:positions], preferred_element_type=jnp.float32)
     spectrum = spectrum[:, :half], spectrum[:, half:]
     for ref in spec_ref:
         ref[0], ref[1] = spectrum
@@ -153,15 +158,16 @@
     if stored is not None:
         more = stored.astype(jnp.float32)
         real, imag = real + more[0], imag + more[1]
-    packed = jnp.concatenate([real, imag], axis=1).astype(jnp.bfloat16)
-    conv = jnp.dot(packed, inv_ref[...], preferred_element_type=jnp.float32)
+    inverse = table_ref[positions:]
+    conv = jnp.dot(real.astype(jnp.bfloat16), inverse[:, :positions], preferred_element_type=jnp.float32)
+    conv += jnp.dot(imag.astype(jnp.bfloat16), inverse[:, positions:], preferred_element_type=jnp.float32)
     mixed = (gates[2 * width :] * conv).astype(mixed_ref.dtype)
     for y in range(copies):
         mixed_ref[y] = mixed
 
 
 def first_mix_kernel(live_ref, packed_ref, gain_ref, value_ref, in_ref, out_ref, *rest):
-    fwd_ref, inv_ref, filt_ref, known_ref, mixed_ref, spec_ref, emit_ref = rest
+    table_ref, filt_ref, known_ref, mixed_ref, spec_ref, emit_ref = rest
     groups = packed_ref.shape[0]
     rows = value_ref.shape[1] // groups
     width = value_ref.shape[0]
@@ -176,10 +182,10 @@
         for piece in range(emit_ref.shape[1]):
             emit_ref[x, piece] = packed_ref[x, rows + piece * width : rows + (piece + 1) * width]
     square = square * (1.0 / (groups * rows))
-    mix_of(gates, square, live_ref[0], fwd_ref, inv_ref, filt_ref, (), known_ref[0], mixed_ref, (spec_ref,))
-
-
-def mix_kernel(tick, past, stored, features, live_ref, terms_ref, fwd_ref, inv_ref, filt_ref, *rest):
+    mix_of(gates, square, live_ref[0], table_ref, filt_ref, (), known_ref[0], mixed_ref, (spec_ref,))
+
+
+def mix_kernel(tick, past, stored, features, live_ref, terms_ref, table_ref, filt_ref, *rest):
     count = past + (stored is not None)
     lagged, mixed_ref, spec_ref = rest[:count], rest[count], rest[count + 1 :]
     width = mixed_ref.shape[1]
@@ -187,7 +193,7 @@
     square = (terms[3 * width : 3 * width + 1] + terms[3 * width + 1 : 3 * width + 2]) * (1.0 / features)
     known = None if stored is None else lagged[-1][stored]
     mix_of(
-        terms[: 3 * width], square, live_ref[tick], fwd_ref, inv_ref, filt_ref, lagged[:past], known, mixed_ref, spec_ref
+        terms[: 3 * width], square, live_ref[tick], table_ref, filt_ref, lagged[:past], known, mixed_ref, spec_ref
     )
 
 
@@ -238,12 +244,13 @@
     part = gather_rows(jnp.broadcast_to(own[None], (copies,) + own.shape))
     gate_w = [w[0].T for w in (value_w, in_w, out_w)]
     half = filters.shape[-1] // 2
-    passed = [jnp.asarray(t) for t in tables(positions, 2 * half)] + [newcomers.transpose(0, 2, 1), own]
-    live, known, filters, forward, inverse, fresh, own = call(
+    fresh = newcomers.transpose(0, 2, 1)
+    passed = [jnp.asarray(tables(positions, 2 * half)), fresh, own]
+    live, known, filters, table, fresh, own = call(
         history_kernel,
         [f32((ticks, 1, positions)), bf16((blocks, 2, width, half)), f32((blocks + 1, 2, width, half))]
         + [jax.ShapeDtypeStruct(t.shape, t.dtype) for t in passed],
-        [place, occupied, skip[0][:, None], filters[0], archive[0]] + passed,
+        [place, occupied, skip, filters[0], archive[0]] + passed,
         "history",
         smem=2,
     )
@@ -253,7 +260,7 @@
     mixed, spectrum, emit_rows = call(
         first_mix_kernel,
         [bf16((copies, width, positions)), f32((2, width, half)), bf16((groups, rows // positions, width, positions))],
-        [live, packed, gain] + gate_w + [forward, inverse, filters, known],
+        [live, packed, gain] + gate_w + [table, filters, known],
         "first_mix",
     )
     spectra = [spectrum]
@@ -282,7 +289,7 @@
             mixed, *spectrum = call(
                 functools.partial(mix_kernel, tick, past, stored, features),
                 [bf16((copies, width, positions))] + [f32((2, width, half))] * (tick < ticks - 1),
-                [live, terms, forward, inverse, filters] + lagged,
+                [live, terms, table, filters] + lagged,
                 "mix",
             )
             spectra += spectrum

time: 229 us -> 228 us (level)
  the two profiles are of different devices: /device:TPU:64 before, /device:TPU:2 now
where the time goes in v7:
time: 228 us; the launch traced here: 227 us
  blocking collectives  162 us (71%)
  starting transfers between devices  25.2 us (11%)
  waiting for transfers between devices  24.3 us (11%)
  Pallas kernels  8.77 us (4%)
  local copies, waits for them, and re-layouts  6.86 us (3%)
    all_to_all x13, blocking collectives, swap(): return lax.all_to_all(blocks, axis, 0, 0, tiled=True)  162 us
    all_to_all x3, starting transfers between devices, swap(): return lax.all_to_all(blocks, axis, 0, 0, tiled=True)  15.4 us
    ppermute x3, waiting for transfers between devices, local(): own = lax.ppermute(send, SECTION, ring)  14.8 us
    ppermute x3, starting transfers between devices, local(): lax.ppermute(dealt[step], 'x', [(i, (i + step) % groups) for i in range(g...  9.8 us
    all_to_all x3, waiting for transfers between devices, swap(): return lax.all_to_all(blocks, axis, 0, 0, tiled=True)  9.14 us
    pallas_call x18, Pallas kernels, call(): pl.pallas_call(body, out_shape=out, in_specs=[scalars] * smem + [vmem] *...  8.77 us
    unnamed x24, local copies, waits for them, and re-layouts  5.25 us
  transfers between devices with their start and end apart: 9, of which 6 were waited for; matrix products, arithmetic and copies ran while one was open for 0% of the time, Pallas kernels for 1%

profile of v7, /device:TPU:2, one launch (start us, length us, event | category | flops | bytes accessed | tf_op | source)
XLA Modules:
  0.0 227.1 jit_solution(15986391632623282203)
XLA Ops:
  1.6 7.1 %all-to-all-start = ((bf16[8,64,256]{2,1,0:T(8,128)(2,1)}), bf16[8,64,256]{2,1,0:T(8,128)(2,1)S(1)}, u32[]{:S(2)}, u32[]{:S(2)}) async-start(bf16[8,64,256]{2,1,0:T(8,128)(2,1)} %broadcast_in_dim.15), calls=%async_computation | async-start | bytes 524288 | tf_op jit(solution)/shard_map/all_to_all | solution.py:66
  15.5 5.0 %all-to-all-done = bf16[8,64,256]{2,1,0:T(8,128)(2,1)S(1)} async-done(((bf16[8,64,256]{2,1,0:T(8,128)(2,1)}), bf16[8,64,256]{2,1,0:T(8,128)(2,1)S(1)}, u32[]{:S(2)}, u32[]{:S(2)}) %all-to-all-start) | async-done | bytes 262176 | tf_op jit(solution)/shard_map/all_to_all | solution.py:66
  20.7 19.4 %all_to_all.80.packed_ref = bf16[4,640,256]{2,1,0:T(8,128)(2,1)S(1)} all-to-all(bf16[4,640,256]{2,1,0:T(8,128)(2,1)S(1)} %pack.1), channel_id=1, replica_groups=mesh['z'=8,'core'=2,'x'=4,'y'=8] {'x'}, dimensions={0} | all-to-all | bytes 2621440 | tf_op jit(solution)/shard_map/all_to_all | solution.py:66
  41.6 3.5 %all-to-all-start.2 = ((bf16[8,64,256]{2,1,0:T(8,128)(2,1)}), bf16[8,64,256]{2,1,0:T(8,128)(2,1)S(1)}, u32[]{:S(2)}, u32[]{:S(2)}) async-start(bf16[8,64,256]{2,1,0:T(8,128)(2,1)} %get-tuple-element.33), calls=%async_computation.2 | async-start | bytes 524288 | tf_op jit(solution)/shard_map/all_to_all | solution.py:66
  45.8 2.1 collective-permute-start
  47.9 5.2 %collective-permute-start.1 = (bf16[192,512]{1,0:T(8,128)(2,1)S(1)}, bf16[192,512]{1,0:T(8,128)(2,1)S(1)}, u32[]{:S(2)}, u32[]{:S(2)}) collective-permute-start(bf16[192,512]{1,0:T(8,128)(2,1)S(1)} %get-tuple-element.39), channel_id=1, source_target_pairs={{0,16},{8,24},{16,0},{24,8},{1,17},{9,25},{17,1},{25,9},{2,18},{10... | collective-permute-start | bytes 589832 | tf_op jit(solution)/shard_map/ppermute | solution.py:271
  53.1 2.5 %collective-permute-start.2 = (bf16[192,512]{1,0:T(8,128)(2,1)S(1)}, bf16[192,512]{1,0:T(8,128)(2,1)S(1)}, u32[]{:S(2)}, u32[]{:S(2)}) collective-permute-start(bf16[192,512]{1,0:T(8,128)(2,1)S(1)} %get-tuple-element.40), channel_id=1, source_target_pairs={{0,24},{8,0},{16,8},{24,16},{1,25},{9,1},{17,9},{25,17},{2,26},{10... | collective-permute-start | bytes 589832 | tf_op jit(solution)/shard_map/ppermute | solution.py:271
  56.6 4.8 %all-to-all-start.3 = ((bf16[4,64,256]{2,1,0:T(8,128)(2,1)}), bf16[4,64,256]{2,1,0:T(8,128)(2,1)S(1)}, u32[]{:S(2)}, u32[]{:S(2)}) async-start(bf16[4,64,256]{2,1,0:T(8,128)(2,1)} %emit_terms.4), calls=%async_computation.3 | async-start | bytes 262144 | tf_op jit(solution)/shard_map/all_to_all | solution.py:66
  61.7 4.1 %all-to-all-done.3.terms_ref = bf16[4,64,256]{2,1,0:T(8,128)(2,1)S(1)} async-done(((bf16[4,64,256]{2,1,0:T(8,128)(2,1)}), bf16[4,64,256]{2,1,0:T(8,128)(2,1)S(1)}, u32[]{:S(2)}, u32[]{:S(2)}) %all-to-all-start.3) | async-done | bytes 131104 | tf_op jit(solution)/shard_map/all_to_all | solution.py:66
  65.9 5.7 %collective-permute-done.3.own_ref = bf16[64,256]{1,0:T(8,128)(2,1)S(1)} collective-permute-done((bf16[64,256]{1,0:T(8,128)(2,1)S(1)}, bf16[64,256]{1,0:T(8,128)(2,1)S(1)}, u32[]{:S(2)}, u32[]{:S(2)}) %collective-permute-start.3) | collective-permute-done | bytes 32800 | tf_op jit(solution)/shard_map/ppermute | solution.py:310
  71.7 17.2 %all_to_all.81 = bf16[8,64,256]{2,1,0:T(8,128)(2,1)S(1)} all-to-all(bf16[8,64,256]{2,1,0:T(8,128)(2,1)S(1)} %broadcast_in_dim.17), channel_id=1, replica_groups=mesh['z'=8,'core'=2,'x'=4,'y'=8] {'y'}, dimensions={0} | all-to-all | bytes 524288 | tf_op jit(solution)/shard_map/all_to_all | solution.py:66
  89.3 10.4 %all_to_all.82.terms_ref = bf16[4,208,256]{2,1,0:T(8,128)(2,1)S(1)} all-to-all(bf16[4,208,256]{2,1,0:T(8,128)(2,1)S(1)} %gate_terms.3), channel_id=1, replica_groups=mesh['z'=8,'core'=2,'x'=4,'y'=8] {'x'}, dimensions={0} | all-to-all | bytes 851968 | tf_op jit(solution)/shard_map/all_to_all | solution.py:66
  100.1 12.9 %all_to_all.83 = bf16[8,64,256]{2,1,0:T(8,128)(2,1)S(1)} all-to-all(bf16[8,64,256]{2,1,0:T(8,128)(2,1)S(1)} %get-tuple-element.42), channel_id=1, replica_groups=mesh['z'=8,'core'=2,'x'=4,'y'=8] {'y'}, dimensions={0} | all-to-all | bytes 524288 | tf_op jit(solution)/shard_map/all_to_all | solution.py:66
  113.3 8.4 %all_to_all.84.terms_ref = bf16[4,64,256]{2,1,0:T(8,128)(2,1)S(1)} all-to-all(bf16[4,64,256]{2,1,0:T(8,128)(2,1)S(1)} %emit_terms.5), channel_id=1, replica_groups=mesh['z'=8,'core'=2,'x'=4,'y'=8] {'x'}, dimensions={0} | all-to-all | bytes 262144 | tf_op jit(solution)/shard_map/all_to_all | solution.py:66
  121.7 4.5 %collective-permute-done.4.own_ref = bf16[64,256]{1,0:T(8,128)(2,1)S(1)} collective-permute-done((bf16[64,256]{1,0:T(8,128)(2,1)S(1)}, bf16[64,256]{1,0:T(8,128)(2,1)S(1)}, u32[]{:S(2)}, u32[]{:S(2)}) %collective-permute-start.4) | collective-permute-done | bytes 32800 | tf_op jit(solution)/shard_map/ppermute | solution.py:310
  126.3 13.0 %all_to_all.85 = bf16[8,64,256]{2,1,0:T(8,128)(2,1)S(1)} all-to-all(bf16[8,64,256]{2,1,0:T(8,128)(2,1)S(1)} %broadcast_in_dim.18), channel_id=1, replica_groups=mesh['z'=8,'core'=2,'x'=4,'y'=8] {'y'}, dimensions={0} | all-to-all | bytes 524288 | tf_op jit(solution)/shard_map/all_to_all | solution.py:66
  139.6 9.9 %all_to_all.86.terms_ref = bf16[4,208,256]{2,1,0:T(8,128)(2,1)S(1)} all-to-all(bf16[4,208,256]{2,1,0:T(8,128)(2,1)S(1)} %gate_terms.4), channel_id=1, replica_groups=mesh['z'=8,'core'=2,'x'=4,'y'=8] {'x'}, dimensions={0} | all-to-all | bytes 851968 | tf_op jit(solution)/shard_map/all_to_all | solution.py:66
  149.9 12.9 %all_to_all.87 = bf16[8,64,256]{2,1,0:T(8,128)(2,1)S(1)} all-to-all(bf16[8,64,256]{2,1,0:T(8,128)(2,1)S(1)} %get-tuple-element.45), channel_id=1, replica_groups=mesh['z'=8,'core'=2,'x'=4,'y'=8] {'y'}, dimensions={0} | all-to-all | bytes 524288 | tf_op jit(solution)/shard_map/all_to_all | solution.py:66
  163.1 8.4 %all_to_all.88.terms_ref = bf16[4,64,256]{2,1,0:T(8,128)(2,1)S(1)} all-to-all(bf16[4,64,256]{2,1,0:T(8,128)(2,1)S(1)} %emit_terms.6), channel_id=1, replica_groups=mesh['z'=8,'core'=2,'x'=4,'y'=8] {'x'}, dimensions={0} | all-to-all | bytes 262144 | tf_op jit(solution)/shard_map/all_to_all | solution.py:66
  171.5 4.5 %collective-permute-done.5.own_ref = bf16[64,256]{1,0:T(8,128)(2,1)S(1)} collective-permute-done((bf16[64,256]{1,0:T(8,128)(2,1)S(1)}, bf16[64,256]{1,0:T(8,128)(2,1)S(1)}, u32[]{:S(2)}, u32[]{:S(2)}) %collective-permute-start.5) | collective-permute-done | bytes 32800 | tf_op jit(solution)/shard_map/ppermute | solution.py:310
  176.1 15.7 %all_to_all.89 = bf16[8,64,256]{2,1,0:T(8,128)(2,1)S(1)} all-to-all(bf16[8,64,256]{2,1,0:T(8,128)(2,1)S(1)} %broadcast_in_dim.38), channel_id=1, replica_groups=mesh['z'=8,'core'=2,'x'=4,'y'=8] {'y'}, dimensions={0} | all-to-all | bytes 524288 | tf_op jit(solution)/shard_map/all_to_all | solution.py:66
  192.1 11.3 %all_to_all.90.terms_ref = bf16[4,208,256]{2,1,0:T(8,128)(2,1)S(1)} all-to-all(bf16[4,208,256]{2,1,0:T(8,128)(2,1)S(1)} %gate_terms.5), channel_id=1, replica_groups=mesh['z'=8,'core'=2,'x'=4,'y'=8] {'x'}, dimensions={0} | all-to-all | bytes 851968 | tf_op jit(solution)/shard_map/all_to_all | solution.py:66
  203.9 13.9 %all_to_all.91 = bf16[8,64,256]{2,1,0:T(8,128)(2,1)S(1)} all-to-all(bf16[8,64,256]{2,1,0:T(8,128)(2,1)S(1)} %mix.5), channel_id=1, replica_groups=mesh['z'=8,'core'=2,'x'=4,'y'=8] {'y'}, dimensions={0} | all-to-all | bytes 524288 | tf_op jit(solution)/shard_map/all_to_all | solution.py:66
  218.1 8.4 %all_to_all.92.terms_ref = bf16[4,64,256]{2,1,0:T(8,128)(2,1)S(1)} all-to-all(bf16[4,64,256]{2,1,0:T(8,128)(2,1)S(1)} %emit_terms.7), channel_id=1, replica_groups=mesh['z'=8,'core'=2,'x'=4,'y'=8] {'x'}, dimensions={0} | all-to-all | bytes 262144 | tf_op jit(solution)/shard_map/all_to_all | solution.py:66
  (53 shorter events, 16.1 us)
Async XLA Ops:
  0.0 8.7 %copy-start.4 = (f32[1,3,2,64,512]{4,3,2,1,0:T(8,128)S(1)}, f32[1,3,2,64,512]{4,3,2,1,0:T(8,128)}, u32[]{:S(2)}) copy-start(f32[1,3,2,64,512]{4,3,2,1,0:T(8,128)} %param.22) | copy-start | bytes 2359300
  1.6 19.0 %all-to-all-start = ((bf16[8,64,256]{2,1,0:T(8,128)(2,1)}), bf16[8,64,256]{2,1,0:T(8,128)(2,1)S(1)}, u32[]{:S(2)}, u32[]{:S(2)}) async-start(bf16[8,64,256]{2,1,0:T(8,128)(2,1)} %broadcast_in_dim.15), calls=%async_computation | async-start | bytes 524288 | tf_op jit(solution)/shard_map/all_to_all | solution.py:66
  8.7 1.2 copy-start
  9.9 1.0 copy-start.5
  10.9 0.8 copy-start.7
  11.7 0.9 copy-start.8
  12.6 0.7 copy-start.10
  13.2 0.7 copy-start.11
  13.9 6.6 %copy-start.6 = (bf16[1,2048,64]{1,2,0:T(8,128)(2,1)S(1)}, bf16[1,2048,64]{1,2,0:T(8,128)(2,1)}, u32[]{:S(2)}) copy-start(bf16[1,2048,64]{1,2,0:T(8,128)(2,1)} %param.19) | copy-start | bytes 786436
  20.6 19.5 %copy-start.1 = (bf16[1,2048,64]{1,2,0:T(8,128)(2,1)S(1)}, bf16[1,2048,64]{1,2,0:T(8,128)(2,1)}, u32[]{:S(2)}) copy-start(bf16[1,2048,64]{1,2,0:T(8,128)(2,1)} %param.16) | copy-start | bytes 786436
  20.6 19.5 %copy-start.2 = (bf16[1,2048,64]{1,2,0:T(8,128)(2,1)S(1)}, bf16[1,2048,64]{1,2,0:T(8,128)(2,1)}, u32[]{:S(2)}) copy-start(bf16[1,2048,64]{1,2,0:T(8,128)(2,1)} %param.17) | copy-start | bytes 786436
  20.6 19.4 %copy-start.3 = (bf16[1,2048,64]{1,2,0:T(8,128)(2,1)S(1)}, bf16[1,2048,64]{1,2,0:T(8,128)(2,1)}, u32[]{:S(2)}) copy-start(bf16[1,2048,64]{1,2,0:T(8,128)(2,1)} %param.18) | copy-start | bytes 786436
  20.7 19.4 %copy-start.9 = (f32[1,2048]{1,0:T(1,128)S(1)}, f32[1,2048]{1,0:T(1,128)}, u32[]{:S(2)}) copy-start(f32[1,2048]{1,0:T(1,128)} %gain_ref.3) | copy-start | bytes 24580
  41.6 14.0 %all-to-all-start.2 = ((bf16[8,64,256]{2,1,0:T(8,128)(2,1)}), bf16[8,64,256]{2,1,0:T(8,128)(2,1)S(1)}, u32[]{:S(2)}, u32[]{:S(2)}) async-start(bf16[8,64,256]{2,1,0:T(8,128)(2,1)} %get-tuple-element.33), calls=%async_computation.2 | async-start | bytes 524288 | tf_op jit(solution)/shard_map/all_to_all | solution.py:66
  45.8 15.6 %collective-permute-start = (bf16[192,512]{1,0:T(8,128)(2,1)}, bf16[192,512]{1,0:T(8,128)(2,1)S(1)}, u32[]{:S(2)}, u32[]{:S(2)}) collective-permute-start(bf16[192,512]{1,0:T(8,128)(2,1)} %get-tuple-element.38), channel_id=1, source_target_pairs={{0,8},{8,16},{16,24},{24,0},{1,9},{9,17},{17,25},{25,1},{2,10},{10... | collective-permute-start | bytes 589832 | tf_op jit(solution)/shard_map/ppermute | solution.py:271
  47.9 13.5 %collective-permute-start.1 = (bf16[192,512]{1,0:T(8,128)(2,1)S(1)}, bf16[192,512]{1,0:T(8,128)(2,1)S(1)}, u32[]{:S(2)}, u32[]{:S(2)}) collective-permute-start(bf16[192,512]{1,0:T(8,128)(2,1)S(1)} %get-tuple-element.39), channel_id=1, source_target_pairs={{0,16},{8,24},{16,0},{24,8},{1,17},{9,25},{17,1},{25,9},{2,18},{10... | collective-permute-start | bytes 589832 | tf_op jit(solution)/shard_map/ppermute | solution.py:271
  53.1 8.6 %collective-permute-start.2 = (bf16[192,512]{1,0:T(8,128)(2,1)S(1)}, bf16[192,512]{1,0:T(8,128)(2,1)S(1)}, u32[]{:S(2)}, u32[]{:S(2)}) collective-permute-start(bf16[192,512]{1,0:T(8,128)(2,1)S(1)} %get-tuple-element.40), channel_id=1, source_target_pairs={{0,24},{8,0},{16,8},{24,16},{1,25},{9,1},{17,9},{25,17},{2,26},{10... | collective-permute-start | bytes 589832 | tf_op jit(solution)/shard_map/ppermute | solution.py:271
  56.6 9.3 %all-to-all-start.3 = ((bf16[4,64,256]{2,1,0:T(8,128)(2,1)}), bf16[4,64,256]{2,1,0:T(8,128)(2,1)S(1)}, u32[]{:S(2)}, u32[]{:S(2)}) async-start(bf16[4,64,256]{2,1,0:T(8,128)(2,1)} %emit_terms.4), calls=%async_computation.3 | async-start | bytes 262144 | tf_op jit(solution)/shard_map/all_to_all | solution.py:66
  65.9 5.8 %collective-permute-start.3 = (bf16[64,256]{1,0:T(8,128)(2,1)S(1)}, bf16[64,256]{1,0:T(8,128)(2,1)S(1)}, u32[]{:S(2)}, u32[]{:S(2)}) collective-permute-start(bf16[64,256]{1,0:T(8,128)(2,1)S(1)} %get-tuple-element.41), channel_id=1, source_target_pairs={{0,32},{32,64},{64,96},{96,128},{128,160},{160,192},{192,224},{224... | collective-permute-start | bytes 98312 | tf_op jit(solution)/shard_map/ppermute | solution.py:310
  121.7 4.6 %collective-permute-start.4 = (bf16[64,256]{1,0:T(8,128)(2,1)S(1)}, bf16[64,256]{1,0:T(8,128)(2,1)S(1)}, u32[]{:S(2)}, u32[]{:S(2)}) collective-permute-start(bf16[64,256]{1,0:T(8,128)(2,1)S(1)} %get-tuple-element.43), channel_id=1, source_target_pairs={{0,32},{32,64},{64,96},{96,128},{128,160},{160,192},{192,224},{224... | collective-permute-start | bytes 98312 | tf_op jit(solution)/shard_map/ppermute | solution.py:310
  171.5 4.6 %collective-permute-start.5 = (bf16[64,256]{1,0:T(8,128)(2,1)S(1)}, bf16[64,256]{1,0:T(8,128)(2,1)S(1)}, u32[]{:S(2)}, u32[]{:S(2)}) collective-permute-start(bf16[64,256]{1,0:T(8,128)(2,1)S(1)} %get-tuple-element.46), channel_id=1, source_target_pairs={{0,32},{32,64},{64,96},{96,128},{128,160},{160,192},{192,224},{224... | collective-permute-start | bytes 98312 | tf_op jit(solution)/shard_map/ppermute | solution.py:310

commit v8 on v7

--- a/solution.py
+++ b/solution.py
@@ -45,10 +45,13 @@
     half = full.shape[-1] // 2
     lower, upper = full[..., :half], full[..., half:]
     at = [lax.broadcasted_iota(jnp.int32, (half, half), axis) for axis in (0, 1)]
-    mirror = jnp.where(at[0] + at[1] == half, 1.0, 0.0)
-    mirrored = jnp.dot(
-        upper.reshape(-1, half), mirror, precision=lax.Precision.HIGHEST, preferred_element_type=jnp.float32
-    ).reshape(upper.shape)
+    mirror = jnp.where(at[0] + at[1] == half, 1.0, 0.0).astype(jnp.bfloat16)
+    flat = upper.reshape(-1, half)
+    high = flat.astype(jnp.bfloat16)
+    low = (flat - high.astype(jnp.float32)).astype(jnp.bfloat16)
+    mirrored = jnp.dot(high, mirror, preferred_element_type=jnp.float32)
+    mirrored += jnp.dot(low, mirror, preferred_element_type=jnp.float32)
+    mirrored = mirrored.reshape(upper.shape)
     first = lax.broadcasted_iota(jnp.int32, lower.shape[1:], 1) == 0
     real = jnp.where(first, lower[0], 0.5 * (lower[0] + mirrored[0]))
     imag = jnp.where(first, upper[0], 0.5 * (lower[1] - mirrored[1]))
@@ -84,8 +87,10 @@
             block[m * width : (m + 1) * width] = scaled(matrix, gain_ref, at)
 
 
-def pack_kernel(part_ref, emit_ref, _, out_ref):
+def pack_kernel(y_ref, part_ref, emit_ref, _, out_ref, own_ref):
     groups, size, positions = out_ref.shape
+    at = pl.multiple_of(y_ref[0] * own_ref.shape[0], own_ref.shape[0])
+    own_ref[...] = part_ref[pl.ds(at, own_ref.shape[0])]
     rows, width = part_ref.shape[0], emit_ref.shape[0]
     for x in range(groups):
         out_ref[x, :rows] = part_ref[...]
@@ -212,8 +217,12 @@
     return total.astype(own_ref.dtype)
 
 
-def add_and_send_kernel(tick, layers, section_ref, terms_ref, own_ref, fresh_ref, *rest):
-    out_ref, send_ref = rest[-2:]
+def spread_kernel(own_ref, *rest):
+    for y in range(rest[-1].shape[0]):
+        rest[-1][y] = own_ref[...]
+
+
+def add_and_send_kernel(tick, layers, section_ref, terms_ref, own_ref, fresh_ref, out_ref, send_ref):
     out = total_of(terms_ref, own_ref)
     out_ref[...] = out
     send_ref[...] = jnp.where(section_ref[0] == layers - 1, fresh_ref[tick], out)
@@ -245,8 +254,8 @@
     gate_w = [w[0].T for w in (value_w, in_w, out_w)]
     half = filters.shape[-1] // 2
     fresh = newcomers.transpose(0, 2, 1)
-    passed = [jnp.asarray(tables(positions, 2 * half)), fresh, own]
-    live, known, filters, table, fresh, own = call(
+    passed = [jnp.asarray(tables(positions, 2 * half)), fresh]
+    live, known, filters, table, fresh = call(
         history_kernel,
         [f32((ticks, 1, positions)), bf16((blocks, 2, width, half)), f32((blocks + 1, 2, width, half))]
         + [jax.ShapeDtypeStruct(t.shape, t.dtype) for t in passed],
@@ -256,7 +265,15 @@
     )
 
     size = rows + width * rows // positions
-    packed = swap(call(pack_kernel, bf16((groups, size, positions)), [part, emit_w[0].T, live], "pack"), "x")
+    packed, own = call(
+        pack_kernel,
+        [bf16((groups, size, positions)), bf16(own.shape)],
+        [lax.axis_index("y").astype(jnp.int32)[None], part, emit_w[0].T, live],
+        "pack",
+        smem=1,
+        after=1,
+    )
+    packed = swap(packed, "x")
     mixed, spectrum, emit_rows = call(
         first_mix_kernel,
         [bf16((copies, width, positions)), f32((2, width, half)), bf16((groups, rows // positions, width, positions))],
@@ -301,14 +318,15 @@
             out, send = call(
                 functools.partial(add_and_send_kernel, tick, layers),
                 [bf16(own.shape)] * 2,
-                [place, terms, own, fresh] + (weights if tick == 0 else []),
+                [place, terms, own, fresh],
                 "add",
                 smem=1,
-                after=len(weights) if tick == 0 else 0,
             )
             outputs.append(out)
             own = lax.ppermute(send, SECTION, ring)
-            part = gather_rows(jnp.broadcast_to(own[None], (copies,) + own.shape))
+            after = weights if tick == 0 else []
+            spread = call(spread_kernel, bf16((copies,) + own.shape), [own] + after, "spread", after=len(after))
+            part = gather_rows(spread)
     layer_out = call(finish_kernel, bf16((ticks,) + own.shape), [terms, own] + outputs, "finish")
     return layer_out.transpose(0, 2, 1)[None]
 

time: 228 us -> 228 us (level)
  the two profiles are of different devices: /device:TPU:2 before, /device:TPU:64 now
where the time goes in v8:
time: 228 us; the launch traced here: 227 us
  blocking collectives  177 us (78%)
  starting transfers between devices  19.7 us (9%)
  waiting for transfers between devices  16.6 us (7%)
  Pallas kernels  7.69 us (3%)
  local copies, waits for them, and re-layouts  6.04 us (3%)
    all_to_all x14, blocking collectives, swap(): return lax.all_to_all(blocks, axis, 0, 0, tiled=True)  177 us
    all_to_all x2, starting transfers between devices, swap(): return lax.all_to_all(blocks, axis, 0, 0, tiled=True)  10.5 us
    ppermute x3, waiting for transfers between devices, local(): own = lax.ppermute(send, SECTION, ring)  9.95 us
    ppermute x3, starting transfers between devices, local(): lax.ppermute(dealt[step], 'x', [(i, (i + step) % groups) for i in range(g...  9.17 us
    pallas_call x21, Pallas kernels, call(): pl.pallas_call(body, out_shape=out, in_specs=[scalars] * smem + [vmem] *...  7.69 us
    all_to_all x2, waiting for transfers between devices, swap(): return lax.all_to_all(blocks, axis, 0, 0, tiled=True)  6.68 us
  transfers between devices with their start and end apart: 8, of which 5 were waited for; matrix products, arithmetic and copies ran while one was open for 0% of the time, Pallas kernels for 1%

profile of v8, /device:TPU:64, one launch (start us, length us, event | category | flops | bytes accessed | tf_op | source)
XLA Modules:
  0.0 227.4 jit_solution(4346966937251860761)
XLA Ops:
  0.0 1.5 broadcast_in_dim.20
  1.6 7.1 %all-to-all-start = ((bf16[8,64,256]{2,1,0:T(8,128)(2,1)}), bf16[8,64,256]{2,1,0:T(8,128)(2,1)S(1)}, u32[]{:S(2)}, u32[]{:S(2)}) async-start(bf16[8,64,256]{2,1,0:T(8,128)(2,1)} %broadcast_in_dim.20), calls=%async_computation | async-start | bytes 524288 | tf_op jit(solution)/shard_map/all_to_all | solution.py:69
  14.3 6.2 %all-to-all-done = bf16[8,64,256]{2,1,0:T(8,128)(2,1)S(1)} async-done(((bf16[8,64,256]{2,1,0:T(8,128)(2,1)}), bf16[8,64,256]{2,1,0:T(8,128)(2,1)S(1)}, u32[]{:S(2)}, u32[]{:S(2)}) %all-to-all-start) | async-done | bytes 262176 | tf_op jit(solution)/shard_map/all_to_all | solution.py:69
  20.7 20.3 %all_to_all.80.packed_ref = bf16[4,640,256]{2,1,0:T(8,128)(2,1)S(1)} all-to-all(bf16[4,640,256]{2,1,0:T(8,128)(2,1)S(1)} %get-tuple-element.30), channel_id=1, replica_groups=mesh['z'=8,'core'=2,'x'=4,'y'=8] {'x'}, dimensions={0} | all-to-all | bytes 2621440 | tf_op jit(solution)/shard_map/all_to_all | solution.py:69
  42.5 3.4 %all-to-all-start.2 = ((bf16[8,64,256]{2,1,0:T(8,128)(2,1)}), bf16[8,64,256]{2,1,0:T(8,128)(2,1)S(1)}, u32[]{:S(2)}, u32[]{:S(2)}) async-start(bf16[8,64,256]{2,1,0:T(8,128)(2,1)} %get-tuple-element.35), calls=%async_computation.2 | async-start | bytes 524288 | tf_op jit(solution)/shard_map/all_to_all | solution.py:69
  46.7 2.5 %collective-permute-start.1 = (bf16[192,512]{1,0:T(8,128)(2,1)}, bf16[192,512]{1,0:T(8,128)(2,1)S(1)}, u32[]{:S(2)}, u32[]{:S(2)}) collective-permute-start(bf16[192,512]{1,0:T(8,128)(2,1)} %get-tuple-element.41), channel_id=1, source_target_pairs={{0,8},{8,16},{16,24},{24,0},{1,9},{9,17},{17,25},{25,1},{2,10},{10... | collective-permute-start | bytes 589832 | tf_op jit(solution)/shard_map/ppermute | solution.py:288
  49.1 4.0 %collective-permute-start.2 = (bf16[192,512]{1,0:T(8,128)(2,1)S(1)}, bf16[192,512]{1,0:T(8,128)(2,1)S(1)}, u32[]{:S(2)}, u32[]{:S(2)}) collective-permute-start(bf16[192,512]{1,0:T(8,128)(2,1)S(1)} %get-tuple-element.42), channel_id=1, source_target_pairs={{0,16},{8,24},{16,0},{24,8},{1,17},{9,25},{17,1},{25,9},{2,18},{10... | collective-permute-start | bytes 589832 | tf_op jit(solution)/shard_map/ppermute | solution.py:288
  53.1 2.7 %collective-permute-start.3 = (bf16[192,512]{1,0:T(8,128)(2,1)S(1)}, bf16[192,512]{1,0:T(8,128)(2,1)S(1)}, u32[]{:S(2)}, u32[]{:S(2)}) collective-permute-start(bf16[192,512]{1,0:T(8,128)(2,1)S(1)} %get-tuple-element.43), channel_id=1, source_target_pairs={{0,24},{8,0},{16,8},{24,16},{1,25},{9,1},{17,9},{25,17},{2,26},{10... | collective-permute-start | bytes 589832 | tf_op jit(solution)/shard_map/ppermute | solution.py:288
  56.6 9.3 %all_to_all.81.terms_ref = bf16[4,64,256]{2,1,0:T(8,128)(2,1)S(1)} all-to-all(bf16[4,64,256]{2,1,0:T(8,128)(2,1)S(1)} %emit_terms.4), channel_id=1, replica_groups=mesh['z'=8,'core'=2,'x'=4,'y'=8] {'x'}, dimensions={0} | all-to-all | bytes 262144 | tf_op jit(solution)/shard_map/all_to_all | solution.py:69
  66.0 3.3 %collective-permute-done.own_ref = bf16[64,256]{1,0:T(8,128)(2,1)S(1)} collective-permute-done((bf16[64,256]{1,0:T(8,128)(2,1)S(1)}, bf16[64,256]{1,0:T(8,128)(2,1)S(1)}, u32[]{:S(2)}, u32[]{:S(2)}) %collective-permute-start) | collective-permute-done | bytes 32800 | tf_op jit(solution)/shard_map/ppermute | solution.py:326
  69.3 19.1 %all_to_all.82 = bf16[8,64,256]{2,1,0:T(8,128)(2,1)S(1)} all-to-all(bf16[8,64,256]{2,1,0:T(8,128)(2,1)S(1)} %spread.3), channel_id=1, replica_groups=mesh['z'=8,'core'=2,'x'=4,'y'=8] {'y'}, dimensions={0} | all-to-all | bytes 524288 | tf_op jit(solution)/shard_map/all_to_all | solution.py:69
  88.8 10.2 %all_to_all.83.terms_ref = bf16[4,208,256]{2,1,0:T(8,128)(2,1)S(1)} all-to-all(bf16[4,208,256]{2,1,0:T(8,128)(2,1)S(1)} %gate_terms.3), channel_id=1, replica_groups=mesh['z'=8,'core'=2,'x'=4,'y'=8] {'x'}, dimensions={0} | all-to-all | bytes 851968 | tf_op jit(solution)/shard_map/all_to_all | solution.py:69
  99.4 12.9 %all_to_all.84 = bf16[8,64,256]{2,1,0:T(8,128)(2,1)S(1)} all-to-all(bf16[8,64,256]{2,1,0:T(8,128)(2,1)S(1)} %get-tuple-element.44), channel_id=1, replica_groups=mesh['z'=8,'core'=2,'x'=4,'y'=8] {'y'}, dimensions={0} | all-to-all | bytes 524288 | tf_op jit(solution)/shard_map/all_to_all | solution.py:69
  112.6 8.4 %all_to_all.85.terms_ref = bf16[4,64,256]{2,1,0:T(8,128)(2,1)S(1)} all-to-all(bf16[4,64,256]{2,1,0:T(8,128)(2,1)S(1)} %emit_terms.5), channel_id=1, replica_groups=mesh['z'=8,'core'=2,'x'=4,'y'=8] {'x'}, dimensions={0} | all-to-all | bytes 262144 | tf_op jit(solution)/shard_map/all_to_all | solution.py:69
  121.0 3.3 %collective-permute-done.4.own_ref = bf16[64,256]{1,0:T(8,128)(2,1)S(1)} collective-permute-done((bf16[64,256]{1,0:T(8,128)(2,1)S(1)}, bf16[64,256]{1,0:T(8,128)(2,1)S(1)}, u32[]{:S(2)}, u32[]{:S(2)}) %collective-permute-start.4) | collective-permute-done | bytes 32800 | tf_op jit(solution)/shard_map/ppermute | solution.py:326
  124.4 14.8 %all_to_all.86 = bf16[8,64,256]{2,1,0:T(8,128)(2,1)S(1)} all-to-all(bf16[8,64,256]{2,1,0:T(8,128)(2,1)S(1)} %spread.4), channel_id=1, replica_groups=mesh['z'=8,'core'=2,'x'=4,'y'=8] {'y'}, dimensions={0} | all-to-all | bytes 524288 | tf_op jit(solution)/shard_map/all_to_all | solution.py:69
  139.6 11.2 %all_to_all.87.terms_ref = bf16[4,208,256]{2,1,0:T(8,128)(2,1)S(1)} all-to-all(bf16[4,208,256]{2,1,0:T(8,128)(2,1)S(1)} %gate_terms.4), channel_id=1, replica_groups=mesh['z'=8,'core'=2,'x'=4,'y'=8] {'x'}, dimensions={0} | all-to-all | bytes 851968 | tf_op jit(solution)/shard_map/all_to_all | solution.py:69
  151.2 13.9 %all_to_all.88 = bf16[8,64,256]{2,1,0:T(8,128)(2,1)S(1)} all-to-all(bf16[8,64,256]{2,1,0:T(8,128)(2,1)S(1)} %get-tuple-element.47), channel_id=1, replica_groups=mesh['z'=8,'core'=2,'x'=4,'y'=8] {'y'}, dimensions={0} | all-to-all | bytes 524288 | tf_op jit(solution)/shard_map/all_to_all | solution.py:69
  165.4 8.4 %all_to_all.89.terms_ref = bf16[4,64,256]{2,1,0:T(8,128)(2,1)S(1)} all-to-all(bf16[4,64,256]{2,1,0:T(8,128)(2,1)S(1)} %emit_terms.6), channel_id=1, replica_groups=mesh['z'=8,'core'=2,'x'=4,'y'=8] {'x'}, dimensions={0} | all-to-all | bytes 262144 | tf_op jit(solution)/shard_map/all_to_all | solution.py:69
  173.8 3.3 %collective-permute-done.5.own_ref = bf16[64,256]{1,0:T(8,128)(2,1)S(1)} collective-permute-done((bf16[64,256]{1,0:T(8,128)(2,1)S(1)}, bf16[64,256]{1,0:T(8,128)(2,1)S(1)}, u32[]{:S(2)}, u32[]{:S(2)}) %collective-permute-start.5) | collective-permute-done | bytes 32800 | tf_op jit(solution)/shard_map/ppermute | solution.py:326
  177.2 14.9 %all_to_all.90 = bf16[8,64,256]{2,1,0:T(8,128)(2,1)S(1)} all-to-all(bf16[8,64,256]{2,1,0:T(8,128)(2,1)S(1)} %spread.5), channel_id=1, replica_groups=mesh['z'=8,'core'=2,'x'=4,'y'=8] {'y'}, dimensions={0} | all-to-all | bytes 524288 | tf_op jit(solution)/shard_map/all_to_all | solution.py:69
  192.5 11.3 %all_to_all.91.terms_ref = bf16[4,208,256]{2,1,0:T(8,128)(2,1)S(1)} all-to-all(bf16[4,208,256]{2,1,0:T(8,128)(2,1)S(1)} %gate_terms.5), channel_id=1, replica_groups=mesh['z'=8,'core'=2,'x'=4,'y'=8] {'x'}, dimensions={0} | all-to-all | bytes 851968 | tf_op jit(solution)/shard_map/all_to_all | solution.py:69
  204.2 13.9 %all_to_all.92 = bf16[8,64,256]{2,1,0:T(8,128)(2,1)S(1)} all-to-all(bf16[8,64,256]{2,1,0:T(8,128)(2,1)S(1)} %mix.5), channel_id=1, replica_groups=mesh['z'=8,'core'=2,'x'=4,'y'=8] {'y'}, dimensions={0} | all-to-all | bytes 524288 | tf_op jit(solution)/shard_map/all_to_all | solution.py:69
  218.4 8.4 %all_to_all.93.terms_ref = bf16[4,64,256]{2,1,0:T(8,128)(2,1)S(1)} all-to-all(bf16[4,64,256]{2,1,0:T(8,128)(2,1)S(1)} %emit_terms.7), channel_id=1, replica_groups=mesh['z'=8,'core'=2,'x'=4,'y'=8] {'x'}, dimensions={0} | all-to-all | bytes 262144 | tf_op jit(solution)/shard_map/all_to_all | solution.py:69
  (50 shorter events, 12.7 us)
Async XLA Ops:
  0.0 8.7 %copy-start.4 = (f32[1,3,2,64,512]{4,3,2,1,0:T(8,128)S(1)}, f32[1,3,2,64,512]{4,3,2,1,0:T(8,128)}, u32[]{:S(2)}) copy-start(f32[1,3,2,64,512]{4,3,2,1,0:T(8,128)} %param.22) | copy-start | bytes 2359300
  1.6 19.0 %all-to-all-start = ((bf16[8,64,256]{2,1,0:T(8,128)(2,1)}), bf16[8,64,256]{2,1,0:T(8,128)(2,1)S(1)}, u32[]{:S(2)}, u32[]{:S(2)}) async-start(bf16[8,64,256]{2,1,0:T(8,128)(2,1)} %broadcast_in_dim.20), calls=%async_computation | async-start | bytes 524288 | tf_op jit(solution)/shard_map/all_to_all | solution.py:69
  8.7 1.2 copy-start.3
  9.9 1.0 copy-start.5
  10.9 0.9 copy-start.7
  11.8 0.7 copy-start.9
  12.5 0.7 copy-start.10
  13.1 7.4 %copy-start.6 = (bf16[1,2048,64]{1,2,0:T(8,128)(2,1)S(1)}, bf16[1,2048,64]{1,2,0:T(8,128)(2,1)}, u32[]{:S(2)}) copy-start(bf16[1,2048,64]{1,2,0:T(8,128)(2,1)} %param.19) | copy-start | bytes 786436
  20.6 20.4 %copy-start = (bf16[1,2048,64]{1,2,0:T(8,128)(2,1)S(1)}, bf16[1,2048,64]{1,2,0:T(8,128)(2,1)}, u32[]{:S(2)}) copy-start(bf16[1,2048,64]{1,2,0:T(8,128)(2,1)} %param.16) | copy-start | bytes 786436
  20.6 20.4 %copy-start.1 = (bf16[1,2048,64]{1,2,0:T(8,128)(2,1)S(1)}, bf16[1,2048,64]{1,2,0:T(8,128)(2,1)}, u32[]{:S(2)}) copy-start(bf16[1,2048,64]{1,2,0:T(8,128)(2,1)} %param.17) | copy-start | bytes 786436
  20.6 20.4 %copy-start.2 = (bf16[1,2048,64]{1,2,0:T(8,128)(2,1)S(1)}, bf16[1,2048,64]{1,2,0:T(8,128)(2,1)}, u32[]{:S(2)}) copy-start(bf16[1,2048,64]{1,2,0:T(8,128)(2,1)} %param.18) | copy-start | bytes 786436
  20.7 20.4 %copy-start.8 = (f32[1,2048]{1,0:T(1,128)S(1)}, f32[1,2048]{1,0:T(1,128)}, u32[]{:S(2)}) copy-start(f32[1,2048]{1,0:T(1,128)} %gain_ref.3) | copy-start | bytes 24580
  42.5 13.8 %all-to-all-start.2 = ((bf16[8,64,256]{2,1,0:T(8,128)(2,1)}), bf16[8,64,256]{2,1,0:T(8,128)(2,1)S(1)}, u32[]{:S(2)}, u32[]{:S(2)}) async-start(bf16[8,64,256]{2,1,0:T(8,128)(2,1)} %get-tuple-element.35), calls=%async_computation.2 | async-start | bytes 524288 | tf_op jit(solution)/shard_map/all_to_all | solution.py:69
  46.7 19.3 %collective-permute-start.1 = (bf16[192,512]{1,0:T(8,128)(2,1)}, bf16[192,512]{1,0:T(8,128)(2,1)S(1)}, u32[]{:S(2)}, u32[]{:S(2)}) collective-permute-start(bf16[192,512]{1,0:T(8,128)(2,1)} %get-tuple-element.41), channel_id=1, source_target_pairs={{0,8},{8,16},{16,24},{24,0},{1,9},{9,17},{17,25},{25,1},{2,10},{10... | collective-permute-start | bytes 589832 | tf_op jit(solution)/shard_map/ppermute | solution.py:288
  49.1 16.9 %collective-permute-start.2 = (bf16[192,512]{1,0:T(8,128)(2,1)S(1)}, bf16[192,512]{1,0:T(8,128)(2,1)S(1)}, u32[]{:S(2)}, u32[]{:S(2)}) collective-permute-start(bf16[192,512]{1,0:T(8,128)(2,1)S(1)} %get-tuple-element.42), channel_id=1, source_target_pairs={{0,16},{8,24},{16,0},{24,8},{1,17},{9,25},{17,1},{25,9},{2,18},{10... | collective-permute-start | bytes 589832 | tf_op jit(solution)/shard_map/ppermute | solution.py:288
  53.1 12.9 %collective-permute-start.3 = (bf16[192,512]{1,0:T(8,128)(2,1)S(1)}, bf16[192,512]{1,0:T(8,128)(2,1)S(1)}, u32[]{:S(2)}, u32[]{:S(2)}) collective-permute-start(bf16[192,512]{1,0:T(8,128)(2,1)S(1)} %get-tuple-element.43), channel_id=1, source_target_pairs={{0,24},{8,0},{16,8},{24,16},{1,25},{9,1},{17,9},{25,17},{2,26},{10... | collective-permute-start | bytes 589832 | tf_op jit(solution)/shard_map/ppermute | solution.py:288
  66.0 3.4 %collective-permute-start = (bf16[64,256]{1,0:T(8,128)(2,1)S(1)}, bf16[64,256]{1,0:T(8,128)(2,1)S(1)}, u32[]{:S(2)}, u32[]{:S(2)}) collective-permute-start(bf16[64,256]{1,0:T(8,128)(2,1)S(1)} %get-tuple-element.38), channel_id=1, source_target_pairs={{0,32},{32,64},{64,96},{96,128},{128,160},{160,192},{192,224},{224... | collective-permute-start | bytes 98312 | tf_op jit(solution)/shard_map/ppermute | solution.py:326
  121.0 3.4 %collective-permute-start.4 = (bf16[64,256]{1,0:T(8,128)(2,1)S(1)}, bf16[64,256]{1,0:T(8,128)(2,1)S(1)}, u32[]{:S(2)}, u32[]{:S(2)}) collective-permute-start(bf16[64,256]{1,0:T(8,128)(2,1)S(1)} %get-tuple-element.45), channel_id=1, source_target_pairs={{0,32},{32,64},{64,96},{96,128},{128,160},{160,192},{192,224},{224... | collective-permute-start | bytes 98312 | tf_op jit(solution)/shard_map/ppermute | solution.py:326
  173.8 3.4 %collective-permute-start.5 = (bf16[64,256]{1,0:T(8,128)(2,1)S(1)}, bf16[64,256]{1,0:T(8,128)(2,1)S(1)}, u32[]{:S(2)}, u32[]{:S(2)}) collective-permute-start(bf16[64,256]{1,0:T(8,128)(2,1)S(1)} %get-tuple-element.48), channel_id=1, source_target_pairs={{0,32},{32,64},{64,96},{96,128},{128,160},{160,192},{192,224},{224... | collective-permute-start | bytes 98312 | tf_op jit(solution)/shard_map/ppermute | solution.py:326

commit v9 on v7

--- a/solution.py
+++ b/solution.py
@@ -212,8 +212,12 @@
     return total.astype(own_ref.dtype)
 
 
-def add_and_send_kernel(tick, layers, section_ref, terms_ref, own_ref, fresh_ref, *rest):
-    out_ref, send_ref = rest[-2:]
+def spread_kernel(own_ref, *rest):
+    for y in range(rest[-1].shape[0]):
+        rest[-1][y] = own_ref[...]
+
+
+def add_and_send_kernel(tick, layers, section_ref, terms_ref, own_ref, fresh_ref, out_ref, send_ref):
     out = total_of(terms_ref, own_ref)
     out_ref[...] = out
     send_ref[...] = jnp.where(section_ref[0] == layers - 1, fresh_ref[tick], out)
@@ -301,14 +305,15 @@
             out, send = call(
                 functools.partial(add_and_send_kernel, tick, layers),
                 [bf16(own.shape)] * 2,
-                [place, terms, own, fresh] + (weights if tick == 0 else []),
+                [place, terms, own, fresh],
                 "add",
                 smem=1,
-                after=len(weights) if tick == 0 else 0,
             )
             outputs.append(out)
             own = lax.ppermute(send, SECTION, ring)
-            part = gather_rows(jnp.broadcast_to(own[None], (copies,) + own.shape))
+            after = weights if tick == 0 else []
+            spread = call(spread_kernel, bf16((copies,) + own.shape), [own] + after, "spread", after=len(after))
+            part = gather_rows(spread)
     layer_out = call(finish_kernel, bf16((ticks,) + own.shape), [terms, own] + outputs, "finish")
     return layer_out.transpose(0, 2, 1)[None]
 

time: 228 us -> 228 us (level)
  the two profiles are of different devices: /device:TPU:2 before, /device:TPU:64 now
where the time goes in v9:
time: 228 us; the launch traced here: 227 us
  blocking collectives  177 us (78%)
  starting transfers between devices  19.8 us (9%)
  waiting for transfers between devices  15.5 us (7%)
  Pallas kernels  8.15 us (4%)
  local copies, waits for them, and re-layouts  6.8 us (3%)
    all_to_all x14, blocking collectives, swap(): return lax.all_to_all(blocks, axis, 0, 0, tiled=True)  177 us
    all_to_all x2, starting transfers between devices, swap(): return lax.all_to_all(blocks, axis, 0, 0, tiled=True)  10.6 us
    ppermute x3, waiting for transfers between devices, local(): own = lax.ppermute(send, SECTION, ring)  9.95 us
    ppermute x3, starting transfers between devices, local(): lax.ppermute(dealt[step], 'x', [(i, (i + step) % groups) for i in range(g...  9.17 us
    pallas_call x21, Pallas kernels, call(): pl.pallas_call(body, out_shape=out, in_specs=[scalars] * smem + [vmem] *...  8.15 us
    all_to_all x2, waiting for transfers between devices, swap(): return lax.all_to_all(blocks, axis, 0, 0, tiled=True)  5.55 us
    unnamed x24, local copies, waits for them, and re-layouts  5.25 us
  transfers between devices with their start and end apart: 8, of which 5 were waited for; matrix products, arithmetic and copies ran while one was open for 0% of the time, Pallas kernels for 1%

profile of v9, /device:TPU:64, one launch (start us, length us, event | category | flops | bytes accessed | tf_op | source)
XLA Modules:
  0.0 227.1 jit_solution(11900663488295085261)
XLA Ops:
  1.6 7.1 %all-to-all-start = ((bf16[8,64,256]{2,1,0:T(8,128)(2,1)}), bf16[8,64,256]{2,1,0:T(8,128)(2,1)S(1)}, u32[]{:S(2)}, u32[]{:S(2)}) async-start(bf16[8,64,256]{2,1,0:T(8,128)(2,1)} %broadcast_in_dim.16), calls=%async_computation | async-start | bytes 524288 | tf_op jit(solution)/shard_map/all_to_all | solution.py:66
  13.9 1.6 history.1
  15.5 5.0 %all-to-all-done = bf16[8,64,256]{2,1,0:T(8,128)(2,1)S(1)} async-done(((bf16[8,64,256]{2,1,0:T(8,128)(2,1)}), bf16[8,64,256]{2,1,0:T(8,128)(2,1)S(1)}, u32[]{:S(2)}, u32[]{:S(2)}) %all-to-all-start) | async-done | bytes 262176 | tf_op jit(solution)/shard_map/all_to_all | solution.py:66
  20.7 20.3 %all_to_all.80.packed_ref = bf16[4,640,256]{2,1,0:T(8,128)(2,1)S(1)} all-to-all(bf16[4,640,256]{2,1,0:T(8,128)(2,1)S(1)} %pack.1), channel_id=1, replica_groups=mesh['z'=8,'core'=2,'x'=4,'y'=8] {'x'}, dimensions={0} | all-to-all | bytes 2621440 | tf_op jit(solution)/shard_map/all_to_all | solution.py:66
  42.5 3.5 %all-to-all-start.2 = ((bf16[8,64,256]{2,1,0:T(8,128)(2,1)}), bf16[8,64,256]{2,1,0:T(8,128)(2,1)S(1)}, u32[]{:S(2)}, u32[]{:S(2)}) async-start(bf16[8,64,256]{2,1,0:T(8,128)(2,1)} %get-tuple-element.33), calls=%async_computation.2 | async-start | bytes 524288 | tf_op jit(solution)/shard_map/all_to_all | solution.py:66
  46.7 2.5 %collective-permute-start.1 = (bf16[192,512]{1,0:T(8,128)(2,1)}, bf16[192,512]{1,0:T(8,128)(2,1)S(1)}, u32[]{:S(2)}, u32[]{:S(2)}) collective-permute-start(bf16[192,512]{1,0:T(8,128)(2,1)} %get-tuple-element.39), channel_id=1, source_target_pairs={{0,8},{8,16},{16,24},{24,0},{1,9},{9,17},{17,25},{25,1},{2,10},{10... | collective-permute-start | bytes 589832 | tf_op jit(solution)/shard_map/ppermute | solution.py:275
  49.2 4.0 %collective-permute-start.2 = (bf16[192,512]{1,0:T(8,128)(2,1)S(1)}, bf16[192,512]{1,0:T(8,128)(2,1)S(1)}, u32[]{:S(2)}, u32[]{:S(2)}) collective-permute-start(bf16[192,512]{1,0:T(8,128)(2,1)S(1)} %get-tuple-element.40), channel_id=1, source_target_pairs={{0,16},{8,24},{16,0},{24,8},{1,17},{9,25},{17,1},{25,9},{2,18},{10... | collective-permute-start | bytes 589832 | tf_op jit(solution)/shard_map/ppermute | solution.py:275
  53.2 2.7 %collective-permute-start.3 = (bf16[192,512]{1,0:T(8,128)(2,1)S(1)}, bf16[192,512]{1,0:T(8,128)(2,1)S(1)}, u32[]{:S(2)}, u32[]{:S(2)}) collective-permute-start(bf16[192,512]{1,0:T(8,128)(2,1)S(1)} %get-tuple-element.41), channel_id=1, source_target_pairs={{0,24},{8,0},{16,8},{24,16},{1,25},{9,1},{17,9},{25,17},{2,26},{10... | collective-permute-start | bytes 589832 | tf_op jit(solution)/shard_map/ppermute | solution.py:275
  56.7 9.2 %all_to_all.81.terms_ref = bf16[4,64,256]{2,1,0:T(8,128)(2,1)S(1)} all-to-all(bf16[4,64,256]{2,1,0:T(8,128)(2,1)S(1)} %emit_terms.4), channel_id=1, replica_groups=mesh['z'=8,'core'=2,'x'=4,'y'=8] {'x'}, dimensions={0} | all-to-all | bytes 262144 | tf_op jit(solution)/shard_map/all_to_all | solution.py:66
  66.0 3.3 %collective-permute-done.own_ref = bf16[64,256]{1,0:T(8,128)(2,1)S(1)} collective-permute-done((bf16[64,256]{1,0:T(8,128)(2,1)S(1)}, bf16[64,256]{1,0:T(8,128)(2,1)S(1)}, u32[]{:S(2)}, u32[]{:S(2)}) %collective-permute-start) | collective-permute-done | bytes 32800 | tf_op jit(solution)/shard_map/ppermute | solution.py:313
  69.4 19.2 %all_to_all.82 = bf16[8,64,256]{2,1,0:T(8,128)(2,1)S(1)} all-to-all(bf16[8,64,256]{2,1,0:T(8,128)(2,1)S(1)} %spread.3), channel_id=1, replica_groups=mesh['z'=8,'core'=2,'x'=4,'y'=8] {'y'}, dimensions={0} | all-to-all | bytes 524288 | tf_op jit(solution)/shard_map/all_to_all | solution.py:66
  89.0 10.2 %all_to_all.83.terms_ref = bf16[4,208,256]{2,1,0:T(8,128)(2,1)S(1)} all-to-all(bf16[4,208,256]{2,1,0:T(8,128)(2,1)S(1)} %gate_terms.3), channel_id=1, replica_groups=mesh['z'=8,'core'=2,'x'=4,'y'=8] {'x'}, dimensions={0} | all-to-all | bytes 851968 | tf_op jit(solution)/shard_map/all_to_all | solution.py:66
  99.5 12.9 %all_to_all.84 = bf16[8,64,256]{2,1,0:T(8,128)(2,1)S(1)} all-to-all(bf16[8,64,256]{2,1,0:T(8,128)(2,1)S(1)} %get-tuple-element.42), channel_id=1, replica_groups=mesh['z'=8,'core'=2,'x'=4,'y'=8] {'y'}, dimensions={0} | all-to-all | bytes 524288 | tf_op jit(solution)/shard_map/all_to_all | solution.py:66
  112.7 8.4 %all_to_all.85.terms_ref = bf16[4,64,256]{2,1,0:T(8,128)(2,1)S(1)} all-to-all(bf16[4,64,256]{2,1,0:T(8,128)(2,1)S(1)} %emit_terms.5), channel_id=1, replica_groups=mesh['z'=8,'core'=2,'x'=4,'y'=8] {'x'}, dimensions={0} | all-to-all | bytes 262144 | tf_op jit(solution)/shard_map/all_to_all | solution.py:66
  121.1 3.3 %collective-permute-done.4.own_ref = bf16[64,256]{1,0:T(8,128)(2,1)S(1)} collective-permute-done((bf16[64,256]{1,0:T(8,128)(2,1)S(1)}, bf16[64,256]{1,0:T(8,128)(2,1)S(1)}, u32[]{:S(2)}, u32[]{:S(2)}) %collective-permute-start.4) | collective-permute-done | bytes 32800 | tf_op jit(solution)/shard_map/ppermute | solution.py:313
  124.5 14.8 %all_to_all.86 = bf16[8,64,256]{2,1,0:T(8,128)(2,1)S(1)} all-to-all(bf16[8,64,256]{2,1,0:T(8,128)(2,1)S(1)} %spread.4), channel_id=1, replica_groups=mesh['z'=8,'core'=2,'x'=4,'y'=8] {'y'}, dimensions={0} | all-to-all | bytes 524288 | tf_op jit(solution)/shard_map/all_to_all | solution.py:66
  139.7 11.2 %all_to_all.87.terms_ref = bf16[4,208,256]{2,1,0:T(8,128)(2,1)S(1)} all-to-all(bf16[4,208,256]{2,1,0:T(8,128)(2,1)S(1)} %gate_terms.4), channel_id=1, replica_groups=mesh['z'=8,'core'=2,'x'=4,'y'=8] {'x'}, dimensions={0} | all-to-all | bytes 851968 | tf_op jit(solution)/shard_map/all_to_all | solution.py:66
  151.3 13.8 %all_to_all.88 = bf16[8,64,256]{2,1,0:T(8,128)(2,1)S(1)} all-to-all(bf16[8,64,256]{2,1,0:T(8,128)(2,1)S(1)} %get-tuple-element.45), channel_id=1, replica_groups=mesh['z'=8,'core'=2,'x'=4,'y'=8] {'y'}, dimensions={0} | all-to-all | bytes 524288 | tf_op jit(solution)/shard_map/all_to_all | solution.py:66
  165.4 8.4 %all_to_all.89.terms_ref = bf16[4,64,256]{2,1,0:T(8,128)(2,1)S(1)} all-to-all(bf16[4,64,256]{2,1,0:T(8,128)(2,1)S(1)} %emit_terms.6), channel_id=1, replica_groups=mesh['z'=8,'core'=2,'x'=4,'y'=8] {'x'}, dimensions={0} | all-to-all | bytes 262144 | tf_op jit(solution)/shard_map/all_to_all | solution.py:66
  173.8 3.3 %collective-permute-done.5.own_ref = bf16[64,256]{1,0:T(8,128)(2,1)S(1)} collective-permute-done((bf16[64,256]{1,0:T(8,128)(2,1)S(1)}, bf16[64,256]{1,0:T(8,128)(2,1)S(1)}, u32[]{:S(2)}, u32[]{:S(2)}) %collective-permute-start.5) | collective-permute-done | bytes 32800 | tf_op jit(solution)/shard_map/ppermute | solution.py:313
  177.2 14.8 %all_to_all.90 = bf16[8,64,256]{2,1,0:T(8,128)(2,1)S(1)} all-to-all(bf16[8,64,256]{2,1,0:T(8,128)(2,1)S(1)} %spread.5), channel_id=1, replica_groups=mesh['z'=8,'core'=2,'x'=4,'y'=8] {'y'}, dimensions={0} | all-to-all | bytes 524288 | tf_op jit(solution)/shard_map/all_to_all | solution.py:66
  192.3 11.2 %all_to_all.91.terms_ref = bf16[4,208,256]{2,1,0:T(8,128)(2,1)S(1)} all-to-all(bf16[4,208,256]{2,1,0:T(8,128)(2,1)S(1)} %gate_terms.5), channel_id=1, replica_groups=mesh['z'=8,'core'=2,'x'=4,'y'=8] {'x'}, dimensions={0} | all-to-all | bytes 851968 | tf_op jit(solution)/shard_map/all_to_all | solution.py:66
  203.9 13.8 %all_to_all.92 = bf16[8,64,256]{2,1,0:T(8,128)(2,1)S(1)} all-to-all(bf16[8,64,256]{2,1,0:T(8,128)(2,1)S(1)} %mix.5), channel_id=1, replica_groups=mesh['z'=8,'core'=2,'x'=4,'y'=8] {'y'}, dimensions={0} | all-to-all | bytes 524288 | tf_op jit(solution)/shard_map/all_to_all | solution.py:66
  218.0 8.4 %all_to_all.93.terms_ref = bf16[4,64,256]{2,1,0:T(8,128)(2,1)S(1)} all-to-all(bf16[4,64,256]{2,1,0:T(8,128)(2,1)S(1)} %emit_terms.7), channel_id=1, replica_groups=mesh['z'=8,'core'=2,'x'=4,'y'=8] {'x'}, dimensions={0} | all-to-all | bytes 262144 | tf_op jit(solution)/shard_map/all_to_all | solution.py:66
  (52 shorter events, 13.9 us)
Async XLA Ops:
  0.0 8.7 %copy-start.4 = (f32[1,3,2,64,512]{4,3,2,1,0:T(8,128)S(1)}, f32[1,3,2,64,512]{4,3,2,1,0:T(8,128)}, u32[]{:S(2)}) copy-start(f32[1,3,2,64,512]{4,3,2,1,0:T(8,128)} %param.22) | copy-start | bytes 2359300
  1.6 19.0 %all-to-all-start = ((bf16[8,64,256]{2,1,0:T(8,128)(2,1)}), bf16[8,64,256]{2,1,0:T(8,128)(2,1)S(1)}, u32[]{:S(2)}, u32[]{:S(2)}) async-start(bf16[8,64,256]{2,1,0:T(8,128)(2,1)} %broadcast_in_dim.16), calls=%async_computation | async-start | bytes 524288 | tf_op jit(solution)/shard_map/all_to_all | solution.py:66
  8.7 1.2 copy-start
  9.9 1.0 copy-start.5
  10.9 0.8 copy-start.7
  11.7 0.9 copy-start.8
  12.6 0.7 copy-start.10
  13.2 0.7 copy-start.11
  13.9 6.6 %copy-start.6 = (bf16[1,2048,64]{1,2,0:T(8,128)(2,1)S(1)}, bf16[1,2048,64]{1,2,0:T(8,128)(2,1)}, u32[]{:S(2)}) copy-start(bf16[1,2048,64]{1,2,0:T(8,128)(2,1)} %param.19) | copy-start | bytes 786436
  20.6 20.4 %copy-start.1 = (bf16[1,2048,64]{1,2,0:T(8,128)(2,1)S(1)}, bf16[1,2048,64]{1,2,0:T(8,128)(2,1)}, u32[]{:S(2)}) copy-start(bf16[1,2048,64]{1,2,0:T(8,128)(2,1)} %param.16) | copy-start | bytes 786436
  20.6 20.4 %copy-start.2 = (bf16[1,2048,64]{1,2,0:T(8,128)(2,1)S(1)}, bf16[1,2048,64]{1,2,0:T(8,128)(2,1)}, u32[]{:S(2)}) copy-start(bf16[1,2048,64]{1,2,0:T(8,128)(2,1)} %param.17) | copy-start | bytes 786436
  20.6 20.4 %copy-start.3 = (bf16[1,2048,64]{1,2,0:T(8,128)(2,1)S(1)}, bf16[1,2048,64]{1,2,0:T(8,128)(2,1)}, u32[]{:S(2)}) copy-start(bf16[1,2048,64]{1,2,0:T(8,128)(2,1)} %param.18) | copy-start | bytes 786436
  20.7 20.4 %copy-start.9 = (f32[1,2048]{1,0:T(1,128)S(1)}, f32[1,2048]{1,0:T(1,128)}, u32[]{:S(2)}) copy-start(f32[1,2048]{1,0:T(1,128)} %gain_ref.3) | copy-start | bytes 24580
  42.5 13.9 %all-to-all-start.2 = ((bf16[8,64,256]{2,1,0:T(8,128)(2,1)}), bf16[8,64,256]{2,1,0:T(8,128)(2,1)S(1)}, u32[]{:S(2)}, u32[]{:S(2)}) async-start(bf16[8,64,256]{2,1,0:T(8,128)(2,1)} %get-tuple-element.33), calls=%async_computation.2 | async-start | bytes 524288 | tf_op jit(solution)/shard_map/all_to_all | solution.py:66
  46.7 19.3 %collective-permute-start.1 = (bf16[192,512]{1,0:T(8,128)(2,1)}, bf16[192,512]{1,0:T(8,128)(2,1)S(1)}, u32[]{:S(2)}, u32[]{:S(2)}) collective-permute-start(bf16[192,512]{1,0:T(8,128)(2,1)} %get-tuple-element.39), channel_id=1, source_target_pairs={{0,8},{8,16},{16,24},{24,0},{1,9},{9,17},{17,25},{25,1},{2,10},{10... | collective-permute-start | bytes 589832 | tf_op jit(solution)/shard_map/ppermute | solution.py:275
  49.2 16.9 %collective-permute-start.2 = (bf16[192,512]{1,0:T(8,128)(2,1)S(1)}, bf16[192,512]{1,0:T(8,128)(2,1)S(1)}, u32[]{:S(2)}, u32[]{:S(2)}) collective-permute-start(bf16[192,512]{1,0:T(8,128)(2,1)S(1)} %get-tuple-element.40), channel_id=1, source_target_pairs={{0,16},{8,24},{16,0},{24,8},{1,17},{9,25},{17,1},{25,9},{2,18},{10... | collective-permute-start | bytes 589832 | tf_op jit(solution)/shard_map/ppermute | solution.py:275
  53.2 12.9 %collective-permute-start.3 = (bf16[192,512]{1,0:T(8,128)(2,1)S(1)}, bf16[192,512]{1,0:T(8,128)(2,1)S(1)}, u32[]{:S(2)}, u32[]{:S(2)}) collective-permute-start(bf16[192,512]{1,0:T(8,128)(2,1)S(1)} %get-tuple-element.41), channel_id=1, source_target_pairs={{0,24},{8,0},{16,8},{24,16},{1,25},{9,1},{17,9},{25,17},{2,26},{10... | collective-permute-start | bytes 589832 | tf_op jit(solution)/shard_map/ppermute | solution.py:275
  66.0 3.4 %collective-permute-start = (bf16[64,256]{1,0:T(8,128)(2,1)S(1)}, bf16[64,256]{1,0:T(8,128)(2,1)S(1)}, u32[]{:S(2)}, u32[]{:S(2)}) collective-permute-start(bf16[64,256]{1,0:T(8,128)(2,1)S(1)} %get-tuple-element.36), channel_id=1, source_target_pairs={{0,32},{32,64},{64,96},{96,128},{128,160},{160,192},{192,224},{224... | collective-permute-start | bytes 98312 | tf_op jit(solution)/shard_map/ppermute | solution.py:313
  121.1 3.4 %collective-permute-start.4 = (bf16[64,256]{1,0:T(8,128)(2,1)S(1)}, bf16[64,256]{1,0:T(8,128)(2,1)S(1)}, u32[]{:S(2)}, u32[]{:S(2)}) collective-permute-start(bf16[64,256]{1,0:T(8,128)(2,1)S(1)} %get-tuple-element.43), channel_id=1, source_target_pairs={{0,32},{32,64},{64,96},{96,128},{128,160},{160,192},{192,224},{224... | collective-permute-start | bytes 98312 | tf_op jit(solution)/shard_map/ppermute | solution.py:313
  173.8 3.4 %collective-permute-start.5 = (bf16[64,256]{1,0:T(8,128)(2,1)S(1)}, bf16[64,256]{1,0:T(8,128)(2,1)S(1)}, u32[]{:S(2)}, u32[]{:S(2)}) collective-permute-start(bf16[64,256]{1,0:T(8,128)(2,1)S(1)} %get-tuple-element.46), channel_id=1, source_target_pairs={{0,32},{32,64},{64,96},{96,128},{128,160},{160,192},{192,224},{224... | collective-permute-start | bytes 98312 | tf_op jit(solution)/shard_map/ppermute | solution.py:313
